TPU v7x, 32 devices: a whole 2x2x4 slice. The times are simulated.
32 devices in a mesh: img: 8 (over z, y), ch: 4 (over x, core).
Axes of the slice: x: 2, y: 2, z: 4, core: 2. Of those that a mesh axis runs over, the one named last changes fastest.
Arguments:
- feats: bfloat16 [8, 24, 24, 512], P('img', None, None, 'ch'), may hold values from -6 to 6
- shared_w: bfloat16 [2, 2, 3, 3, 512, 512], P(None, None, None, None, None, 'ch'), may hold values from -0.09375 to 0.09375
- task_w: bfloat16 [2, 3, 3, 3, 512, 512], P(None, None, None, None, None, 'ch'), may hold values from -0.09375 to 0.09375
- down_w: bfloat16 [2, 3, 512, 128], P(None, None, 'ch'), may hold values from -0.25 to 0.25
- up_w: bfloat16 [2, 3, 128, 512], P(None, None, None, 'ch'), may hold values from -0.5 to 0.5
- norm_gain: float32 [2, 8, 512], P(None, None, 'ch'), may hold values from 0.1 to 1.9
- norm_shift: float32 [2, 8, 512], P(None, None, 'ch'), may hold values from -3 to 3
- bottle_gain: float32 [2, 3, 128], replicated, may hold values from 0.1 to 1.9
- bottle_shift: float32 [2, 3, 128], replicated, may hold values from -3 to 3
- seg_mask: int32 [8, 6, 6], P('img'), may hold values 0 or 1
- depth_mask: int32 [8, 6, 6], P('img'), may hold values 0 or 1
- shared_cot: bfloat16 [8, 6, 6, 512], P('img', None, None, 'ch'), may hold values from -6 to 6
- task_cot: bfloat16 [3, 8, 6, 6, 512], P(None, 'img', None, None, 'ch'), may hold values from -6 to 6
Outputs:
- shared_out: bfloat16 [8, 6, 6, 512], P('img', None, None, 'ch')
- task_out: bfloat16 [3, 8, 6, 6, 512], P(None, 'img', None, None, 'ch')
- feats_grad: float32 [8, 24, 24, 512], P('img', None, None, 'ch')
- shared_w_grad: float32 [2, 2, 3, 3, 512, 512], P(None, None, None, None, 'img', 'ch')
- task_w_grad: float32 [2, 3, 3, 3, 512, 512], P(None, None, None, None, 'img', 'ch')
- down_w_grad: float32 [2, 3, 512, 128], P(None, None, 'ch')
- up_w_grad: float32 [2, 3, 128, 512], P(None, None, None, 'ch')
- norm_gain_grad: float32 [2, 8, 512], P(None, None, 'ch')
- norm_shift_grad: float32 [2, 8, 512], P(None, None, 'ch')
- bottle_gain_grad: float32 [2, 3, 128], replicated
- bottle_shift_grad: float32 [2, 3, 128], replicated
Inputs may be any that keep to these rules, and one draw needn't show every extreme that they name: `seg_mask`: a pixel's mask is 0 or 1. `depth_mask`: a pixel's mask is 0 or 1.
All inputs are finite; a program needn't handle non-finite values. No bound on the sum of `seg_mask` or of `depth_mask` on one device may be relied on, other than what follows from the above.
Results may differ from a plain program's by a relative error of at most 0.035.
Values may be sent and summed in bfloat16 or wider, within the bound.
No kernel may reach another device: no remote copies, remote signals or barrier semaphores. Data moves between devices by JAX's collectives and lax.ppermute only.
A program may use at most 192 MiB of HBM per device.

v0:
```python
import jax
import jax.numpy as jnp
from jax import lax
from jax.sharding import PartitionSpec as P

EPSILON = 1e-05


def shortened(array):

    def short(part):
        return part.astype(jnp.bfloat16) if part.dtype == jnp.float32 else part

    return jax.tree.map(short, array)


def conv_plain(inputs, kernel):
    return lax.conv_general_dilated(
        inputs,
        kernel,
        (1, 1),
        "SAME",
        dimension_numbers=("NHWC", "HWIO", "NHWC"),
        preferred_element_type=jnp.float32,
    )


def group_conv(inputs, kernel):
    return jax.vmap(conv_plain)(inputs, kernel)


def pooled(values):
    dims_in = values.shape
    blocks = values.reshape(dims_in[:-3] + (dims_in[-3] // 2, 2, dims_in[-2] // 2, 2, dims_in[-1]))
    return jnp.mean(blocks, axis=(-4, -2))


def unpooled(incoming):
    return 0.25 * jnp.repeat(jnp.repeat(incoming, 2, axis=-3), 2, axis=-2)


def silu_slope(values):
    sigma_v = jax.nn.sigmoid(values)
    return sigma_v * (1.0 + values * (1.0 - sigma_v))


def as_tasks(per_task):
    return per_task[:, None, None, None, :]


def batch_count(values, norm_axes):
    entries = lax.axis_size("img")
    for axis_no in norm_axes:
        entries = entries * values.shape[axis_no]
    return entries


def norm_forward(values, gain_rows, offset, norm_axes):
    partial_sums = (
        jnp.sum(values, axis=norm_axes, keepdims=True),
        jnp.sum(values * values, axis=norm_axes, keepdims=True),
    )
    value_sum, square_sum = lax.psum((partial_sums[0], partial_sums[1]), "img")
    entries = batch_count(values, norm_axes)
    center = value_sum / entries
    spread = square_sum / entries - center * center
    inverse = lax.rsqrt(spread + EPSILON)
    normal = (values - center) * inverse
    return (normal * gain_rows + offset, normal, inverse)


def norm_backward(upstream, normal, inverse, gain_rows, norm_axes):
    partial_sums = (
        jnp.sum(upstream, axis=norm_axes, keepdims=True),
        jnp.sum(upstream * normal, axis=norm_axes, keepdims=True),
    )
    shift_grad, gain_grad = lax.psum((partial_sums[0], partial_sums[1]), "img")
    entries = batch_count(upstream, norm_axes)
    result = gain_rows * inverse * (upstream - shift_grad / entries - normal * gain_grad / entries)
    return (result, gain_grad, shift_grad)


def conv_forward(shard, kernel):
    gathered = lax.all_gather(shard, "ch", axis=4, tiled=True)
    return (group_conv(gathered, kernel), gathered)


def weight_terms(inputs, incoming):
    height = inputs.shape[2]
    breadth = inputs.shape[3]
    padded = jnp.pad(inputs, ((0, 0), (0, 0), (1, 1), (1, 1), (0, 0)))
    kernel_rows = []
    for row_no in range(3):
        kernel_cols = []
        for col_no in range(3):
            window = padded[:, :, row_no : row_no + height, col_no : col_no + breadth, :]
            kernel_cols.append(
                jnp.einsum("gnhwc,gnhwd->gcd", window, incoming, preferred_element_type=jnp.float32)
            )
        kernel_rows.append(jnp.stack(kernel_cols, 1))
    return jnp.stack(kernel_rows, 1)


def weight_grad(kept_input, incoming):
    kernel_terms = weight_terms(kept_input, incoming)
    return lax.psum_scatter(kernel_terms, "img", scatter_dimension=3, tiled=True)


def input_grad(incoming, kernel):
    flipped = jnp.swapaxes(jnp.flip(kernel, (1, 2)), 3, 4)
    partial_value = group_conv(incoming, flipped)
    return jax.tree.map(
        lambda part: part.astype(jnp.float32),
        lax.psum_scatter(shortened(partial_value), "ch", scatter_dimension=4, tiled=True),
    )


def layer_forward(
    inputs, previous, shared_k, task_k, down_k, up_k, gain_rows, offset, bottle_g, bottle_s
):
    first_in = inputs.astype(jnp.bfloat16)[None]
    conv_one, kept_one = conv_forward(first_in, shared_k[0][None])
    norm_one, normal_one, inverse_one = norm_forward(conv_one, gain_rows[0], offset[0], (1, 2, 3))
    act_one = jax.nn.silu(norm_one)
    low_one = act_one.astype(jnp.bfloat16)
    conv_two, kept_two = conv_forward(low_one, shared_k[1][None])
    norm_two, normal_two, inverse_two = norm_forward(conv_two, gain_rows[1], offset[1], (1, 2, 3))
    act_two = jax.nn.silu(norm_two)
    if previous is None:
        attend = low_one
        bottle = jnp.einsum(
            "nhwc,tcb->tnhwb", low_one[0], down_k, preferred_element_type=jnp.float32
        )
    else:
        attend = (act_one + previous).astype(jnp.bfloat16)
        bottle = jnp.einsum("tnhwc,tcb->tnhwb", attend, down_k, preferred_element_type=jnp.float32)
    bottle = lax.psum(bottle.astype(jnp.bfloat16), "ch").astype(jnp.float32)
    bottle_norm, bottle_normal, bottle_inverse = norm_forward(
        bottle, as_tasks(bottle_g), as_tasks(bottle_s), (1, 2, 3)
    )
    hidden = jax.nn.silu(bottle_norm).astype(jnp.bfloat16)
    expand = jnp.einsum("tnhwb,tbc->tnhwc", hidden, up_k, preferred_element_type=jnp.float32)
    gate_norm, gate_normal, gate_inverse = norm_forward(
        expand, as_tasks(gain_rows[5:8]), as_tasks(offset[5:8]), (1, 2, 3)
    )
    gating = jax.nn.sigmoid(gate_norm)
    masked = (gating * act_two).astype(jnp.bfloat16)
    task_conv, kept_task = conv_forward(masked, task_k)
    task_norm, task_normal, task_inverse = norm_forward(
        task_conv, as_tasks(gain_rows[2:5]), as_tasks(offset[2:5]), (1, 2, 3)
    )
    task_act = jax.nn.silu(task_norm)
    kept_state = (
        kept_one,
        norm_one,
        normal_one,
        inverse_one,
        kept_two,
        norm_two,
        normal_two,
        inverse_two,
        act_two,
        attend,
        bottle_norm,
        bottle_normal,
        bottle_inverse,
        hidden,
        gate_normal,
        gate_inverse,
        gating,
        kept_task,
        task_norm,
        task_normal,
        task_inverse,
    )
    return (pooled(act_two[0]), pooled(task_act), kept_state)


def layer_backward(
    kept_state,
    grad_shared,
    grad_tasks,
    shared_k,
    task_k,
    down_k,
    up_k,
    gain_rows,
    bottle_g,
    first_layer,
):
    (
        kept_one,
        norm_one,
        normal_one,
        inverse_one,
        kept_two,
        norm_two,
        normal_two,
        inverse_two,
        act_two,
        attend,
        bottle_norm,
        bottle_normal,
        bottle_inverse,
        hidden,
        gate_normal,
        gate_inverse,
        gating,
        kept_task,
        task_norm,
        task_normal,
        task_inverse,
    ) = kept_state
    task_upstream = unpooled(grad_tasks) * silu_slope(task_norm)
    grad_task_conv, task_gain_grad, task_shift_grad = norm_backward(
        task_upstream, task_normal, task_inverse, as_tasks(gain_rows[2:5]), (1, 2, 3)
    )
    grad_task_conv = grad_task_conv.astype(jnp.bfloat16)
    task_kernel_grad = weight_grad(kept_task, grad_task_conv)
    grad_masked = input_grad(grad_task_conv, task_k)
    grad_two = unpooled(grad_shared)[None] + jnp.sum(grad_masked * gating, axis=0, keepdims=True)
    gate_upstream = grad_masked * act_two * gating * (1.0 - gating)
    grad_expand, gate_gain_grad, gate_shift_grad = norm_backward(
        gate_upstream, gate_normal, gate_inverse, as_tasks(gain_rows[5:8]), (1, 2, 3)
    )
    grad_expand = grad_expand.astype(jnp.bfloat16)
    up_grad = jnp.einsum(
        "tnhwb,tnhwc->tbc", hidden, grad_expand, preferred_element_type=jnp.float32
    )
    grad_hidden = lax.psum(
        jnp.einsum(
            "tnhwc,tbc->tnhwb", grad_expand, up_k, preferred_element_type=jnp.float32
        ).astype(jnp.bfloat16),
        "ch",
    ).astype(jnp.float32)
    grad_bottle, bottle_gain_grad, bottle_shift_grad = norm_backward(
        grad_hidden * silu_slope(bottle_norm),
        bottle_normal,
        bottle_inverse,
        as_tasks(bottle_g),
        (1, 2, 3),
    )
    grad_bottle = grad_bottle.astype(jnp.bfloat16)
    grad_attend = jnp.einsum(
        "tnhwb,tcb->tnhwc", grad_bottle, down_k, preferred_element_type=jnp.float32
    )
    if first_layer:
        down_grad = jnp.einsum(
            "nhwc,tnhwb->tcb", attend[0], grad_bottle, preferred_element_type=jnp.float32
        )
        grad_previous = None
    else:
        down_grad = jnp.einsum(
            "tnhwc,tnhwb->tcb", attend, grad_bottle, preferred_element_type=jnp.float32
        )
        grad_previous = grad_attend
    down_grad, up_grad = lax.psum((down_grad, up_grad), "img")
    grad_conv_two, gain_two, shift_two = norm_backward(
        grad_two * silu_slope(norm_two), normal_two, inverse_two, gain_rows[1], (1, 2, 3)
    )
    grad_conv_two = grad_conv_two.astype(jnp.bfloat16)
    kernel_two = weight_grad(kept_two, grad_conv_two)
    grad_one = input_grad(grad_conv_two, shared_k[1][None]) + jnp.sum(
        grad_attend, axis=0, keepdims=True
    )
    grad_conv_one, gain_one, shift_one = norm_backward(
        grad_one * silu_slope(norm_one), normal_one, inverse_one, gain_rows[0], (1, 2, 3)
    )
    grad_conv_one = grad_conv_one.astype(jnp.bfloat16)
    kernel_one = weight_grad(kept_one, grad_conv_one)
    grad_inputs = input_grad(grad_conv_one, shared_k[0][None])[0]
    task_count = task_k.shape[0]
    gain_table = jnp.concatenate(
        [
            gain_one.reshape(1, -1),
            gain_two.reshape(1, -1),
            task_gain_grad.reshape(task_count, -1),
            gate_gain_grad.reshape(task_count, -1),
        ],
        0,
    )
    shift_table = jnp.concatenate(
        [
            shift_one.reshape(1, -1),
            shift_two.reshape(1, -1),
            task_shift_grad.reshape(task_count, -1),
            gate_shift_grad.reshape(task_count, -1),
        ],
        0,
    )
    layer_grads = (
        jnp.concatenate([kernel_one, kernel_two], 0),
        task_kernel_grad,
        down_grad,
        up_grad,
        gain_table,
        shift_table,
        bottle_gain_grad.reshape(task_count, -1),
        bottle_shift_grad.reshape(task_count, -1),
    )
    return (grad_inputs, grad_previous, layer_grads)


def on_device(
    feats,
    shared_w,
    task_w,
    down_w,
    up_w,
    norm_gain,
    norm_shift,
    bottle_gain,
    bottle_shift,
    seg_mask,
    depth_mask,
    shared_cot,
    task_cot,
):
    layer_count = shared_w.shape[0]
    inputs = feats
    previous = None
    states_all = []
    for layer_no in range(layer_count):
        inputs, previous, kept_state = layer_forward(
            inputs,
            previous,
            shared_w[layer_no],
            task_w[layer_no],
            down_w[layer_no],
            up_w[layer_no],
            norm_gain[layer_no],
            norm_shift[layer_no],
            bottle_gain[layer_no],
            bottle_shift[layer_no],
        )
        states_all.append(kept_state)
    shared_out = inputs.astype(jnp.bfloat16)
    task_out = previous.astype(jnp.bfloat16)
    scales = jnp.stack([seg_mask, depth_mask, jnp.ones_like(seg_mask)]).astype(jnp.float32)
    grad_shared = shared_cot.astype(jnp.float32)
    grad_tasks = task_cot.astype(jnp.float32) * scales[..., None]
    grads_all = [None] * layer_count
    for layer_no in range(layer_count - 1, -1, -1):
        grad_shared, grad_tasks, grads_all[layer_no] = layer_backward(
            states_all[layer_no],
            grad_shared,
            grad_tasks,
            shared_w[layer_no],
            task_w[layer_no],
            down_w[layer_no],
            up_w[layer_no],
            norm_gain[layer_no],
            bottle_gain[layer_no],
            layer_no == 0,
        )
    stacked = [jnp.stack([entry[member] for entry in grads_all]) for member in range(8)]
    return (
        shared_out,
        task_out,
        grad_shared,
        stacked[0],
        stacked[1],
        stacked[2],
        stacked[3],
        stacked[4],
        stacked[5],
        stacked[6],
        stacked[7],
    )


def solution(mesh):
    placed = (
        P("img", None, None, "ch"),
        P(None, None, None, None, None, "ch"),
        P(None, None, None, None, None, "ch"),
        P(None, None, "ch", None),
        P(None, None, None, "ch"),
        P(None, None, "ch"),
        P(None, None, "ch"),
        P(),
        P(),
        P("img", None, None),
        P("img", None, None),
        P("img", None, None, "ch"),
        P(None, "img", None, None, "ch"),
    )
    return jax.shard_map(
        on_device,
        mesh=mesh,
        in_specs=placed,
        out_specs=(
            P("img", None, None, "ch"),
            P(None, "img", None, None, "ch"),
            P("img", None, None, "ch"),
            P(None, None, None, None, "img", "ch"),
            P(None, None, None, None, "img", "ch"),
            P(None, None, "ch", None),
            P(None, None, None, "ch"),
            P(None, None, "ch"),
            P(None, None, "ch"),
            P(),
            P(),
        ),
        check_vma=False,
    )
```

profile of v0, /device:TPU:0, one launch (start us, length us, event | category | flops | bytes accessed | tf_op | source)
XLA Modules:
  0.0 1423.7 jit_solution(5309524279456798271)
XLA Ops:
  21.3 21.7 %all-reduce.19 = (f32[1,1,1,1,128]{4,3,2,1,0:T(1,128)S(1)}, f32[1,1,1,1,128]{4,3,2,1,0:T(1,128)S(1)}) all-reduce(f32[1,1,1,1,128]{4,3,2,1,0:T(1,128)S(1)} %bitcast.1335, f32[1,1,1,1,128]{4,3,2,1,0:T(1,128)S(1)} %bitcast.1334), channel_id=1, replica_groups=mesh['img'=8,'ch'=4] {'img'}, use_global_device_ids=true, to_apply=%region_3.0 | all-reduce | flops 256 | bytes 2048 | tf_op jit(solution)/shard_map/psum | solution.py:63
  76.3 21.4 %all-reduce.18 = (f32[3,1,1,1,128]{4,0,3,2,1:T(4,128)S(1)}, f32[3,1,1,1,128]{4,0,3,2,1:T(4,128)S(1)}) all-reduce(f32[3,1,1,1,128]{4,0,3,2,1:T(4,128)S(1)} %bitcast.1277, f32[3,1,1,1,128]{4,0,3,2,1:T(4,128)S(1)} %bitcast.1276), channel_id=1, replica_groups=mesh['img'=8,'ch'=4] {'img'}, use_global_device_ids=true, to_apply=%region_20.21 | all-reduce | flops 768 | bytes 6144 | tf_op jit(solution)/shard_map/psum | solution.py:63
  141.0 36.1 %multiply_reduce_fusion.1 = (f32[3,128]{1,0:T(4,128)S(1)}, f32[3,128]{1,0:T(4,128)S(1)}, f32[3,1,24,24,128]{4,1,0,3,2:T(1,128)S(1)}) fusion(bf16[1,3,3,3,512,128]{5,4,3,2,1,0:T(8,128)(2,1)} %get-tuple-element.162, bf16[3,1,24,24,512]{4,3,2,0,1:T(8,128)(2,1)} %bitcast.1323), kind=kOutput, calls=%fused_computation.215 | convolution fusion | flops 1927421184 | bytes 6196224 | tf_op jit(solution)/shard_map/vmap()/transpose | solution.py:29
  177.1 21.6 %all-reduce.16 = (f32[1,1,1,1,128]{4,3,2,1,0:T(1,128)S(1)}, f32[1,1,1,1,128]{4,3,2,1,0:T(1,128)S(1)}, f32[3,1,1,1,128]{4,0,3,2,1:T(4,128)S(1)}, f32[3,1,1,1,128]{4,0,3,2,1:T(4,128)S(1)}) all-reduce(f32[1,1,1,1,128]{4,3,2,1,0:T(1,128)S(1)} %bitcast.1322, ...), channel_id=1, replica_groups=mesh['img'=8,'ch'=4] {'img'}, use_global_device_ids=true, to_apply=%region_12.13 | all-reduce | flops 1024 | bytes 8192 | tf_op jit(solution)/shard_map/psum | solution.py:63
  211.2 24.4 %all-reduce.29.cloned.1.call-done = bf16[3,1,12,12,128]{4,3,2,0,1:T(8,128)(2,1)} async-done(((bf16[3,1,12,12,128]{4,3,2,0,1:T(8,128)(2,1)}), bf16[3,1,12,12,128]{4,3,2,0,1:T(8,128)(2,1)}) %all-reduce.29.cloned.1.call-update) | async-done | bytes 110608 | tf_op jit(solution)/shard_map/psum | solution.py:137
  236.5 21.4 %all-reduce.15 = (f32[3,1,1,1,128]{4,0,3,2,1:T(4,128)S(1)}, f32[3,1,1,1,128]{4,0,3,2,1:T(4,128)S(1)}) all-reduce(f32[3,1,1,1,128]{4,0,3,2,1:T(4,128)S(1)} %bitcast.1279, f32[3,1,1,1,128]{4,0,3,2,1:T(4,128)S(1)} %bitcast.1278), channel_id=1, replica_groups=mesh['img'=8,'ch'=4] {'img'}, use_global_device_ids=true, to_apply=%region_34.35 | all-reduce | flops 768 | bytes 6144 | tf_op jit(solution)/shard_map/psum | solution.py:63
  296.1 19.5 %all-reduce.13 = (f32[3,1,1,1,128]{4,0,3,2,1:T(4,128)S(1)}, f32[3,1,1,1,128]{4,0,3,2,1:T(4,128)S(1)}) all-reduce(f32[3,1,1,1,128]{4,0,3,2,1:T(4,128)S(1)} %bitcast.1310, f32[3,1,1,1,128]{4,0,3,2,1:T(4,128)S(1)} %bitcast.1309), channel_id=1, replica_groups=mesh['img'=8,'ch'=4] {'img'}, use_global_device_ids=true, to_apply=%region_42.43 | all-reduce | flops 768 | bytes 6144 | tf_op jit(solution)/shard_map/psum | solution.py:63
  382.1 21.4 %all-reduce.11 = (f32[3,128]{1,0:T(4,128)S(1)}, f32[3,1,1,1,128]{4,1,3,2,0:T(1,128)S(1)}) all-reduce(f32[3,128]{1,0:T(4,128)S(1)} %get-tuple-element.67, f32[3,1,1,1,128]{4,1,3,2,0:T(1,128)S(1)} %broadcast_in_dim.210), channel_id=1, replica_groups=mesh['img'=8,'ch'=4] {'img'}, use_global_device_ids=true, to_apply=%region_60.61 | all-reduce | flops 768 | bytes 6144 | tf_op jit(solution)/shard_map/psum | solution.py:77
  407.7 26.0 %all-reduce.31.cloned.1.call-done = bf16[3,1,12,12,128]{4,3,2,0,1:T(8,128)(2,1)} async-done(((bf16[3,1,12,12,128]{4,3,2,0,1:T(8,128)(2,1)}), bf16[3,1,12,12,128]{4,3,2,0,1:T(8,128)(2,1)}) %all-reduce.31.cloned.1.call-update) | async-done | bytes 110608 | tf_op jit(solution)/shard_map/psum | solution.py:230
  434.9 21.4 %all-reduce.10 = (f32[3,1,1,1,128]{4,1,3,2,0:T(1,128)S(1)}, f32[3,1,1,1,128]{4,1,3,2,0:T(1,128)S(1)}) all-reduce(f32[3,1,1,1,128]{4,1,3,2,0:T(1,128)S(1)} %broadcast_in_dim.213, f32[3,1,1,1,128]{4,1,3,2,0:T(1,128)S(1)} %broadcast_in_dim.212), channel_id=1, replica_groups=mesh['img'=8,'ch'=4] {'img'}, use_global_device_ids=true, to_apply=%region_65.66 | all-reduce | flops 768 | bytes 6144 | tf_op jit(solution)/shard_map/psum | solution.py:77
  479.3 34.5 %copy.320 = bf16[1,1,12,12,512]{0,3,2,1,4:T(8,128)(2,1)} copy(bf16[1,1,12,12,512]{4,0,3,2,1:T(2,128)(2,1)S(1)} %fusion.84) | data formatting | bytes 294912
  513.8 18.7 %bitcast_reduce_fusion = bf16[512,12,12]{2,1,0:T(8,128)(2,1)S(1)} fusion(bf16[1,1,12,12,512]{0,3,2,1,4:T(8,128)(2,1)} %copy.320), kind=kLoop, calls=%fused_computation | loop fusion | bytes 294912
  536.7 22.1 %convolution_convert_fusion = bf16[3,1,24,24,512]{4,1,0,3,2:T(2,128)(2,1)} fusion(bf16[1,3,3,3,512,128]{5,4,3,2,1,0:T(8,128)(2,1)} %get-tuple-element.162, bf16[3,1,24,24,128]{4,3,0,2,1:T(8,128)(2,1)S(1)} %multiply_convert_fusion), kind=kOutput, calls=%fused_computation.3 | convolution fusion | flops 1927643136 | bytes 5750784 | tf_op jit(solution)/shard_map/vmap()/transpose | solution.py:29
  626.3 19.5 %all-reduce.8 = (f32[3,128]{1,0:T(4,128)S(1)}, f32[3,1,1,1,128]{4,0,3,2,1:T(4,128)S(1)}, f32[1,1,1,1,128]{4,3,2,1,0:T(1,128)S(1)}, f32[1,1,1,1,128]{4,3,2,1,0:T(1,128)S(1)}) all-reduce(f32[3,128]{1,0:T(4,128)S(1)} %get-tuple-element.56, f32[3,1,1,1,128]{4,0,3,2,1:T(4,128)S(1)} %bitcast.1287, ...), channel_id=1, replica_groups=mesh['img'=8,'ch'=4] {'img'}, use_global_device_ids=true, to_apply=%region_86.87 | all-reduce | flops 1024 | bytes 8192 | tf_op jit(solution)/shard_map/psum | solution.py:77
  655.4 23.4 %all-reduce.33.cloned.1.call-done = bf16[3,1,24,24,128]{4,3,0,2,1:T(8,128)(2,1)} async-done(((bf16[3,1,24,24,128]{4,3,0,2,1:T(8,128)(2,1)}), bf16[3,1,24,24,128]{4,3,0,2,1:T(8,128)(2,1)}) %all-reduce.33.cloned.1.call-update) | async-done | bytes 442384 | tf_op jit(solution)/shard_map/psum | solution.py:230
  681.2 20.4 %reduce-scatter.41.cloned.1.call-done = bf16[128,144]{1,0:T(8,128)(2,1)} async-done(((bf16[512,144]{1,0:T(8,128)(2,1)}), bf16[128,144]{1,0:T(8,128)(2,1)}) %reduce-scatter.41.cloned.1.call-update) | async-done | bytes 36880
  703.7 21.7 %all-reduce.7 = (f32[3,1,1,1,128]{4,1,3,2,0:T(1,128)S(1)}, f32[3,1,1,1,128]{4,0,3,2,1:T(4,128)S(1)}, f32[1,1,1,1,128]{4,3,2,1,0:T(1,128)S(1)}, f32[1,1,1,1,128]{4,3,2,1,0:T(1,128)S(1)}) all-reduce(f32[3,1,1,1,128]{4,1,3,2,0:T(1,128)S(1)} %broadcast_in_dim.230, ...), channel_id=1, replica_groups=mesh['img'=8,'ch'=4] {'img'}, use_global_device_ids=true, to_apply=%region_91.92 | all-reduce | flops 1024 | bytes 8192 | tf_op jit(solution)/shard_map/psum | solution.py:77
  756.8 21.5 %all-reduce.6 = (f32[1,1,1,1,128]{4,3,2,1,0:T(1,128)S(1)}, f32[1,1,1,1,128]{4,3,2,1,0:T(1,128)S(1)}) all-reduce(f32[1,1,1,1,128]{4,3,2,1,0:T(1,128)S(1)} %bitcast.1333, f32[1,1,1,1,128]{4,3,2,1,0:T(1,128)S(1)} %bitcast.1332), channel_id=1, replica_groups=mesh['img'=8,'ch'=4] {'img'}, use_global_device_ids=true, to_apply=%region_95.96 | all-reduce | flops 256 | bytes 2048 | tf_op jit(solution)/shard_map/psum | solution.py:77
  861.5 70.6 %reduce-scatter.31.cloned.1.call-done = f32[1,3,3,64,128]{4,3,2,1,0:T(8,128)} async-done(((f32[1,3,3,512,128]{4,3,2,1,0:T(8,128)}), f32[1,3,3,64,128]{4,3,2,1,0:T(8,128)}) %reduce-scatter.31.cloned.1.call-update) | async-done | bytes 294928 | tf_op jit(solution)/shard_map/reduce_scatter | solution.py:106
  932.1 72.3 %reduce-scatter.29.cloned.1.call-done = f32[1,3,3,64,128]{4,3,2,1,0:T(8,128)} async-done(((f32[1,3,3,512,128]{4,3,2,1,0:T(8,128)}), f32[1,3,3,64,128]{4,3,2,1,0:T(8,128)}) %reduce-scatter.29.cloned.1.call-update) | async-done | bytes 294928 | tf_op jit(solution)/shard_map/reduce_scatter | solution.py:106
  1005.5 71.2 %reduce-scatter.27.cloned.1.call-done = f32[1,3,3,64,128]{4,3,2,1,0:T(8,128)} async-done(((f32[1,3,3,512,128]{4,3,2,1,0:T(8,128)}), f32[1,3,3,64,128]{4,3,2,1,0:T(8,128)}) %reduce-scatter.27.cloned.1.call-update) | async-done | bytes 294928 | tf_op jit(solution)/shard_map/reduce_scatter | solution.py:106
  1076.6 72.2 %reduce-scatter.25.cloned.1.call-done = f32[1,3,3,64,128]{4,3,2,1,0:T(8,128)} async-done(((f32[1,3,3,512,128]{4,3,2,1,0:T(8,128)}), f32[1,3,3,64,128]{4,3,2,1,0:T(8,128)}) %reduce-scatter.25.cloned.1.call-update) | async-done | bytes 294928 | tf_op jit(solution)/shard_map/reduce_scatter | solution.py:106
  1151.1 130.2 %reduce-scatter.35.cloned.1.call-done = f32[3,3,3,64,128]{4,3,0,2,1:T(8,128)} async-done(((f32[3,3,3,512,128]{4,3,0,2,1:T(8,128)}), f32[3,3,3,64,128]{4,3,0,2,1:T(8,128)}) %reduce-scatter.35.cloned.1.call-update) | async-done | bytes 884752 | tf_op jit(solution)/shard_map/reduce_scatter | solution.py:106
  1281.3 132.0 %reduce-scatter.33.cloned.1.call-done = f32[3,3,3,64,128]{4,3,0,2,1:T(8,128)} async-done(((f32[3,3,3,512,128]{4,3,0,2,1:T(8,128)}), f32[3,3,3,64,128]{4,3,0,2,1:T(8,128)}) %reduce-scatter.33.cloned.1.call-update) | async-done | bytes 884752 | tf_op jit(solution)/shard_map/reduce_scatter | solution.py:106
  (736 shorter events, 440.6 us)
Async XLA Ops:
  7.2 68.0 %all-reduce.27.cloned.1.call-start = ((), (), s32[]{:S(2)}) async-start(), calls=%async_computation.12 | async-start | bytes 884736 | tf_op jit(solution)/shard_map/psum | solution.py:137
  17.9 181.4 %copy-start.125 = (f32[128]{0:T(128)}, f32[128]{0:T(128)S(1)}, u32[]{:S(2)}) copy-start(f32[128]{0:T(128)S(1)} %get-tuple-element.195) | copy-start | bytes 1540
  17.9 181.4 %copy-start.127 = (f32[128]{0:T(128)}, f32[128]{0:T(128)S(1)}, u32[]{:S(2)}) copy-start(f32[128]{0:T(128)S(1)} %get-tuple-element.231) | copy-start | bytes 1540
  45.5 95.5 %all-gather.6.cloned.1.call-start = ((), (), s32[]{:S(2)}) async-start(), calls=%async_computation.22 | async-start | bytes 2211840 | tf_op jit(solution)/shard_map/all_gather | solution.py:84
  46.1 160.0 %copy-start.107 = (f32[3,128]{1,0:T(4,128)}, f32[3,128]{1,0:T(4,128)S(1)}, u32[]{:S(2)}) copy-start(f32[3,128]{1,0:T(4,128)S(1)} %get-tuple-element.187) | copy-start | bytes 4612
  46.1 160.0 %copy-start.109 = (f32[3,128]{1,0:T(4,128)}, f32[3,128]{1,0:T(4,128)S(1)}, u32[]{:S(2)}) copy-start(f32[3,128]{1,0:T(4,128)S(1)} %get-tuple-element.237) | copy-start | bytes 4612
  120.9 114.7 %all-reduce.29.cloned.1.call-start = ((), (), s32[]{:S(2)}) async-start(), calls=%async_computation.13 | async-start | bytes 294912 | tf_op jit(solution)/shard_map/psum | solution.py:137
  177.1 281.1 %copy-start = (f32[3,1,24,24,128]{4,1,0,3,2:T(1,128)}, f32[3,1,24,24,128]{4,1,0,3,2:T(1,128)S(1)}, u32[]{:S(2)}) copy-start(f32[3,1,24,24,128]{4,1,0,3,2:T(1,128)S(1)} %get-tuple-element.224) | copy-start | bytes 2654212
  208.4 168.2 %reduce-scatter.37.cloned.1.call-start = ((), (), s32[]{:S(2)}) async-start(), calls=%async_computation.23 | async-start | bytes 655360
  211.2 266.6 %copy-start.29 = (f32[1,12,12,128]{3,0,2,1:T(1,128)}, f32[1,12,12,128]{3,0,2,1:T(1,128)S(1)}, u32[]{:S(2)}) copy-start(f32[1,12,12,128]{3,0,2,1:T(1,128)S(1)} %get-tuple-element.225) | copy-start | bytes 221188
  356.9 76.8 %all-reduce.31.cloned.1.call-start = ((), (), s32[]{:S(2)}) async-start(), calls=%async_computation.14 | async-start | bytes 294912 | tf_op jit(solution)/shard_map/psum | solution.py:230
  406.5 194.2 %reduce-scatter.39.cloned.1.call-start = ((), (), s32[]{:S(2)}) async-start(), calls=%async_computation.24 | async-start | bytes 327680
  535.0 84.1 %reduce-scatter.43.cloned.1.call-start = ((), (), s32[]{:S(2)}) async-start(), calls=%async_computation.26 | async-start | bytes 2293760
  586.0 92.7 %all-reduce.33.cloned.1.call-start = ((), (), s32[]{:S(2)}) async-start(), calls=%async_computation.15 | async-start | bytes 884736 | tf_op jit(solution)/shard_map/psum | solution.py:230
  648.7 52.9 %reduce-scatter.41.cloned.1.call-start = ((), (), s32[]{:S(2)}) async-start(), calls=%async_computation.25 | async-start | bytes 327680
  654.9 99.4 %reduce-scatter.45.cloned.1.call-start = ((), (), s32[]{:S(2)}) async-start(), calls=%async_computation.27 | async-start | bytes 819200
  735.4 102.4 %all-reduce.35.cloned.1.call-start = ((), (), s32[]{:S(2)}) async-start(), calls=%async_computation.29 | async-start | bytes 1572864 | tf_op jit(solution)/shard_map/psum | solution.py:257
  742.0 116.7 %reduce-scatter.47.cloned.1.call-start = ((), (), s32[]{:S(2)}) async-start(), calls=%async_computation.28 | async-start | bytes 819200
  787.6 144.5 %reduce-scatter.31.cloned.1.call-start = ((), (), s32[]{:S(2)}) async-start(), calls=%async_computation.19 | async-start | bytes 2654208 | tf_op jit(solution)/shard_map/reduce_scatter | solution.py:106
  793.3 211.1 %reduce-scatter.29.cloned.1.call-start = ((), (), s32[]{:S(2)}) async-start(), calls=%async_computation.18 | async-start | bytes 2654208 | tf_op jit(solution)/shard_map/reduce_scatter | solution.py:106
  798.5 278.1 %reduce-scatter.27.cloned.1.call-start = ((), (), s32[]{:S(2)}) async-start(), calls=%async_computation.17 | async-start | bytes 2654208 | tf_op jit(solution)/shard_map/reduce_scatter | solution.py:106
  804.9 344.0 %reduce-scatter.25.cloned.1.call-start = ((), (), s32[]{:S(2)}) async-start(), calls=%async_computation.16 | async-start | bytes 2654208 | tf_op jit(solution)/shard_map/reduce_scatter | solution.py:106
  811.2 470.1 %reduce-scatter.35.cloned.1.call-start = ((), (), s32[]{:S(2)}) async-start(), calls=%async_computation.21 | async-start | bytes 7962624 | tf_op jit(solution)/shard_map/reduce_scatter | solution.py:106
  820.3 593.0 %reduce-scatter.33.cloned.1.call-start = ((), (), s32[]{:S(2)}) async-start(), calls=%async_computation.20 | async-start | bytes 7962624 | tf_op jit(solution)/shard_map/reduce_scatter | solution.py:106
  (198 other events, 3476.8 us)
Sparse Core Ops, SparseCore 0:
  45.6 29.5 all-reduce.26
  120.9 19.9 all-gather.5
  208.4 27.0 all-reduce.28
  357.0 19.5 reduce-scatter.36
  406.6 27.0 all-reduce.30
  535.1 18.5 reduce-scatter.38
  586.2 28.3 reduce-scatter.42
  648.8 29.8 all-reduce.32
  681.4 20.2 reduce-scatter.40
  735.5 18.7 reduce-scatter.44
  758.6 75.3 all-reduce.34
  837.2 21.4 reduce-scatter.46
  862.6 69.4 reduce-scatter.30
  935.9 68.4 reduce-scatter.28
  1008.1 68.4 reduce-scatter.26
  1080.4 68.4 reduce-scatter.24
  1152.9 128.3 reduce-scatter.34
  1284.9 128.4 reduce-scatter.32
where the time goes:
time: 1440 us; the launch traced here: 1420 us
  waiting for transfers between devices  699 us (49%)
  blocking collectives  319 us (22%)
  local copies, waits for them, and re-layouts  195 us (14%)
  matrix products  134 us (9%)
  other arithmetic  57 us (4%)
  between operations  18 us (1%)
    reduce_scatter x6, waiting for transfers between devices, weight_grad(): lax.psum_scatter(kernel_terms, 'img', scatter_dimension=3, tiled=True)  549 us
    unnamed x446, local copies, waits for them, and re-layouts  164 us
    psum x7, blocking collectives, norm_forward(): value_sum, square_sum = lax.psum((partial_sums[0], partial_sums[1]), 'img')  140 us
    psum x7, blocking collectives, norm_backward(): shift_grad, gain_grad = lax.psum((partial_sums[0], partial_sums[1]), 'img')  140 us
    transpose x4, matrix products, group_conv(): return jax.vmap(conv_plain)(inputs, kernel)  75.7 us
    unnamed x24, waiting for transfers between devices  63.1 us
    psum x2, waiting for transfers between devices, layer_backward(): lax.psum(jnp.einsum('tnhwc,tbc->tnhwb', grad_expand, up_k, preferred_elem...  49.3 us
    all_gather x5, blocking collectives, conv_forward(): gathered = lax.all_gather(shard, 'ch', axis=4, tiled=True)  38.8 us
  transfers between devices with their start and end apart: 18, of which 15 were waited for; matrix products, arithmetic and copies ran while one was open for 13% of the time, Pallas kernels for 0%

commit v1 on v0

v1 whole, which is shorter than its diff:
```python
import functools

import jax
import jax.numpy as jnp
from jax import lax
from jax.experimental import pallas as pl
from jax.experimental.pallas import tpu as pltpu
from jax.sharding import PartitionSpec as P

EPSILON = 1e-05
F32 = jnp.float32
LOW = jnp.bfloat16
VMEM_LIMIT = 16 * 2**20


def sigmoid(v):
    return 0.5 * jnp.tanh(0.5 * v) + 0.5


def silu_slope(v, s):
    return s * (1.0 + v * (1.0 - s))


def dot(a, b):
    return lax.dot_general(a, b, (((1,), (0,)), ((), ())), preferred_element_type=F32)


def dot_nt(a, b):
    return lax.dot_general(a, b, (((1,), (1,)), ((), ())), preferred_element_type=F32)


def dot_tn(a, b):
    return lax.dot_general(a, b, (((0,), (0,)), ((), ())), preferred_element_type=F32)


def sums(v):
    return jnp.sum(v, axis=0, keepdims=True)


def column_of(shape, width):
    place = lax.broadcasted_iota(jnp.int32, shape, 0)
    row = (place * (2731 if width == 24 else 5462)) >> 16
    return place - row * width


def move_columns(v, step, width):
    if step == 0:
        return v
    column = column_of(v.shape, width)
    keep = column < width - 1 if step == 1 else column > 0
    return jnp.where(keep, pltpu.roll(v, (-step) % v.shape[0], 0), 0.0)


def move_rows(v, step, width):
    if step == 0:
        return v
    size = v.shape[0]
    place = lax.broadcasted_iota(jnp.int32, v.shape, 0)
    keep = place < size - width if step == 1 else place >= width
    return jnp.where(keep, pltpu.roll(v, (-step * width) % size, 0), 0.0)


def centre(total, count):
    mean = total[0:1] / count
    spread = total[1:2] / count - mean * mean
    return mean, lax.rsqrt(spread + EPSILON)


def place_blocks(ch_ref, blocks, full_ref):
    own = ch_ref[0]
    for k, block in enumerate(blocks):
        start = pl.multiple_of((own ^ k) * 128, 128)
        full_ref[:, pl.ds(start, 128)] = block[...]


def conv(values, taps_ref, lead, width):
    total = None
    for col in range(3):
        kernel = jnp.concatenate([taps_ref[lead, 3 * row + col] for row in range(3)], 1)
        part = dot(values, kernel)
        line = part[:, 128:256]
        line = line + move_rows(part[:, 0:128], -1, width)
        line = line + move_rows(part[:, 256:384], 1, width)
        line = move_columns(line, col - 1, width)
        total = line if total is None else total + line
    return total


def spread_taps(grad, width, taps_out):
    for col in range(3):
        line = move_columns(grad, 1 - col, width)
        for row in range(3):
            tap = 3 * row + col
            taps_out[:, tap * 128 : tap * 128 + 128] = move_rows(line, 1 - row, width).astype(LOW)


def conv_back(taps_value, taps_ref, lead):
    kernel = jnp.concatenate([taps_ref[lead, tap] for tap in range(9)], 1)
    return dot_nt(taps_value, kernel)


def pool(v, scratch, width):
    size = v.shape[0]
    if width % 8 == 0:
        pairs = v.reshape(size // (2 * width), 2 * width, 128)
        rows = (pairs[:, :width] + pairs[:, width:]).reshape(size // 2, 128)
        scratch[0 : size // 2] = rows
        return 0.25 * (
            scratch[pl.ds(0, size // 4, stride=2)] + scratch[pl.ds(1, size // 4, stride=2)]
        )
    v = v + pltpu.roll(v, size - width, 0)
    v = v + pltpu.roll(v, size - 1, 0)
    scratch[...] = v
    half = scratch[pl.ds(0, size // 2, stride=2)]
    scratch[0 : size // 2] = half
    parts = [scratch[a * width : a * width + width // 2] for a in range(size // (2 * width))]
    return 0.25 * jnp.concatenate(parts, 0)


def unpool(v, scratch, width):
    size = 4 * v.shape[0]
    v = 0.25 * v
    scratch[pl.ds(0, size // 4, stride=2)] = v
    scratch[pl.ds(1, size // 4, stride=2)] = v
    rows = scratch[0 : size // 2]
    if width % 8 == 0:
        rows = rows.reshape(size // (2 * width), width, 128)
        return jnp.concatenate([rows, rows], 1).reshape(size, 128)
    parts = []
    for a in range(size // (2 * width)):
        part = rows[a * width : a * width + width]
        parts += [part, part]
    return jnp.concatenate(parts, 0)

def bn_of(total, row, count):
    return centre(total[row : row + 2], count)


def spread_stats(out, rows):
    for place, row in enumerate(rows):
        out[place : place + 1] = row


def moments(v):
    return [sums(v), sums(v * v)]


def pack_body(down, up, gain, shift, wide, narrow, params):
    for l in range(down.shape[0]):
        wide[l, 0] = down[l]
        wide[l, 1] = up[l]
        narrow[l, 0:3] = gain[l, 5:8]
        narrow[l, 3:6] = shift[l, 5:8]
        params[l, 0:8] = gain[l, 0:8]
        params[l, 8:16] = shift[l, 0:8]


def unpack_body(ch, w0, w1, w2, w3, n0, n1, n2, n3, down, up, gates):
    own = ch[0]
    for k, (wide, narrow) in enumerate(((w0, n0), (w1, n1), (w2, n2), (w3, n3))):
        start = pl.ds(pl.multiple_of((own ^ k) * 128, 128), 128)
        for l in range(down.shape[0]):
            for t in range(3):
                down[l, t, start, :] = wide[l, 0, t]
                up[l, t, :, start] = wide[l, 1, t]
            gates[l, :, start] = narrow[l]


def first_conv_body(width, lead, ch, x0, x1, x2, x3, taps, full, y, stats):
    place_blocks(ch, (x0, x1, x2, x3), full)
    flush(full)
    out = conv(full[...], taps, lead, width)
    y[...] = out
    spread_stats(stats, moments(out))


def next_conv_body(width, lead, skip, ch, x0, x1, x2, x3, taps, full, y, stats):
    own = ch[0]
    for k, block in enumerate((x0, x1, x2, x3)):
        start = pl.multiple_of((own ^ k) * 128, 128)
        full[:, pl.ds(start, 128)] = block[skip:]
    flush(full)
    out = conv(full[...], taps, lead, width)
    y[...] = out
    for place, row in enumerate(moments(out)):
        stats[place : place + 1] = row


def first_act_body(count, y, raw, gain, shift, low, again):
    mean, inverse = bn_of(raw, 0, count)
    v = (y[...] - mean) * inverse * gain[0, 0:1] + shift[0, 0:1]
    act = (v * sigmoid(v)).astype(LOW)
    low[...] = act
    again[...] = act


def second_conv_body(width, lead, ch, x0, x1, x2, x3, taps, down, full, y, p, stats):
    place_blocks(ch, (x0, x1, x2, x3), full)
    flush(full)
    values = full[...]
    out = conv(values, taps, lead, width)
    y[...] = out
    rows = moments(out)
    for t in range(3):
        part = dot(values, down[0, t])
        p[t] = part
        rows += moments(part)
    spread_stats(stats, rows)


def second_conv_next_body(width, lead, ch, x0, x1, x2, x3, taps, near, far, full, y, p, stats):
    place_blocks(ch, (x0, x1, x2, x3), full)
    flush(full)
    out = conv(full[...], taps, lead, width)
    y[...] = out
    rows = moments(out)
    for t in range(3):
        part = near[t].astype(F32) + far[t].astype(F32)
        p[t] = part
        rows += moments(part)
    spread_stats(stats, rows)


def hidden_body(l, count, width, y, p, raw, gain, shift, bgain, bshift, up, s, u, pooled_u, zstats, scratch):
    mean, inverse = bn_of(raw, 0, count)
    v = (y[...] - mean) * inverse * gain[l, 1:2] + shift[l, 1:2]
    act = v * sigmoid(v)
    size = y.shape[0]
    u[0:size] = act.astype(LOW)
    pooled = pool(act, scratch, width).astype(LOW)
    if pooled_u is None:
        u[size:] = pooled
    else:
        pooled_u[...] = pooled
    rows = []
    for t in range(3):
        mean, inverse = bn_of(raw, 2 + 2 * t, count)
        v = (p[t] - mean) * inverse * bgain[l, t : t + 1] + bshift[l, t : t + 1]
        low = (v * sigmoid(v)).astype(LOW)
        s[t] = low
        rows += moments(dot(low, up[l, t]))
    spread_stats(zstats, rows)


def task_conv_body(l, count, width, ch, s, up, u0, u1, u2, u3, zraw, gates, taps, more, k, y, stats, full, acc):
    size = s.shape[1]
    own = ch[0]
    for i, block in enumerate((u0, u1, u2, u3)):
        start = pl.multiple_of((own ^ i) * 128, 128)
        full[:, pl.ds(start, 128)] = block[0:size]
    ztotal = zraw[...]
    for t in range(3):
        mean, inverse = centre(ztotal[2 * t : 2 * t + 2], count)
        scale = inverse * gates[l, t : t + 1]
        v = dot(s[t], up[l, t]) * scale + (gates[l, 3 + t : 4 + t] - mean * scale)
        k[t] = (sigmoid(v) * full[...].astype(F32)).astype(LOW)
    flush(k)
    ready(taps)

    def one(t, carry):
        out = conv(k[t], taps, t, width)
        y[t] = out
        rows = moments(out)
        acc[t, 0:1] = rows[0]
        acc[t, 1:2] = rows[1]
        return carry

    lax.fori_loop(0, 3, one, 0)
    rows = [acc[t, i : i + 1] for t in range(3) for i in range(2)]
    if more is not None:
        rows += [more[0:1], more[1:2]]
    spread_stats(stats, rows)


def attend_body(count, count_next, width, yt, y, raw, gain, shift, down, low, g, part, scratch):
    mean, inverse = bn_of(raw, 6, count_next)
    v = (y[...] - mean) * inverse * gain[1, 0:1] + shift[1, 0:1]
    act = v * sigmoid(v)
    low[...] = act.astype(LOW)
    for t in range(3):
        mean, inverse = bn_of(raw, 2 * t, count)
        v = (yt[t] - mean) * inverse * gain[0, 2 + t : 3 + t] + shift[0, 2 + t : 3 + t]
        attend = (act + pool(v * sigmoid(v), scratch, width)).astype(LOW)
        g[t] = attend
        part[t] = dot(attend, down[1, t]).astype(LOW)


def pair_body(a, b, out):
    out[...] = (a[...].astype(F32) + b[...].astype(F32)).astype(LOW)


def pair_second_body(keep, far, got, out, part):
    out[...] = (far[...] + got[1].astype(F32)).astype(LOW)
    part[...] = keep[...] + got[0].astype(F32)


def mixed_body(a, b, out):
    out[...] = a[...] + b[...].astype(F32)


def stack_body(a, b, out):
    out[0] = a[...]
    out[1] = b[...]


def add_body(a, b, out):
    out[...] = (a[...].astype(F32) + b[...].astype(F32)).astype(out.dtype)


def sum_body(*refs):
    parts = [ref[...] for ref in refs[:-1]]
    while len(parts) > 1:
        parts = [a + b for a, b in zip(parts[::2], parts[1::2])]
    refs[-1][...] = parts[0]


def task_last_body(l, count, width, y, raw, gain, shift, dq, out, d, stats, scratch):
    rows = []
    for t in range(3):
        mean, inverse = bn_of(raw, 2 * t, count)
        normal = (y[t] - mean) * inverse
        v = normal * gain[l, 2 + t : 3 + t] + shift[l, 2 + t : 3 + t]
        sg = sigmoid(v)
        out[t] = pool(v * sg, scratch, width).astype(LOW)
        grad = unpool(dq[t], scratch, width) * silu_slope(v, sg)
        d[t] = grad
        rows += [sums(grad), sums(grad * normal)]
    spread_stats(stats, rows)


def norm_back(d, y, bn, dtotal, gain, count):
    mean, inverse = bn
    scale = gain * inverse
    normal = (y - mean) * inverse
    return scale * (d - dtotal[0:1] / count - normal * (dtotal[1:2] / count))


def input_grads(width, ch, dy, taps, lead, outs, cat, dv):
    spread_taps(dy, width, cat)
    dv[...] = conv_back(cat[...], taps, lead)
    own = ch[0]
    blocks = []
    for k in range(4):
        start = pl.multiple_of((own ^ k) * 128, 128)
        blocks.append(dv[:, pl.ds(start, 128)])
    return blocks


def task_back_body(l, count, width, row0, ch, d, y, raw, draw, gain, taps, dys, send, keep, far, cat, dv):
    total = raw[...]
    dtotal = draw[...]
    for t in range(3):
        bn = centre(total[2 * t : 2 * t + 2], count)
        dts = dtotal[row0 + 2 * t : row0 + 2 * t + 2]
        dy = norm_back(d[t], y[t], bn, dts, gain[l, 2 + t : 3 + t], count)
        dys[t] = dy.astype(LOW)
    ready(taps)

    def one(t, carry):
        blocks = input_grads(width, ch, dys[t].astype(F32), taps, t, None, cat, dv)
        send[0, t] = blocks[1].astype(LOW)
        send[1, t] = blocks[3].astype(LOW)
        keep[t] = blocks[0]
        far[t] = blocks[2]
        return carry

    lax.fori_loop(0, 3, one, 0)


def conv_back_body(l, k, count, width, ch, d, y, raw, rawrow, draw, gain, taps, dys, send, keep, far, cat, dv):
    dtotal = draw[0:2]
    dy = norm_back(d[...], y[...], bn_of(raw, rawrow, count), dtotal, gain[l, k : k + 1], count)
    dys[...] = dy.astype(LOW)
    blocks = input_grads(width, ch, dy, taps, 0, None, cat, dv)
    send[0] = blocks[1].astype(LOW)
    send[1] = blocks[3].astype(LOW)
    keep[...] = blocks[0]
    far[...] = blocks[2]


def weight_body(width, many, im, x, dys, dk, cat, dkf):
    images = dk.shape[0]
    share = 512 // images
    ready(x)
    ready(dys)

    def one(t, carry):
        dy = dys[t] if many else dys[...]
        spread_taps(dy.astype(F32), width, cat)
        dkf[...] = dot_tn(x[t] if many else x[...], cat[...])

        def copy(r, carry):
            rows = pl.ds(pl.multiple_of(r * share, share), share)
            for tap in range(9):
                dk[r, t, tap] = dkf[rows, tap * 128 : tap * 128 + 128].astype(LOW)
            return carry

        return lax.fori_loop(0, images, copy, carry)

    lax.fori_loop(0, dk.shape[1], one, 0)


def split_body(bit, im, x, out):
    low = (im[0] >> bit) & 1
    ready(x)
    for i in range(2):
        start = pl.multiple_of((2 * i + 1 - low) * 128, 128)
        out[i] = x.ref[0, :, pl.ds(start, 128)]


def pair_weight_body(width, bit, rest, im, x, other_x, dy, other_dy, stay, leave, cat, total):
    low = (im[0] >> bit) & 1
    ready(x)
    ready(dy)
    mine = [x.ref[0, :, pl.ds(pl.multiple_of((2 * i + low) * 128, 128), 128)] for i in range(2)]
    spread_taps(dy[0].astype(F32), width, cat)
    total[...] = dot_tn(jnp.concatenate(mine, 1), cat[...])
    spread_taps(other_dy[...].astype(F32), width, cat)
    total[...] += dot_tn(jnp.concatenate([other_x[0], other_x[1]], 1), cat[...])
    half = stay.shape[0]
    share = stay.shape[2]
    for e in range(2 * half):
        mask = 0
        for s, b in enumerate(rest):
            mask |= ((e >> (len(rest) - 1 - s)) & 1) << b
        block = im[0] ^ mask
        row = ((block >> (bit + 1)) & 1) * 128 + (block & ((1 << bit) - 1)) * share
        rows = pl.ds(pl.multiple_of(row, share), share)
        target = stay if e < half else leave
        for tap in range(9):
            target[e % half, tap] = total[rows, tap * 128 : tap * 128 + 128].astype(LOW)


def halve_body(a, b, stay, leave):
    half = stay.shape[0]
    for i in range(half):
        stay[i] = a[i].astype(F32) + b[i].astype(F32)
        leave[i] = (a[half + i].astype(F32) + b[half + i].astype(F32)).astype(LOW)


def gate_grad_body(l, count, width, ch, part, far, s, up, zraw, y, raw, gain, shift, dx, d, d2, stats, scratch):
    mean, inverse = bn_of(raw, 0, count)
    normal = (y[...] - mean) * inverse
    v = normal * gain[l, 1:2] + shift[l, 1:2]
    sg = sigmoid(v)
    act = v * sg
    own = pl.ds(pl.multiple_of(ch[0] * 128, 128), 128)
    ztotal = zraw[:, own]
    upstream = unpool(dx[...], scratch, width)
    rows = []
    for t in range(3):
        zmean, zinverse = centre(ztotal[2 * t : 2 * t + 2], count)
        znormal = (dot(s[t], up[l, t]) - zmean) * zinverse
        m = sigmoid(znormal * gain[l, 5 + t : 6 + t] + shift[l, 5 + t : 6 + t])
        dr = part[t] + far[t].astype(F32)
        through = dr * m
        upstream = upstream + through
        grad = through * act * (1.0 - m)
        d[t] = grad
        rows += [sums(grad), sums(grad * znormal)]
    grad = upstream * silu_slope(v, sg)
    d2[...] = grad
    spread_stats(stats, [sums(grad), sums(grad * normal)] + rows)


def hidden_grad_body(l, count, ch, d, s, up, zraw, draw, gain, ds, dup):
    own = pl.ds(pl.multiple_of(ch[0] * 128, 128), 128)
    ztotal = zraw[:, own]
    dtotal = draw[2:8]
    for t in range(3):
        z = dot(s[t], up[l, t])
        rows = slice(2 * t, 2 * t + 2)
        bn = centre(ztotal[rows], count)
        dz = norm_back(d[t], z, bn, dtotal[rows], gain[l, 5 + t : 6 + t], count).astype(LOW)
        dup[t] = dot_tn(s[t], dz).astype(LOW)
        ds[t] = dot_nt(dz, up[l, t]).astype(LOW)


def bottle_grad_body(l, count, ds0, ds1, p, raw, bgain, bshift, d, stats):
    rows = []
    for t in range(3):
        mean, inverse = bn_of(raw, 2 + 2 * t, count)
        normal = (p[t] - mean) * inverse
        v = normal * bgain[l, t : t + 1] + bshift[l, t : t + 1]
        grad = (ds0[t].astype(F32) + ds1[t].astype(F32)) * silu_slope(v, sigmoid(v))
        d[t] = grad
        rows += [sums(grad), sums(grad * normal)]
    spread_stats(stats, rows)


def attend_grad_body(l, count, rawrow, d, p, raw, draw, bgain, g, down, part, far, y, raw1, gain, shift, more, ddown, d1, stats, more_out):
    upstream = part[...] + far[...].astype(F32)
    dtotal = draw[...]
    rows = []
    for t in range(3):
        bn = bn_of(raw, 2 + 2 * t, count)
        dp = norm_back(d[t], p[t], bn, dtotal[2 * t : 2 * t + 2], bgain[l, t : t + 1], count).astype(LOW)
        ddown[t] = dot_tn(g[...] if more is None else g[t], dp).astype(LOW)
        grad = dot_nt(dp, down[l, t])
        upstream = upstream + grad
        if more is not None:
            yt, traw, tcount, twidth, scratch = more
            mean, inverse = bn_of(traw, 2 * t, tcount)
            normal = (yt[t] - mean) * inverse
            v = normal * gain[l - 1, 2 + t : 3 + t] + shift[l - 1, 2 + t : 3 + t]
            grad = unpool(grad, scratch, twidth) * silu_slope(v, sigmoid(v))
            more_out[t] = grad
            rows += [sums(grad), sums(grad * normal)]
    mean, inverse = bn_of(raw1, rawrow, count)
    normal = (y[...] - mean) * inverse
    v = normal * gain[l, 0:1] + shift[l, 0:1]
    grad = upstream * silu_slope(v, sigmoid(v))
    d1[...] = grad
    spread_stats(stats, [sums(grad), sums(grad * normal)] + rows)


def attend_grad_last_body(l, count, rawrow, d, p, raw, draw, bgain, g, down, part, far, y, raw1, gain, shift, ddown, d1, stats):
    attend_grad_body(l, count, rawrow, d, p, raw, draw, bgain, g, down, part, far, y, raw1, gain, shift, None, ddown, d1, stats, None)


def attend_grad_first_body(l, count, rawrow, tcount, twidth, d, p, raw, draw, bgain, g, down, part, far, y, raw1, gain, shift, yt, traw, ddown, d1, stats, dt, scratch):
    more = (yt, traw, tcount, twidth, scratch)
    attend_grad_body(l, count, rawrow, d, p, raw, draw, bgain, g, down, part, far, y, raw1, gain, shift, more, ddown, d1, stats, dt)


def finish_body(order, refs_in, gain, shift, bgain, bshift):
    for l in range(gain.shape[0]):
        for row, (place, start) in enumerate(order[l]):
            total = refs_in[place][start : start + 2]
            if row < 8:
                shift[l, row : row + 1] = total[0:1]
                gain[l, row : row + 1] = total[1:2]
            else:
                bshift[l, row - 8 : row - 7] = total[0:1]
                bgain[l, row - 8 : row - 7] = total[1:2]


def shape_of(shape, dtype=F32):
    return jax.ShapeDtypeStruct(tuple(shape), dtype)


class Long:
    def __init__(self, near, home=None):
        self.near, self.home = near, home
        some = home if near is None else near
        self.shape, self.dtype = some.shape, some.dtype


class Taps:
    def __init__(self, home, first, count):
        self.home, self.first, self.shape = home, first, (count,) + home.shape[1:]
        self.dtype = home.dtype


class Rows:
    def __init__(self, whole, first, last):
        self.whole, self.first, self.last = whole, first, last


class Coming:
    def __init__(self, ref, copy):
        self.ref, self.copy, self.shape, self.dtype = ref, copy, ref.shape, ref.dtype

    def ready(self):
        if self.copy is not None:
            self.copy.wait()
            self.copy = None

    def __getitem__(self, place):
        self.ready()
        return self.ref[place]


class Going:
    def __init__(self, ref, copy):
        self.ref, self.copy, self.shape, self.dtype = ref, copy, ref.shape, ref.dtype
        self.started = False

    def flush(self):
        if not self.started:
            self.copy.start()
            self.started = True

    def __getitem__(self, place):
        return self.ref[place]

    def __setitem__(self, place, value):
        self.ref[place] = value


class SomeRows:
    def __init__(self, ref, first):
        self.ref, self.first = ref, first

    def __getitem__(self, place):
        layer, rows = place
        return self.ref[layer, self.first + rows.start : self.first + rows.stop]


def ready(ref):
    if isinstance(ref, Coming):
        ref.ready()


def flush(ref):
    if isinstance(ref, Going):
        ref.flush()


TURN = []


def run(body, args, outs, scratch=(), name=None, keep=(), away=(), save=(), after=()):
    values, picks = [], []
    for v in list(args) + list(save):
        whole = v.whole if isinstance(v, Rows) else v
        place = next((i for i, other in enumerate(values) if other is whole), None)
        if place is None:
            place = len(values)
            values.append(whole)
        picks.append((place, v))
    picks = picks[: len(args)]
    count = len(values)
    far = [
        isinstance(v, Taps) or (isinstance(v, Long) and v.near is None) for v in values
    ]
    saved = [i for i, v in enumerate(values) if isinstance(v, Long) and v.home is None]
    hbm, vmem = pl.BlockSpec(memory_space=pltpu.HBM), pl.BlockSpec(memory_space=pltpu.VMEM)
    operands, specs = [], []
    for v, apart in zip(values, far):
        if apart:
            operands.append(pltpu.with_memory_space_constraint(v.home, pltpu.HBM))
            specs.append(hbm)
        else:
            operands.append(v.near if isinstance(v, Long) else v)
            specs.append(spec_of(operands[-1]))
    after = list(after) + TURN
    TURN.clear()
    outs = list(outs) + [shape_of((8, 128))]
    stage = [pltpu.VMEM(v.shape, v.dtype) for v, apart in zip(values, far) if apart]
    leave = [pltpu.VMEM(outs[i].shape, outs[i].dtype) for i in away]
    moves = len(stage) + len(leave) + len(saved)

    def kernel(*refs):
        ins = list(refs[:count])
        results = list(refs[count + len(after) : count + len(after) + len(outs)])
        homes = refs[count + len(after) + len(outs) :][: len(saved)]
        rest = refs[count + len(after) + len(outs) + len(saved) :]
        own, rest = rest[: len(scratch)], rest[len(scratch) :]
        sems = rest[-1] if moves else None
        wait = []
        slot = 0
        for i in range(count):
            if not far[i]:
                continue
            source = ins[i]
            if isinstance(values[i], Taps):
                source = source.at[values[i].first : values[i].first + values[i].shape[0]]
            copy = pltpu.make_async_copy(source, rest[slot], sems.at[slot])
            copy.start()
            ins[i] = Coming(rest[slot], copy)
            wait.append(ins[i])
            slot += 1
        end = []
        for i, home in zip(saved, homes):
            copy = pltpu.make_async_copy(ins[i], home, sems.at[slot])
            copy.start()
            end.append(copy)
            slot += 1
        for n, i in enumerate(away):
            ref = rest[len(stage) + n]
            copy = pltpu.make_async_copy(ref, results[i], sems.at[slot])
            results[i] = Going(ref, copy)
            end.append(results[i])
            slot += 1
        turn = results.pop()
        turn[...] = jnp.zeros_like(turn)
        views = [SomeRows(ins[i], v.first) if isinstance(v, Rows) else ins[i] for i, v in picks]
        body(*views, *results, *own)
        for item in wait:
            item.ready()
        for item in end:
            if isinstance(item, Going):
                item.flush()
        for item in end:
            (item.copy if isinstance(item, Going) else item).wait()

    out_shape = []
    for i, v in enumerate(outs):
        kind = pltpu.HBM if i in away else pltpu.VMEM
        out_shape.append(kind(v.shape, v.dtype))
    out_shape += [pltpu.HBM(values[i].shape, values[i].dtype) for i in saved]
    results = pl.pallas_call(
        kernel,
        out_shape=out_shape,
        in_specs=specs + [vmem] * len(after),
        out_specs=[hbm if i in away else vmem for i in range(len(outs))] + [hbm] * len(saved),
        scratch_shapes=list(scratch)
        + stage
        + leave
        + ([pltpu.SemaphoreType.DMA((moves,))] if moves else []),
        compiler_params=pltpu.CompilerParams(vmem_limit_bytes=VMEM_LIMIT),
        cost_estimate=pl.CostEstimate(flops=0, bytes_accessed=1, transcendentals=0),
        name=name,
    )(*operands, *after)
    answer = list(results[: len(outs)])
    TURN.append(answer.pop())
    for i, home in zip(saved, results[len(outs) :]):
        values[i].home, values[i].near = home, None
    for i in keep:
        answer[i] = Long(answer[i])
    for i in away:
        answer[i] = Long(None, answer[i])
    return answer


def spec_of(value):
    return pl.BlockSpec(memory_space=pltpu.SMEM if value.dtype == jnp.int32 else pltpu.VMEM)


CORE = ((0, 1), (1, 0), (2, 3), (3, 2))
CHIP = ((0, 2), (2, 0), (1, 3), (3, 1))


def near_and_far(value):
    far = lax.ppermute(value, "ch", CHIP)
    return [value, lax.ppermute(value, "ch", CORE), far]


def add_last(blocks, after=None):
    far = blocks[2] if after is None else hold(blocks[2], after)
    blocks.append(lax.ppermute(far, "ch", CORE))


def gather_ch(value):
    blocks = near_and_far(value)
    add_last(blocks)
    return blocks


def hold(value, after):
    return lax.optimization_barrier((value, after))[0]


def swap_img(copies):
    return lax.all_to_all(copies, "img", 0, 0)


class Layer:
    pass


def on_device(
    feats,
    shared_w,
    task_w,
    down_w,
    up_w,
    norm_gain,
    norm_shift,
    bottle_gain,
    bottle_shift,
    seg_mask,
    depth_mask,
    shared_cot,
    task_cot,
):
    images = lax.axis_size("img")
    tasks = task_w.shape[1]
    layers = shared_w.shape[0]
    share = 512 // images
    own = lax.axis_index("ch").astype(jnp.int32).reshape(1)
    img = lax.axis_index("img").astype(jnp.int32).reshape(1)
    shared_taps = shared_w.reshape(2 * layers, 9, 512, 128)
    task_taps = task_w.reshape(tasks * layers, 9, 512, 128)
    widths = [feats.shape[2], feats.shape[2] // 2]
    sizes = [w * w for w in widths]
    counts = [float(images * n) for n in sizes]
    n0, n1 = sizes

    def stats_of(rows, lanes=128):
        return shape_of((rows, lanes))

    one, two = Layer(), Layer()
    kept = [one, two]

    TURN.clear()
    pending, held = [], []

    def total_of(rows, name, first=(), second=(), mid=()):
        if pending:
            rows = hold(rows, list(pending))
            pending.clear()
        low = min(1, bits - 1)
        groups = [range(low, bits), range(low)] if bits <= 3 else [[b] for b in range(bits)]
        for place, group in enumerate(groups):
            shifts = [0]
            for bit in group:
                shifts += [s | 1 << bit for s in shifts]
            parts = [rows] + [
                lax.ppermute(rows, "img", [(i, i ^ s) for i in range(images)]) for s in shifts[1:]
            ]
            last = place == len(groups) - 1
            if place == 0:
                for step in first:
                    step()
            if last:
                for step in second:
                    step()
            rows = run(
                sum_body,
                parts,
                [shape_of(rows.shape)],
                name=f"{name}_{place}",
                keep=(0,) if last else (),
            )[0]
            for blocks in mid if place == 0 else ():
                add_last(blocks, rows.near if last else rows)
        for make in held:
            make(rows.near)
        held.clear()
        return rows

    def gap(steps):
        for step in steps:
            step()
        for make in held:
            make(None)
        held.clear()

    def send_img(value, bit):
        got = lax.ppermute(value, "img", [(i, i ^ (1 << bit)) for i in range(images)])
        pending.append(got)
        return got

    bits = images.bit_length() - 1
    pair_bit = 7 - (share.bit_length() - 1)
    rest = [b for b in range(bits) if b != pair_bit]

    class Weights:
        def __init__(self, l, name):
            self.l, self.name, self.step, self.done = l, name, 0, None

        def take(self, x, place):
            self.x = Taps(x.home.reshape((-1,) + x.shape[-2:]), place, 1)

        def split(self):
            out = run(
                functools.partial(split_body, pair_bit),
                (img, self.x),
                [shape_of((2, sizes[self.l], 128), LOW)],
                name=f"split{self.name}",
            )[0]
            self.later(out, pair_bit, "other_x")

        def later(self, value, bit, name):
            def make(total):
                setattr(self, name, send_img(value if total is None else hold(value, total), bit))

            held.append(make)

        def meet(self, dys, place, other):
            self.dy = Taps(dys.home.reshape((-1,) + dys.shape[-2:]), place, 1)
            self.other_dy = other

        def weigh(self):
            n, half = sizes[self.l], images // 4
            stay, leave = run(
                functools.partial(pair_weight_body, widths[self.l], pair_bit, rest),
                (img, self.x, self.other_x, self.dy, self.other_dy),
                [shape_of((half, 9, share, 128), LOW)] * 2,
                scratch=[pltpu.VMEM((n, 1152), LOW), pltpu.VMEM((256, 1152), F32)],
                name=f"weigh{self.name}",
                away=(0,),
            )
            self.stay, self.step = stay, 1
            self.later(leave, rest[0], "got")

        def halve(self):
            half = self.stay.shape[0] // 2
            stay, leave = run(
                halve_body,
                (self.stay, self.got),
                [shape_of((half, 9, share, 128)), shape_of((half, 9, share, 128), LOW)],
                name=f"halve{self.name}_{self.step}",
                away=(0,),
            )
            self.stay = stay
            self.later(leave, rest[self.step], "got")
            self.step += 1

    class Shared(Weights):
        def __init__(self, name):
            self.name, self.step, self.got = name, 0, None

        def add(self):
            if self.step > 0:
                self.value = run(
                    add_body,
                    (self.value, self.got),
                    [shape_of(self.value.shape, LOW)],
                    name=f"{self.name}_{self.step}",
                    )[0]
            else:
                self.value = self.value.home
            self.later(self.value, self.step, "got")
            self.step += 1

    jobs = {
        name: Weights(int(name[-1]), name)
        for name in ["t0_0", "t1_0", "t2_0", "t0_1", "t1_1", "t2_1", "a_0", "b_0", "a_1", "b_1"]
    }
    for name in ["up_0", "up_1", "down_0", "down_1"]:
        jobs[name] = Shared(name)

    def tasks_of(l):
        return [jobs[f"t{t}_{l}"] for t in range(tasks)]

    def meet(names, dys):
        got = send_img(dys.home, pair_bit)
        if len(names) == 1:
            jobs[names[0]].meet(dys, 0, got)
        else:
            for t, name in enumerate(names):
                jobs[name].meet(dys, t, got[t])

    blocks = near_and_far(feats.reshape(n0, 128))
    add_last(blocks)
    down_w, up_w = Long(None, down_w), Long(None, up_w)
    wide, narrow, params = run(
        pack_body,
        (down_w, up_w, Long(None, norm_gain), Long(None, norm_shift)),
        [
            shape_of((layers, 2, tasks, 128, 128), LOW),
            shape_of((layers, 6, 128)),
            shape_of((layers, 16, 128)),
        ],
        name="pack",
        away=(2,),
    )
    gains = Rows(params, 0, 8)
    norms = (gains, Rows(params, 8, 16))
    bottles = (Long(None, bottle_gain), Long(None, bottle_shift))
    one.x, one.y1, stats = run(
        functools.partial(first_conv_body, widths[0], 0),
        (own, *blocks, Taps(shared_taps, 0, 1)),
        [shape_of((n0, 512), LOW), shape_of((n0, 128)), stats_of(2)],
        name="conv1_0",
        keep=(1,),
        away=(0,),
    )
    wides, narrows = near_and_far(hold(wide, stats)), near_and_far(hold(narrow, stats))
    scales = jnp.stack([seg_mask, depth_mask, jnp.ones_like(seg_mask)]).astype(F32)
    dq = (task_cot.astype(F32) * scales[..., None]).reshape(tasks, n1 // 4, 128)
    dq, dx = Long(dq), Long(shared_cot.astype(F32).reshape(n1 // 4, 128))
    jobs["a_0"].take(one.x, 0)
    one.raw1 = total_of(stats, "total1_0", [jobs["a_0"].split], mid=(wides, narrows))
    one.row1 = 0
    low, one.g = run(
        functools.partial(first_act_body, counts[0]),
        (one.y1, one.raw1, *norms),
        [shape_of((n0, 128), LOW)] * 2,
        name="act1_0",
        away=(1,),
    )
    blocks = gather_ch(low)
    down_all, up_all, gates = run(
        unpack_body,
        (own, *wides, *narrows),
        [
            shape_of((layers, tasks, 512, 128), LOW),
            shape_of((layers, tasks, 128, 512), LOW),
            shape_of((layers, 6, 512)),
        ],
        name="unpack",
        keep=(0,),
        away=(1, 2),
        save=(dq, dx),
    )
    one.x2, one.y2, one.p, stats = run(
        functools.partial(second_conv_body, widths[0], 0),
        (own, *blocks, Taps(shared_taps, 1, 1), down_all),
        [shape_of((n0, 512), LOW), shape_of((n0, 128)), shape_of((tasks, n0, 128)), stats_of(8)],
        name="conv2_0",
        keep=(1, 2),
        away=(0,),
    )
    one.raw2 = total_of(stats, "total2_0")

    def hidden(l):
        k, n = kept[l], sizes[l]
        body = functools.partial(hidden_body, l, counts[l], widths[l])
        outs = [shape_of((tasks, n, 128), LOW)]
        if l == 0:

            def inner(y, p, raw, gain, shift, bgain, bshift, up, s, u, zstats, scratch):
                body(y, p, raw, gain, shift, bgain, bshift, up, s, u, None, zstats, scratch)

            outs += [shape_of((n + n // 4, 128), LOW), stats_of(6, 512)]
        else:
            inner = body
            outs += [shape_of((n, 128), LOW), shape_of((n // 4, 128), LOW), stats_of(6, 512)]
        return run(
            inner,
            (k.y2, k.p, k.raw2, *norms, *bottles, up_all),
            outs,
            scratch=[pltpu.VMEM((n, 128), F32)],
            name=f"hidden_{l}",
            keep=(0,),
        )

    def task_convs(l, u_blocks, taps, more=None):
        k, n = kept[l], sizes[l]
        body = functools.partial(task_conv_body, l, counts[l], widths[l])
        args = (own, k.s, up_all, *u_blocks, k.zraw, gates, taps)
        if more is None:

            def inner(ch, s, up, u0, u1, u2, u3, zraw, gt, taps, kk, y, stats, full, acc):
                body(ch, s, up, u0, u1, u2, u3, zraw, gt, taps, None, kk, y, stats, full, acc)

        else:
            inner = body
            args += (more,)
        return run(
            inner,
            args,
            [
                shape_of((tasks, n, 512), LOW),
                shape_of((tasks, n, 128)),
                stats_of(6 if more is None else 8),
            ],
            scratch=[pltpu.VMEM((n, 512), LOW), pltpu.VMEM((tasks, 2, 128), F32)],
            name=f"taskconv_{l}",
            keep=(1,),
            away=(0,),
        )

    one.s, u, zstats = hidden(0)
    u_blocks = near_and_far(u)

    def next_conv():
        two.x, two.y1, two.more = run(
            functools.partial(next_conv_body, widths[1], 0, n0),
            (own, *u_blocks, Taps(shared_taps, 2, 1)),
            [shape_of((n1, 512), LOW), shape_of((n1, 128)), shape_of((2, 128))],
            name="conv1_1",
            away=(0, 1),
        )

    jobs["b_0"].take(one.x2, 0)
    one.zraw = total_of(zstats, "totalz_0", [jobs["b_0"].split], [next_conv], mid=(u_blocks,))
    one.k, one.yt, stats = task_convs(0, u_blocks, Taps(task_taps, 0, tasks), two.more)
    for t, job in enumerate(tasks_of(0)):
        job.take(one.k, t)
    one.traw = total_of(stats, "totalt_0", *[[job.split] for job in tasks_of(0)[:2]])
    two.raw1, two.row1 = one.traw, 6

    low, two.g, part = run(
        functools.partial(attend_body, counts[0], counts[1], widths[0]),
        (one.yt, two.y1, one.traw, *norms, down_w),
        [
            shape_of((n1, 128), LOW),
            shape_of((tasks, n1, 128), LOW),
            shape_of((tasks, n1, 128), LOW),
        ],
        scratch=[pltpu.VMEM((n0, 128), F32)],
        name="attend_1",
        away=(1,),
    )

    def sum_ch(value, name):
        got = lax.ppermute(value, "ch", CORE)
        near = run(pair_body, (value, got), [shape_of(value.shape, LOW)], name=name)[0]
        return near, lax.ppermute(near, "ch", CHIP)

    blocks = gather_ch(low)
    halves = sum_ch(part, "pairp_1")
    two.x2, two.y2, two.p, stats = run(
        functools.partial(second_conv_next_body, widths[1], 0),
        (own, *blocks, Taps(shared_taps, 3, 1), *halves),
        [shape_of((n1, 512), LOW), shape_of((n1, 128)), shape_of((tasks, n1, 128)), stats_of(8)],
        name="conv2_1",
        keep=(1, 2),
        away=(0,),
    )
    two.raw2 = total_of(stats, "total2_1")
    jobs["a_1"].take(two.x, 0)
    jobs["b_1"].take(two.x2, 0)
    two.s, u, shared_out, zstats = hidden(1)
    u_blocks = near_and_far(u)
    two.zraw = total_of(zstats, "totalz_1", mid=(u_blocks,))
    two.k, two.yt, stats = task_convs(1, u_blocks, Taps(task_taps, tasks, tasks))
    for t, job in enumerate(tasks_of(1)):
        job.take(two.k, t)
    two.traw = total_of(stats, "totalt_1")

    task_out, d, stats = run(
        functools.partial(task_last_body, 1, counts[1], widths[1]),
        (two.yt, two.traw, *norms, dq),
        [shape_of((tasks, n1 // 4, 128), LOW), shape_of((tasks, n1, 128)), stats_of(6)],
        scratch=[pltpu.VMEM((n1, 128), F32)],
        name="tasklast_1",
    )
    splits = [job.split for job in tasks_of(1)]
    two.dtraw = total_of(stats, "dtotalt_1", splits[:2], splits[2:])
    two.dtrow = 0

    def back_outs(n, lead=()):
        return [
            shape_of(lead + (n, 128), LOW),
            shape_of((2,) + lead + (n, 128), LOW),
            shape_of(lead + (n, 128)),
            shape_of(lead + (n, 128)),
        ]

    def back_scratch(n):
        return [pltpu.VMEM((n, 1152), LOW), pltpu.VMEM((n, 512), F32)]

    def scatter_ch(send, keep, far, name, away=()):
        near, part = run(
            pair_second_body,
            (keep, far, lax.ppermute(send, "ch", CORE)),
            [shape_of(far.shape, LOW), shape_of(far.shape)],
            name=name,
            away=away,
        )
        return (part, lax.ppermute(near, "ch", CHIP))

    def steps(weigh="", halve="", add="", split=""):
        return (
            [jobs[name].weigh for name in weigh.split()]
            + [jobs[name].halve for name in halve.split()]
            + [jobs[name].add for name in add.split()]
            + [jobs[name].split for name in split.split()]
        )

    plan = {
        "gate_1": (steps("t0_1", "", "", "t2_0"), steps("t1_1", "", "", "b_1")),
        "bottle_1": (steps("t2_1", "", "", "a_1"), steps()),
        "first_1": (steps("b_1", "t0_1"), steps("", "t1_1")),
        "gate_0": (steps("t0_0"), steps("", "t2_1")),
        "hidden_0": steps("a_1 t1_0", "b_1", "up_1 down_1"),
        "bottle_0": (steps("t2_0"), steps("", "t0_0", "up_1 down_1")),
        "first_0": (steps("b_0"), steps("", "t1_0 a_1", "up_0")),
    }
    unfinished = None

    for l in range(layers - 1, -1, -1):
        k, n, w, count = kept[l], sizes[l], widths[l], counts[l]
        dys, send, keep, far = run(
            functools.partial(task_back_body, l, count, w, k.dtrow),
            (own, d, k.yt, k.traw, k.dtraw, gains, Taps(task_taps, tasks * l, tasks)),
            back_outs(n, (tasks,)),
            scratch=back_scratch(n),
            name=f"taskback_{l}",
            away=(0,),
        )
        meet([f"t{t}_{l}" for t in range(tasks)], dys)
        if unfinished is not None:
            parts_before = unfinished()
        parts = scatter_ch(send, keep, far, f"pairr_{l}")
        gap(plan.get(f"task_{l}", ()))
        if unfinished is not None:
            dx = run(mixed_body, parts_before, [shape_of((sizes[l + 1], 128))], name=f"dx_{l + 1}")[0]
        d, d2, stats = run(
            functools.partial(gate_grad_body, l, count, w),
            (own, *parts, k.s, up_w, k.zraw, k.y2, k.raw2, *norms, dx),
            [shape_of((tasks, n, 128)), shape_of((n, 128)), stats_of(8)],
            scratch=[pltpu.VMEM((n, 128), F32)],
            name=f"gategrad_{l}",
        )
        k.draw2 = total_of(stats, f"dtotal2_{l}", *plan[f"gate_{l}"])
        d2 = Long(d2)
        ds, dup = run(
            functools.partial(hidden_grad_body, l, count),
            (own, d, k.s, up_w, k.zraw, k.draw2, gains),
            [shape_of((tasks, n, 128), LOW), shape_of((tasks, 128, 128), LOW)],
            name=f"hiddengrad_{l}",
            away=(1,),
            save=(d2,),
        )
        jobs[f"up_{l}"].value = dup
        got = lax.ppermute(ds, "ch", CORE)
        near = run(pair_body, (ds, got), [shape_of(ds.shape, LOW)], name=f"pairs_{l}")[0]
        halves = near, lax.ppermute(near, "ch", CHIP)

        def conv2_back(ch, d, y, raw, draw, gain, taps, *rest, l=l, count=count, w=w):
            conv_back_body(l, 1, count, w, ch, d, y, raw, 0, draw, gain, taps, *rest)

        dys, send, keep, far = run(
            conv2_back,
            (own, d2, k.y2, k.raw2, k.draw2, gains, Taps(shared_taps, 2 * l + 1, 1)),
            back_outs(n),
            scratch=back_scratch(n),
            name=f"conv2back_{l}",
            away=(0,),
        )
        meet([f"b_{l}"], dys)
        parts = scatter_ch(send, keep, far, f"pairv_{l}", (1,))
        gap(plan.get(f"hidden_{l}", ()))
        d, stats = run(
            functools.partial(bottle_grad_body, l, count),
            (*halves, k.p, k.raw2, *bottles),
            [shape_of((tasks, n, 128)), stats_of(6)],
            name=f"bottlegrad_{l}",
        )
        k.draw3 = total_of(stats, f"dtotal3_{l}", *plan[f"bottle_{l}"])
        args = (d, k.p, k.raw2, k.draw3, bottles[0], k.g, down_w, *parts, k.y1, k.raw1, *norms)
        outs = [shape_of((tasks, 128, 128), LOW), shape_of((n, 128))]
        if l > 0:
            ddown, d1, stats, d = run(
                functools.partial(
                    attend_grad_first_body, l, count, k.row1, counts[l - 1], widths[l - 1]
                ),
                args + (kept[l - 1].yt, kept[l - 1].traw),
                outs + [stats_of(8), shape_of((tasks, sizes[l - 1], 128))],
                scratch=[pltpu.VMEM((sizes[l - 1], 128), F32)],
                name=f"attendgrad_{l}",
                away=(0,),
            )
        else:
            ddown, d1, stats = run(
                functools.partial(attend_grad_last_body, l, count, k.row1),
                args,
                outs + [stats_of(2)],
                name=f"attendgrad_{l}",
                away=(0,),
            )
        jobs[f"down_{l}"].value = ddown
        k.draw1 = total_of(stats, f"dtotal1_{l}", *plan[f"first_{l}"])
        if l > 0:
            kept[l - 1].dtraw, kept[l - 1].dtrow = k.draw1, 2
            d1 = Long(d1)

        def conv1_back(ch, d, y, raw, draw, gain, taps, *rest, l=l, count=count, w=w, row=k.row1):
            conv_back_body(l, 0, count, w, ch, d, y, raw, row, draw, gain, taps, *rest)

        dys, send, keep, far = run(
            conv1_back,
            (own, d1, k.y1, k.raw1, k.draw1, gains, Taps(shared_taps, 2 * l, 1)),
            back_outs(n),
            scratch=back_scratch(n),
            name=f"conv1back_{l}",
            away=(0,),
        )
        meet([f"a_{l}"], dys)

        def unfinished(l=l, send=send, keep=keep, far=far):
            return scatter_ch(send, keep, far, f"pairx_{l}")

    parts = unfinished()
    rows_of = [k.draw1, k.draw2, k.dtraw, k.draw3]
    gap(steps("", "t2_0", "down_0 up_0"))
    dx = run(mixed_body, parts, [shape_of((n0, 128))], name="dx_0", away=(0,))[0].home
    gap(steps("a_0", "b_0"))
    order, places = [], []
    for k in kept:
        base = len(places)
        places += [k.draw1, k.draw2, k.dtraw, k.draw3]
        rows = [(base, 0), (base + 1, 0)]
        rows += [(base + 2, k.dtrow + 2 * t) for t in range(3)]
        rows += [(base + 1, 2 + 2 * t) for t in range(3)]
        rows += [(base + 3, 2 * t) for t in range(3)]
        order.append(rows)

    def norms_body(*refs):
        finish_body(order, refs[: len(places)], *refs[len(places) :])

    gains = run(
        norms_body,
        places,
        [shape_of((layers, 8, 128))] * 2 + [shape_of((layers, tasks, 128))] * 2,
        name="norms",
    )
    gap(steps("", "", "down_0 up_0"))
    gap(steps("", "a_0", "down_0"))
    while any(job.step < (bits if isinstance(job, Shared) else len(rest)) for job in jobs.values()):
        for job in jobs.values():
            if job.step < (bits if isinstance(job, Shared) else len(rest)):
                gap([job.add if isinstance(job, Shared) else job.halve])

    names = ["b_0", "a_1", "b_1"]
    names += [f"t{t}_{l}" for l in range(layers) for t in range(tasks)]
    sums = ["up_0", "up_1", "down_0", "down_1"]
    pieces = []
    for name in names:
        pieces += [jobs[name].stay, jobs[name].got]
    for name in sums:
        pieces += [jobs[name].value, jobs[name].got]

    def finish(*refs):
        sw, tw, down, up = refs[len(pieces) :]
        for i in range(len(names)):
            value = refs[2 * i][0].astype(F32) + refs[2 * i + 1][0].astype(F32)
            if i < 3:
                sw[i + 1] = value
            else:
                tw[i - 3] = value
        flush(tw)
        flush(sw)
        for i in range(len(sums)):
            first, second = refs[2 * (len(names) + i)], refs[2 * (len(names) + i) + 1]
            value = first[...].astype(F32) + second[...].astype(F32)
            (up if i < layers else down)[i % layers] = value

    sw, tw, down, up = run(
        finish,
        pieces,
        [
            shape_of((2 * layers, 9, share, 128)),
            shape_of((tasks * layers, 9, share, 128)),
            shape_of((layers, tasks, 128, 128)),
            shape_of((layers, tasks, 128, 128)),
        ],
        name="finish",
        away=range(4),
    )
    tw, down, up = tw.home, down.home, up.home

    def put_body(buffer, stay, got, turn, out, total, sem):
        total[...] = stay[0].astype(F32) + got[0].astype(F32)
        copy = pltpu.make_async_copy(total, out.at[0], sem)
        copy.start()
        copy.wait()

    job = jobs["a_0"]
    hbm, vmem = pl.BlockSpec(memory_space=pltpu.HBM), pl.BlockSpec(memory_space=pltpu.VMEM)
    sw = pl.pallas_call(
        put_body,
        out_shape=pltpu.HBM(sw.shape, F32),
        in_specs=[hbm, vmem, vmem, vmem],
        out_specs=hbm,
        input_output_aliases={0: 0},
        scratch_shapes=[pltpu.VMEM((9, share, 128), F32), pltpu.SemaphoreType.DMA],
        compiler_params=pltpu.CompilerParams(vmem_limit_bytes=VMEM_LIMIT),
        name="put",
    )(pltpu.with_memory_space_constraint(sw.home, pltpu.HBM), job.stay.home, job.got, TURN.pop())
    return (
        shared_out.reshape(1, widths[1] // 2, widths[1] // 2, 128),
        task_out.reshape(tasks, 1, widths[1] // 2, widths[1] // 2, 128),
        dx.reshape(1, widths[0], widths[0], 128),
        sw.reshape(layers, 2, 3, 3, share, 128),
        tw.reshape(layers, tasks, 3, 3, share, 128),
        down,
        up,
        *gains,
    )


def solution(mesh):
    placed = (
        P("img", None, None, "ch"),
        P(None, None, None, None, None, "ch"),
        P(None, None, None, None, None, "ch"),
        P(None, None, "ch", None),
        P(None, None, None, "ch"),
        P(None, None, "ch"),
        P(None, None, "ch"),
        P(),
        P(),
        P("img", None, None),
        P("img", None, None),
        P("img", None, None, "ch"),
        P(None, "img", None, None, "ch"),
    )
    return jax.shard_map(
        on_device,
        mesh=mesh,
        in_specs=placed,
        out_specs=(
            P("img", None, None, "ch"),
            P(None, "img", None, None, "ch"),
            P("img", None, None, "ch"),
            P(None, None, None, None, "img", "ch"),
            P(None, None, None, None, "img", "ch"),
            P(None, None, "ch", None),
            P(None, None, None, "ch"),
            P(None, None, "ch"),
            P(None, None, "ch"),
            P(),
            P(),
        ),
        check_vma=False,
    )
```

time: 1440 us -> 433 us (0.30)
  waiting for transfers between devices: 699 us -> 128 us
  blocking collectives: 319 us -> 0 us
  local copies, waits for them, and re-layouts: 195 us -> 5.88 us
  starting transfers between devices: 1.62 us -> 154 us
  Pallas kernels: 0 us -> 135 us
  matrix products: 134 us -> 0 us
  other arithmetic: 57 us -> 0.15 us
  between operations: 18 us -> 2.29 us
    reduce_scatter x6 -> x0, waiting for transfers between devices: 549 us -> none  [weight_grad(): lax.psum_scatter(kernel_terms, 'img', scatter_dimension=3, tiled=True)]
    psum x14 -> x0, blocking collectives: 280 us -> none  [the longest x7 140 us: norm_forward(): value_sum, square_sum = lax.psum((partial_sums[0], partial_sums[1]), 'img')]
    unnamed x446 -> x36, local copies, waits for them, and re-layouts: 164 us -> 4.51 us
    ppermute x0 -> x143, starting transfers between devices: none -> 154 us  [the longest x56 83.4 us: total_of(): lax.ppermute(rows, 'img', [(i, i ^ s) for i in range(images)])]
    pallas_call x0 -> x107, Pallas kernels: none -> 135 us  [the longest x106 134 us: run(): pl.pallas_call(kernel, out_shape=out_shape, in_specs=specs + [vmem] * len...]
    ppermute x0 -> x143, waiting for transfers between devices: none -> 128 us  [the longest x48 51.4 us: send_img(): got = lax.ppermute(value, 'img', [(i, i ^ 1 << bit) for i in range(images)])]
    psum x5 -> x0, waiting for transfers between devices: 86 us -> none  [the longest x2 49.3 us: layer_backward(): lax.psum(jnp.einsum('tnhwc,tbc->tnhwb', grad_expand, up_k, preferred_elem...]
    transpose x4 -> x0, matrix products: 75.7 us -> none  [group_conv(): return jax.vmap(conv_plain)(inputs, kernel)]
  transfers between devices with their start and end apart: 18 -> 143, of which waited for: 15 -> 61; matrix products, arithmetic and copies ran while one was open for 13% -> 1% of each run, Pallas kernels for 0% -> 24%
where the time goes in v1:
time: 433 us; the launch traced here: 425 us
  starting transfers between devices  154 us (36%)
  Pallas kernels  135 us (31%)
  waiting for transfers between devices  128 us (30%)
  local copies, waits for them, and re-layouts  5.88 us (1%)
    pallas_call x106, Pallas kernels, run(): pl.pallas_call(kernel, out_shape=out_shape, in_specs=specs + [vmem] * len...  134 us
    ppermute x56, starting transfers between devices, total_of(): lax.ppermute(rows, 'img', [(i, i ^ s) for i in range(images)])  83.4 us
    ppermute x48, waiting for transfers between devices, send_img(): got = lax.ppermute(value, 'img', [(i, i ^ 1 << bit) for i in range(images)])  51.4 us
    ppermute x48, starting transfers between devices, send_img(): got = lax.ppermute(value, 'img', [(i, i ^ 1 << bit) for i in range(images)])  49 us
    ppermute x56, waiting for transfers between devices, total_of(): lax.ppermute(rows, 'img', [(i, i ^ s) for i in range(images)])  40.1 us
    ppermute x6, waiting for transfers between devices, scatter_ch(): return (part, lax.ppermute(near, 'ch', CHIP))  12.5 us
    ppermute x7, starting transfers between devices, near_and_far(): far = lax.ppermute(value, 'ch', CHIP)  10.3 us
    ppermute x7, waiting for transfers between devices, near_and_far(): far = lax.ppermute(value, 'ch', CHIP)  10.2 us
  transfers between devices with their start and end apart: 143, of which 61 were waited for; matrix products, arithmetic and copies ran while one was open for 1% of the time, Pallas kernels for 24%

profile of v1, /device:TPU:0, one launch (start us, length us, event | category | flops | bytes accessed | tf_op | source)
XLA Modules:
  0.0 425.2 jit_solution(3677057507875954331)
XLA Ops:
  3.6 4.1 collective-permute-done.1.refs_3_
  40.0 3.5 collective-permute-start.18
  45.2 3.8 collective-permute-done.19.refs_3_
  67.7 6.0 %taskconv_0.1 = (bf16[3,576,512]{2,1,0:T(8,128)(2,1)}, f32[3,576,128]{2,1,0:T(8,128)S(1)}, f32[8,128]{1,0:T(8,128)S(1)}, f32[8,128]{1,0:T(8,128)S(1)}, bf16[3,576,128]{2,1,0:T(8,128)(2,1)}, /*index=5*/f32[6,512]{1,0:T(8,128)}) custom-call(s32[1]{0:T(128)} %bitcast.refs_0_, bf16[3,576,128]{2,1,0:T(8,128)(2,1)S(1)} %get-tuple-element.415.refs_1_, ...), custom_call_target="tpu_custom_call" | custom-call | bytes 1 | tf_op jit(solution)/shard_map/taskconv_0/pallas_call | solution.py:693
  97.2 3.9 collective-permute-done.34.refs_3_
  116.8 3.6 collective-permute-start.47
  122.1 3.8 collective-permute-done.48.refs_3_
  129.8 3.6 taskconv_1.1
  145.1 3.6 collective-permute-start.56
  157.7 4.4 %taskback_1.1 = (bf16[3,144,128]{2,1,0:T(8,128)(2,1)}, bf16[2,3,144,128]{3,2,1,0:T(8,128)(2,1)S(1)}, f32[3,144,128]{2,1,0:T(8,128)S(1)}, f32[3,144,128]{2,1,0:T(...) custom-call(s32[1]{0:T(128)} %bitcast.refs_0_, f32[3,144,128]{2,1,0:T(8,128)S(1)} %get-tuple-element.480.refs_1_, ...), custom_call_target="tpu_custom_call" | custom-call | bytes 1 | tf_op jit(solution)/shard_map/taskback_1/pallas_call | solution.py:693
  240.4 6.0 %taskback_0.1 = (bf16[3,576,128]{2,1,0:T(8,128)(2,1)}, bf16[2,3,576,128]{3,2,1,0:T(8,128)(2,1)S(1)}, f32[3,576,128]{2,1,0:T(8,128)S(1)}, f32[3,576,128]{2,1,0:T(8,128)S(1)}, f32[8,128]{1,0:T(8,128)S(1)}) custom-call(s32[1]{0:T(128)} %bitcast.refs_0_, f32[3,576,128]{2,1,0:T(8,128)S(1)} %get-tuple-element.563.refs_1_, ...), custom_call_target="tpu_custom_call" | custom-call | bytes 1 | tf_op jit(solution)/shard_map/taskback_0/pallas_call | solution.py:693
  254.9 7.4 %collective-permute-done.91.refs_1_ = bf16[144,128]{1,0:T(8,128)(2,1)S(1)} collective-permute-done((bf16[144,128]{1,0:T(8,128)(2,1)S(1)}, bf16[144,128]{1,0:T(8,128)(2,1)S(1)}, u32[]{:S(2)}, u32[]{:S(2)}) %collective-permute-start.91) | collective-permute-done | bytes 36896 | tf_op jit(solution)/shard_map/ppermute | solution.py:1127
  266.9 4.4 %collective-permute-done.93.refs_13_ = bf16[1,9,64,128]{3,2,1,0:T(8,128)(2,1)S(1)} collective-permute-done((bf16[1,9,64,128]{3,2,1,0:T(8,128)(2,1)S(1)}, bf16[1,9,64,128]{3,2,1,0:T(8,128)(2,1)S(1)}, u32[]{:S(2)}, u32[]{:S(2)}) %collective-permute-start.93) | collective-permute-done | bytes 147488 | tf_op jit(solution)/shard_map/ppermute | solution.py:832
  275.7 3.5 weight0_0.1
  298.8 3.5 weight1_0.1
  313.3 3.6 collective-permute-done.109.refs_5_
  322.5 3.5 weight2_0.1
  344.0 3.5 weighb_0.1
  364.6 3.5 weigha_0.1
  372.8 4.6 %collective-permute-done.135.refs_1_ = bf16[3,128,128]{2,1,0:T(8,128)(2,1)S(1)} collective-permute-done((bf16[3,128,128]{2,1,0:T(8,128)(2,1)S(1)}, bf16[3,128,128]{2,1,0:T(8,128)(2,1)S(1)}, u32[]{:S(2)}, u32[]{:S(2)}) %collective-permute-start.135) | collective-permute-done | bytes 98336 | tf_op jit(solution)/shard_map/ppermute | solution.py:832
  391.4 6.8 %collective-permute-done.131.refs_3_ = bf16[1,9,64,128]{3,2,1,0:T(8,128)(2,1)S(1)} collective-permute-done((bf16[1,9,64,128]{3,2,1,0:T(8,128)(2,1)S(1)}, bf16[1,9,64,128]{3,2,1,0:T(8,128)(2,1)S(1)}, u32[]{:S(2)}, u32[]{:S(2)}) %collective-permute-start.131) | collective-permute-done | bytes 147488 | tf_op jit(solution)/shard_map/ppermute | solution.py:832
  401.4 5.3 %collective-permute-done.136.refs_19_ = bf16[3,128,128]{2,1,0:T(8,128)(2,1)S(1)} collective-permute-done((bf16[3,128,128]{2,1,0:T(8,128)(2,1)S(1)}, bf16[3,128,128]{2,1,0:T(8,128)(2,1)S(1)}, u32[]{:S(2)}, u32[]{:S(2)}) %collective-permute-start.136) | collective-permute-done | bytes 98336 | tf_op jit(solution)/shard_map/ppermute | solution.py:832
  410.8 6.3 %collective-permute-done.141.refs_25_ = bf16[3,128,128]{2,1,0:T(8,128)(2,1)S(1)} collective-permute-done((bf16[3,128,128]{2,1,0:T(8,128)(2,1)S(1)}, bf16[3,128,128]{2,1,0:T(8,128)(2,1)S(1)}, u32[]{:S(2)}, u32[]{:S(2)}) %collective-permute-start.141) | collective-permute-done | bytes 98336 | tf_op jit(solution)/shard_map/ppermute | solution.py:832
  420.5 3.7 finish.1
  (415 shorter events, 317.3 us)
Async XLA Ops:
  13.0 18.5 %collective-permute-start.11 = (bf16[2,2,3,128,128]{4,3,2,1,0:T(8,128)(2,1)S(1)}, bf16[2,2,3,128,128]{4,3,2,1,0:T(8,128)(2,1)S(1)}, u32[]{:S(2)}, u32[]{:S(2)}) collective-permute-start(bf16[2,2,3,128,128]{4,3,2,1,0:T(8,128)(2,1)S(1)} %get-tuple-element.395.refs_1_), channel_id=1, source_target_pairs={{0,2},{2,0},{1,3},{3,1},{4,6},{6,4},{5,7},{7,5},{8,10},{10,8},{9,1... | collective-permute-start | bytes 1179656 | tf_op jit(solution)/shard_map/ppermute | solution.py:726
  14.8 16.7 %collective-permute-start.14 = (f32[2,6,128]{2,1,0:T(8,128)S(1)}, f32[2,6,128]{2,1,0:T(8,128)S(1)}, u32[]{:S(2)}, u32[]{:S(2)}) collective-permute-start(f32[2,6,128]{2,1,0:T(8,128)S(1)} %get-tuple-element.398.refs_5_), channel_id=1, source_target_pairs={{0,2},{2,0},{1,3},{3,1},{4,6},{6,4},{5,7},{7,5},{8,10},{10,8},{9,1... | collective-permute-start | bytes 18440 | tf_op jit(solution)/shard_map/ppermute | solution.py:726
  15.1 16.5 %collective-permute-start.13 = (f32[2,6,128]{2,1,0:T(8,128)S(1)}, f32[2,6,128]{2,1,0:T(8,128)S(1)}, u32[]{:S(2)}, u32[]{:S(2)}) collective-permute-start(f32[2,6,128]{2,1,0:T(8,128)S(1)} %get-tuple-element.398.refs_5_), channel_id=1, source_target_pairs={{0,1},{1,0},{2,3},{3,2},{4,5},{5,4},{6,7},{7,6},{8,9},{9,8},{10,11... | collective-permute-start | bytes 18440 | tf_op jit(solution)/shard_map/ppermute | solution.py:727
  89.4 14.7 %collective-permute-start.39 = (bf16[2,576,128]{2,1,0:T(8,128)(2,1)S(1)}, bf16[2,576,128]{2,1,0:T(8,128)(2,1)S(1)}, u32[]{:S(2)}, u32[]{:S(2)}) collective-permute-start(bf16[2,576,128]{2,1,0:T(8,128)(2,1)S(1)} %get-tuple-element.454), channel_id=1, source_target_pairs={{0,8},{4,12},{8,0},{12,4},{16,24},{20,28},{24,16},{28,20},{1,9},{5... | collective-permute-start | bytes 884744 | tf_op jit(solution)/shard_map/ppermute | solution.py:832
  89.4 14.7 %collective-permute-start.38 = (bf16[2,576,128]{2,1,0:T(8,128)(2,1)S(1)}, bf16[2,576,128]{2,1,0:T(8,128)(2,1)S(1)}, u32[]{:S(2)}, u32[]{:S(2)}) collective-permute-start(bf16[2,576,128]{2,1,0:T(8,128)(2,1)S(1)} %get-tuple-element.452), channel_id=1, source_target_pairs={{0,8},{4,12},{8,0},{12,4},{16,24},{20,28},{24,16},{28,20},{1,9},{5... | collective-permute-start | bytes 884744 | tf_op jit(solution)/shard_map/ppermute | solution.py:832
  187.8 17.7 %collective-permute-start.74 = (bf16[2,9,64,128]{3,2,1,0:T(8,128)(2,1)S(1)}, bf16[2,9,64,128]{3,2,1,0:T(8,128)(2,1)S(1)}, u32[]{:S(2)}, u32[]{:S(2)}) collective-permute-start(bf16[2,9,64,128]{3,2,1,0:T(8,128)(2,1)S(1)} %get-tuple-element.545), channel_id=1, source_target_pairs={{0,4},{4,0},{8,12},{12,8},{16,20},{20,16},{24,28},{28,24},{1,5},{5... | collective-permute-start | bytes 884744 | tf_op jit(solution)/shard_map/ppermute | solution.py:832
  188.5 17.0 %collective-permute-start.73 = (bf16[2,576,128]{2,1,0:T(8,128)(2,1)S(1)}, bf16[2,576,128]{2,1,0:T(8,128)(2,1)S(1)}, u32[]{:S(2)}, u32[]{:S(2)}) collective-permute-start(bf16[2,576,128]{2,1,0:T(8,128)(2,1)S(1)} %get-tuple-element.543), channel_id=1, source_target_pairs={{0,8},{4,12},{8,0},{12,4},{16,24},{20,28},{24,16},{28,20},{1,9},{5... | collective-permute-start | bytes 884744 | tf_op jit(solution)/shard_map/ppermute | solution.py:832
  188.5 17.0 %collective-permute-start.72 = (bf16[2,9,64,128]{3,2,1,0:T(8,128)(2,1)S(1)}, bf16[2,9,64,128]{3,2,1,0:T(8,128)(2,1)S(1)}, u32[]{:S(2)}, u32[]{:S(2)}) collective-permute-start(bf16[2,9,64,128]{3,2,1,0:T(8,128)(2,1)S(1)} %get-tuple-element.541), channel_id=1, source_target_pairs={{0,4},{4,0},{8,12},{12,8},{16,20},{20,16},{24,28},{28,24},{1,5},{5... | collective-permute-start | bytes 884744 | tf_op jit(solution)/shard_map/ppermute | solution.py:832
  249.9 21.4 %collective-permute-start.96 = (bf16[3,576,128]{2,1,0:T(8,128)(2,1)S(1)}, bf16[3,576,128]{2,1,0:T(8,128)(2,1)S(1)}, u32[]{:S(2)}, u32[]{:S(2)}) collective-permute-start(bf16[3,576,128]{2,1,0:T(8,128)(2,1)S(1)} %copy-done.6), channel_id=1, source_target_pairs={{0,8},{4,12},{8,0},{12,4},{16,24},{20,28},{24,16},{28,20},{1,9},{5... | collective-permute-start | bytes 1327112 | tf_op jit(solution)/shard_map/ppermute | solution.py:832
  249.9 21.4 %collective-permute-start.92 = (bf16[2,9,64,128]{3,2,1,0:T(8,128)(2,1)S(1)}, bf16[2,9,64,128]{3,2,1,0:T(8,128)(2,1)S(1)}, u32[]{:S(2)}, u32[]{:S(2)}) collective-permute-start(bf16[2,9,64,128]{3,2,1,0:T(8,128)(2,1)S(1)} %get-tuple-element.605), channel_id=1, source_target_pairs={{0,4},{4,0},{8,12},{12,8},{16,20},{20,16},{24,28},{28,24},{1,5},{5... | collective-permute-start | bytes 884744 | tf_op jit(solution)/shard_map/ppermute | solution.py:832
  290.7 18.2 %collective-permute-start.102 = (bf16[3,576,128]{2,1,0:T(8,128)(2,1)S(1)}, bf16[3,576,128]{2,1,0:T(8,128)(2,1)S(1)}, u32[]{:S(2)}, u32[]{:S(2)}) collective-permute-start(bf16[3,576,128]{2,1,0:T(8,128)(2,1)S(1)} %get-tuple-element.624.refs_0_), channel_id=1, source_target_pairs={{0,2},{2,0},{1,3},{3,1},{4,6},{6,4},{5,7},{7,5},{8,10},{10,8},{9,1... | collective-permute-start | bytes 1327112 | tf_op jit(solution)/shard_map/ppermute | solution.py:1185
  294.3 16.8 %collective-permute-start.104 = (bf16[2,9,64,128]{3,2,1,0:T(8,128)(2,1)S(1)}, bf16[2,9,64,128]{3,2,1,0:T(8,128)(2,1)S(1)}, u32[]{:S(2)}, u32[]{:S(2)}) collective-permute-start(bf16[2,9,64,128]{3,2,1,0:T(8,128)(2,1)S(1)} %get-tuple-element.641), channel_id=1, source_target_pairs={{0,4},{4,0},{8,12},{12,8},{16,20},{20,16},{24,28},{28,24},{1,5},{5... | collective-permute-start | bytes 884744 | tf_op jit(solution)/shard_map/ppermute | solution.py:832
  302.4 14.5 %collective-permute-start.108 = (bf16[2,9,64,128]{3,2,1,0:T(8,128)(2,1)S(1)}, bf16[2,9,64,128]{3,2,1,0:T(8,128)(2,1)S(1)}, u32[]{:S(2)}, u32[]{:S(2)}) collective-permute-start(bf16[2,9,64,128]{3,2,1,0:T(8,128)(2,1)S(1)} %get-tuple-element.646), channel_id=1, source_target_pairs={{0,4},{4,0},{8,12},{12,8},{16,20},{20,16},{24,28},{28,24},{1,5},{5... | collective-permute-start | bytes 884744 | tf_op jit(solution)/shard_map/ppermute | solution.py:832
  303.2 14.9 %collective-permute-start.107 = (bf16[2,9,64,128]{3,2,1,0:T(8,128)(2,1)S(1)}, bf16[2,9,64,128]{3,2,1,0:T(8,128)(2,1)S(1)}, u32[]{:S(2)}, u32[]{:S(2)}) collective-permute-start(bf16[2,9,64,128]{3,2,1,0:T(8,128)(2,1)S(1)} %get-tuple-element.645), channel_id=1, source_target_pairs={{0,4},{4,0},{8,12},{12,8},{16,20},{20,16},{24,28},{28,24},{1,5},{5... | collective-permute-start | bytes 884744 | tf_op jit(solution)/shard_map/ppermute | solution.py:832
  359.1 20.6 %collective-permute-start.128 = (bf16[2,9,64,128]{3,2,1,0:T(8,128)(2,1)S(1)}, bf16[2,9,64,128]{3,2,1,0:T(8,128)(2,1)S(1)}, u32[]{:S(2)}, u32[]{:S(2)}) collective-permute-start(bf16[2,9,64,128]{3,2,1,0:T(8,128)(2,1)S(1)} %get-tuple-element.702), channel_id=1, source_target_pairs={{0,4},{4,0},{8,12},{12,8},{16,20},{20,16},{24,28},{28,24},{1,5},{5... | collective-permute-start | bytes 884744 | tf_op jit(solution)/shard_map/ppermute | solution.py:832
  368.1 17.7 %collective-permute-start.138 = (bf16[2,9,64,128]{3,2,1,0:T(8,128)(2,1)S(1)}, bf16[2,9,64,128]{3,2,1,0:T(8,128)(2,1)S(1)}, u32[]{:S(2)}, u32[]{:S(2)}) collective-permute-start(bf16[2,9,64,128]{3,2,1,0:T(8,128)(2,1)S(1)} %get-tuple-element.733), channel_id=1, source_target_pairs={{0,4},{4,0},{8,12},{12,8},{16,20},{20,16},{24,28},{28,24},{1,5},{5... | collective-permute-start | bytes 884744 | tf_op jit(solution)/shard_map/ppermute | solution.py:832
  370.2 14.6 %collective-permute-start.132 = (bf16[1,9,64,128]{3,2,1,0:T(8,128)(2,1)S(1)}, bf16[1,9,64,128]{3,2,1,0:T(8,128)(2,1)S(1)}, u32[]{:S(2)}, u32[]{:S(2)}) collective-permute-start(bf16[1,9,64,128]{3,2,1,0:T(8,128)(2,1)S(1)} %get-tuple-element.715), channel_id=1, source_target_pairs={{0,16},{4,20},{8,24},{12,28},{16,0},{20,4},{24,8},{28,12},{1,17},{... | collective-permute-start | bytes 442376 | tf_op jit(solution)/shard_map/ppermute | solution.py:832
  377.5 20.7 %collective-permute-start.131 = (bf16[1,9,64,128]{3,2,1,0:T(8,128)(2,1)S(1)}, bf16[1,9,64,128]{3,2,1,0:T(8,128)(2,1)S(1)}, u32[]{:S(2)}, u32[]{:S(2)}) collective-permute-start(bf16[1,9,64,128]{3,2,1,0:T(8,128)(2,1)S(1)} %get-tuple-element.710), channel_id=1, source_target_pairs={{0,16},{4,20},{8,24},{12,28},{16,0},{20,4},{24,8},{28,12},{1,17},{... | collective-permute-start | bytes 442376 | tf_op jit(solution)/shard_map/ppermute | solution.py:832
  379.7 21.6 %collective-permute-start.133 = (bf16[1,9,64,128]{3,2,1,0:T(8,128)(2,1)S(1)}, bf16[1,9,64,128]{3,2,1,0:T(8,128)(2,1)S(1)}, u32[]{:S(2)}, u32[]{:S(2)}) collective-permute-start(bf16[1,9,64,128]{3,2,1,0:T(8,128)(2,1)S(1)} %get-tuple-element.717), channel_id=1, source_target_pairs={{0,16},{4,20},{8,24},{12,28},{16,0},{20,4},{24,8},{28,12},{1,17},{... | collective-permute-start | bytes 442376 | tf_op jit(solution)/shard_map/ppermute | solution.py:832
  384.8 21.8 %collective-permute-start.136 = (bf16[3,128,128]{2,1,0:T(8,128)(2,1)S(1)}, bf16[3,128,128]{2,1,0:T(8,128)(2,1)S(1)}, u32[]{:S(2)}, u32[]{:S(2)}) collective-permute-start(bf16[3,128,128]{2,1,0:T(8,128)(2,1)S(1)} %get-tuple-element.730.refs_18_), channel_id=1, source_target_pairs={{0,16},{4,20},{8,24},{12,28},{16,0},{20,4},{24,8},{28,12},{1,17},{... | collective-permute-start | bytes 294920 | tf_op jit(solution)/shard_map/ppermute | solution.py:832
  385.8 25.1 %collective-permute-start.130 = (bf16[1,9,64,128]{3,2,1,0:T(8,128)(2,1)S(1)}, bf16[1,9,64,128]{3,2,1,0:T(8,128)(2,1)S(1)}, u32[]{:S(2)}, u32[]{:S(2)}) collective-permute-start(bf16[1,9,64,128]{3,2,1,0:T(8,128)(2,1)S(1)} %get-tuple-element.707), channel_id=1, source_target_pairs={{0,16},{4,20},{8,24},{12,28},{16,0},{20,4},{24,8},{28,12},{1,17},{... | collective-permute-start | bytes 442376 | tf_op jit(solution)/shard_map/ppermute | solution.py:832
  389.5 34.6 %collective-permute-start.142 = (bf16[1,9,64,128]{3,2,1,0:T(8,128)(2,1)S(1)}, bf16[1,9,64,128]{3,2,1,0:T(8,128)(2,1)S(1)}, u32[]{:S(2)}, u32[]{:S(2)}) collective-permute-start(bf16[1,9,64,128]{3,2,1,0:T(8,128)(2,1)S(1)} %get-tuple-element.744), channel_id=1, source_target_pairs={{0,16},{4,20},{8,24},{12,28},{16,0},{20,4},{24,8},{28,12},{1,17},{... | collective-permute-start | bytes 442376 | tf_op jit(solution)/shard_map/ppermute | solution.py:832
  398.2 19.0 %collective-permute-start.141 = (bf16[3,128,128]{2,1,0:T(8,128)(2,1)S(1)}, bf16[3,128,128]{2,1,0:T(8,128)(2,1)S(1)}, u32[]{:S(2)}, u32[]{:S(2)}) collective-permute-start(bf16[3,128,128]{2,1,0:T(8,128)(2,1)S(1)} %get-tuple-element.740.refs_24_), channel_id=1, source_target_pairs={{0,16},{4,20},{8,24},{12,28},{16,0},{20,4},{24,8},{28,12},{1,17},{... | collective-permute-start | bytes 294920 | tf_op jit(solution)/shard_map/ppermute | solution.py:832
  401.4 17.9 %collective-permute-start.139 = (bf16[3,128,128]{2,1,0:T(8,128)(2,1)S(1)}, bf16[3,128,128]{2,1,0:T(8,128)(2,1)S(1)}, u32[]{:S(2)}, u32[]{:S(2)}) collective-permute-start(bf16[3,128,128]{2,1,0:T(8,128)(2,1)S(1)} %get-tuple-element.737.refs_20_), channel_id=1, source_target_pairs={{0,16},{4,20},{8,24},{12,28},{16,0},{20,4},{24,8},{28,12},{1,17},{... | collective-permute-start | bytes 294920 | tf_op jit(solution)/shard_map/ppermute | solution.py:832
  (134 other events, 889.8 us)

commit v2 on v1

--- a/solution.py
+++ b/solution.py
@@ -138,7 +138,10 @@
 
 def spread_stats(out, rows):
     for place, row in enumerate(rows):
-        out[place : place + 1] = row
+        if len(out.shape) == 2:
+            out[place : place + 1] = row
+        else:
+            out[:, place : place + 1] = jnp.broadcast_to(row[None], (out.shape[0],) + row.shape)
 
 
 def moments(v):
@@ -294,6 +297,15 @@
     part[...] = keep[...] + got[0].astype(F32)
 
 
+def pair_tasks_body(keep, far, got, keep_x, far_x, got_x, out, part, part_x):
+    size = far.shape[1]
+    for t in range(far.shape[0]):
+        out[t * size : (t + 1) * size] = (far[t] + got[1, t].astype(F32)).astype(LOW)
+        part[t] = keep[t] + got[0, t].astype(F32)
+    out[far.shape[0] * size :] = (far_x[...] + got_x[1].astype(F32)).astype(LOW)
+    part_x[...] = keep_x[...] + got_x[0].astype(F32)
+
+
 def mixed_body(a, b, out):
     out[...] = a[...] + b[...].astype(F32)
 
@@ -307,11 +319,22 @@
     out[...] = (a[...].astype(F32) + b[...].astype(F32)).astype(out.dtype)
 
 
-def sum_body(*refs):
+def sum_body(copies, out):
+    total = copies[0]
+    for i in range(1, copies.shape[0]):
+        total = total + copies[i]
+    out[...] = total
+
+
+def sum_all_body(*refs):
     parts = [ref[...] for ref in refs[:-1]]
     while len(parts) > 1:
         parts = [a + b for a, b in zip(parts[::2], parts[1::2])]
     refs[-1][...] = parts[0]
+
+
+def mark_body(out):
+    out[...] = jnp.zeros_like(out)
 
 
 def task_last_body(l, count, width, y, raw, gain, shift, dq, out, d, stats, scratch):
@@ -378,67 +401,103 @@
     far[...] = blocks[2]
 
 
-def weight_body(width, many, im, x, dys, dk, cat, dkf):
-    images = dk.shape[0]
-    share = 512 // images
+def task_weights_body(width, x, dys, out, cat, total):
     ready(x)
     ready(dys)
 
     def one(t, carry):
-        dy = dys[t] if many else dys[...]
-        spread_taps(dy.astype(F32), width, cat)
-        dkf[...] = dot_tn(x[t] if many else x[...], cat[...])
-
-        def copy(r, carry):
-            rows = pl.ds(pl.multiple_of(r * share, share), share)
+        spread_taps(dys.ref[t].astype(F32), width, cat)
+        total[...] = dot_tn(x.ref[t], cat[...])
+        for tap in range(9):
+            out.ref[t, tap] = total[:, tap * 128 : tap * 128 + 128].astype(LOW)
+        return carry
+
+    lax.fori_loop(0, 3, one, 0)
+
+
+def widen_body(*refs):
+    out = refs[-1]
+    first = 0
+    for ref in refs[:-1]:
+        last = first + ref.shape[0]
+        out[first:last] = ref[...].astype(F32)
+        first = last
+
+
+def split_body(bit, im, *refs):
+    out = refs[-1]
+    low = (im[0] >> bit) & 1
+    for n, x in enumerate(refs[:-1]):
+        ready(x)
+        for i in range(2):
+            start = pl.multiple_of((2 * i + 1 - low) * 128, 128)
+            out[n, i] = x.ref[0, :, pl.ds(start, 128)]
+
+
+def pair_weight_body(width, bit, rest, picks, im, *refs):
+    stay, leave, cat, total = refs[-4:]
+    low = (im[0] >> bit) & 1
+    half = stay.shape[0]
+    share = stay.shape[3]
+    for n, (place_x, place_dy) in enumerate(picks):
+        x, other_x, dy, other_dy = refs[4 * n : 4 * n + 4]
+        ready(x)
+        ready(dy)
+        mine = [
+            x.ref[0, :, pl.ds(pl.multiple_of((2 * i + low) * 128, 128), 128)] for i in range(2)
+        ]
+        spread_taps(dy[0].astype(F32), width, cat)
+        total[...] = dot_tn(jnp.concatenate(mine, 1), cat[...])
+        theirs = [other_x[place_x, i] for i in range(2)]
+        grad = other_dy[...] if place_dy is None else other_dy[place_dy]
+        spread_taps(grad.astype(F32), width, cat)
+        total[...] += dot_tn(jnp.concatenate(theirs, 1), cat[...])
+        for e in range(2 * half):
+            mask = 0
+            for s, b in enumerate(rest):
+                mask |= ((e >> (len(rest) - 1 - s)) & 1) << b
+            block = im[0] ^ mask
+            row = ((block >> (bit + 1)) & 1) * 128 + (block & ((1 << bit) - 1)) * share
+            rows = pl.ds(pl.multiple_of(row, share), share)
+            target = stay if e < half else leave
             for tap in range(9):
-                dk[r, t, tap] = dkf[rows, tap * 128 : tap * 128 + 128].astype(LOW)
-            return carry
-
-        return lax.fori_loop(0, images, copy, carry)
-
-    lax.fori_loop(0, dk.shape[1], one, 0)
-
-
-def split_body(bit, im, x, out):
-    low = (im[0] >> bit) & 1
-    ready(x)
-    for i in range(2):
-        start = pl.multiple_of((2 * i + 1 - low) * 128, 128)
-        out[i] = x.ref[0, :, pl.ds(start, 128)]
-
-
-def pair_weight_body(width, bit, rest, im, x, other_x, dy, other_dy, stay, leave, cat, total):
-    low = (im[0] >> bit) & 1
-    ready(x)
-    ready(dy)
-    mine = [x.ref[0, :, pl.ds(pl.multiple_of((2 * i + low) * 128, 128), 128)] for i in range(2)]
-    spread_taps(dy[0].astype(F32), width, cat)
-    total[...] = dot_tn(jnp.concatenate(mine, 1), cat[...])
-    spread_taps(other_dy[...].astype(F32), width, cat)
-    total[...] += dot_tn(jnp.concatenate([other_x[0], other_x[1]], 1), cat[...])
+                target[e % half, n, tap] = total[rows, tap * 128 : tap * 128 + 128].astype(LOW)
+
+
+def halve_body(*refs):
+    stay, leave = refs[-2:]
     half = stay.shape[0]
-    share = stay.shape[2]
-    for e in range(2 * half):
-        mask = 0
-        for s, b in enumerate(rest):
-            mask |= ((e >> (len(rest) - 1 - s)) & 1) << b
-        block = im[0] ^ mask
-        row = ((block >> (bit + 1)) & 1) * 128 + (block & ((1 << bit) - 1)) * share
-        rows = pl.ds(pl.multiple_of(row, share), share)
-        target = stay if e < half else leave
-        for tap in range(9):
-            target[e % half, tap] = total[rows, tap * 128 : tap * 128 + 128].astype(LOW)
-
-
-def halve_body(a, b, stay, leave):
-    half = stay.shape[0]
-    for i in range(half):
-        stay[i] = a[i].astype(F32) + b[i].astype(F32)
-        leave[i] = (a[half + i].astype(F32) + b[half + i].astype(F32)).astype(LOW)
+    first = 0
+    for a, b in zip(refs[:-2:2], refs[1:-2:2]):
+        last = first + a.shape[1]
+        for i in range(half):
+            stay[i, first:last] = a[i].astype(F32) + b[i].astype(F32)
+            leave[i, first:last] = (a[half + i].astype(F32) + b[half + i].astype(F32)).astype(LOW)
+        first = last
+
+
+def flat_body(*refs):
+    out = refs[-1]
+    share = out.shape[1]
+    rows = [ref[t] for ref in refs[:-1] for t in range(ref.shape[0])]
+    whole = jnp.concatenate(rows, 0)
+    for i in range(out.shape[0]):
+        out[i] = whole[i * share : (i + 1) * share]
+
+
+def spread_sum_body(copies, out):
+    total = copies[0].astype(F32)
+    for i in range(1, copies.shape[0]):
+        total = total + copies[i].astype(F32)
+    out[...] = jnp.broadcast_to(total.astype(LOW)[None], out.shape)
 
 
 def gate_grad_body(l, count, width, ch, part, far, s, up, zraw, y, raw, gain, shift, dx, d, d2, stats, scratch):
+    size = y.shape[0]
+    if len(dx) == 1:
+        grad = dx[0][...]
+    else:
+        grad = dx[0][...] + far[3 * size :].astype(F32)
     mean, inverse = bn_of(raw, 0, count)
     normal = (y[...] - mean) * inverse
     v = normal * gain[l, 1:2] + shift[l, 1:2]
@@ -446,13 +505,13 @@
     act = v * sg
     own = pl.ds(pl.multiple_of(ch[0] * 128, 128), 128)
     ztotal = zraw[:, own]
-    upstream = unpool(dx[...], scratch, width)
+    upstream = unpool(grad, scratch, width)
     rows = []
     for t in range(3):
         zmean, zinverse = centre(ztotal[2 * t : 2 * t + 2], count)
         znormal = (dot(s[t], up[l, t]) - zmean) * zinverse
         m = sigmoid(znormal * gain[l, 5 + t : 6 + t] + shift[l, 5 + t : 6 + t])
-        dr = part[t] + far[t].astype(F32)
+        dr = part[t] + (far[t] if len(dx) == 1 else far[t * size : (t + 1) * size]).astype(F32)
         through = dr * m
         upstream = upstream + through
         grad = through * act * (1.0 - m)
@@ -549,7 +608,7 @@
 class Taps:
     def __init__(self, home, first, count):
         self.home, self.first, self.shape = home, first, (count,) + home.shape[1:]
-        self.dtype = home.dtype
+        self.dtype, self.near = home.dtype, None
 
 
 class Rows:
@@ -621,9 +680,7 @@
         picks.append((place, v))
     picks = picks[: len(args)]
     count = len(values)
-    far = [
-        isinstance(v, Taps) or (isinstance(v, Long) and v.near is None) for v in values
-    ]
+    far = [isinstance(v, (Taps, Long)) and v.near is None for v in values]
     saved = [i for i, v in enumerate(values) if isinstance(v, Long) and v.home is None]
     hbm, vmem = pl.BlockSpec(memory_space=pltpu.HBM), pl.BlockSpec(memory_space=pltpu.VMEM)
     operands, specs = [], []
@@ -632,7 +689,7 @@
             operands.append(pltpu.with_memory_space_constraint(v.home, pltpu.HBM))
             specs.append(hbm)
         else:
-            operands.append(v.near if isinstance(v, Long) else v)
+            operands.append(v.near if isinstance(v, (Taps, Long)) else v)
             specs.append(spec_of(operands[-1]))
     after = list(after) + TURN
     TURN.clear()
@@ -706,12 +763,50 @@
     answer = list(results[: len(outs)])
     TURN.append(answer.pop())
     for i, home in zip(saved, results[len(outs) :]):
-        values[i].home, values[i].near = home, None
+        values[i].home = home
+    for v in values:
+        if isinstance(v, (Taps, Long)):
+            v.near = None
     for i in keep:
         answer[i] = Long(answer[i])
     for i in away:
         answer[i] = Long(None, answer[i])
     return answer
+
+
+def bring(items, name):
+    items = [v for v in items if v.near is None]
+    if not items:
+        return
+    count = len(items)
+
+    def body(*refs):
+        turn, sems = refs[2 * count + 1], refs[-1]
+        copies = []
+        for i, item in enumerate(items):
+            source = refs[i]
+            if isinstance(item, Taps):
+                source = source.at[item.first : item.first + item.shape[0]]
+            copies.append(pltpu.make_async_copy(source, refs[count + 1 + i], sems.at[i]))
+            copies[-1].start()
+        turn[...] = jnp.zeros_like(turn)
+        for copy in copies:
+            copy.wait()
+
+    hbm, vmem = pl.BlockSpec(memory_space=pltpu.HBM), pl.BlockSpec(memory_space=pltpu.VMEM)
+    results = pl.pallas_call(
+        body,
+        out_shape=[pltpu.VMEM(v.shape, v.dtype) for v in items] + [pltpu.VMEM((8, 128), F32)],
+        in_specs=[hbm] * count + [vmem],
+        out_specs=[vmem] * (count + 1),
+        scratch_shapes=[pltpu.SemaphoreType.DMA((count,))],
+        compiler_params=pltpu.CompilerParams(vmem_limit_bytes=VMEM_LIMIT),
+        cost_estimate=pl.CostEstimate(flops=0, bytes_accessed=1, transcendentals=0),
+        name=name,
+    )(*[pltpu.with_memory_space_constraint(v.home, pltpu.HBM) for v in items], TURN.pop())
+    TURN.append(results[count])
+    for v, near in zip(items, results):
+        v.near = near
 
 
 def spec_of(value):
@@ -779,7 +874,7 @@
     n0, n1 = sizes
 
     def stats_of(rows, lanes=128):
-        return shape_of((rows, lanes))
+        return shape_of((images, rows, lanes))
 
     one, two = Layer(), Layer()
     kept = [one, two]
@@ -787,7 +882,29 @@
     TURN.clear()
     pending, held = [], []
 
-    def total_of(rows, name, first=(), second=(), mid=()):
+    def total_of(copies, name, steps=(), mid=(), ahead=()):
+        if pending:
+            copies = hold(copies, list(pending))
+            pending.clear()
+        got = swap_img(copies)
+        if mid and not steps:
+            run(mark_body, (), [shape_of((8, 128))], name="mark")
+        for place, step in enumerate(steps):
+            step()
+            if place == 0:
+                for blocks in mid:
+                    add_last(blocks, TURN[0])
+        if mid and not steps:
+            for blocks in mid:
+                add_last(blocks, TURN[0])
+        bring(ahead, f"bring{name}")
+        total = run(sum_body, (got,), [shape_of(copies.shape[1:])], name=name, keep=(0,))[0]
+        for make in held:
+            make(total.near)
+        held.clear()
+        return total
+
+    def total_by_pairs(rows, name, first, second, mid, ahead=()):
         if pending:
             rows = hold(rows, list(pending))
             pending.clear()
@@ -801,14 +918,12 @@
                 lax.ppermute(rows, "img", [(i, i ^ s) for i in range(images)]) for s in shifts[1:]
             ]
             last = place == len(groups) - 1
+            for step in (first if place == 0 else []) + (second if last else []):
+                step()
             if place == 0:
-                for step in first:
-                    step()
-            if last:
-                for step in second:
-                    step()
+                bring(ahead, f"bring{name}")
             rows = run(
-                sum_body,
+                sum_all_body,
                 parts,
                 [shape_of(rows.shape)],
                 name=f"{name}_{place}",
@@ -822,11 +937,13 @@
         return rows
 
     def gap(steps):
+        waiting = list(held)
+        held.clear()
         for step in steps:
             step()
         for make in held:
             make(None)
-        held.clear()
+        held[:] = waiting
 
     def send_img(value, bit):
         got = lax.ppermute(value, "img", [(i, i ^ (1 << bit)) for i in range(images)])
@@ -837,95 +954,163 @@
     pair_bit = 7 - (share.bit_length() - 1)
     rest = [b for b in range(bits) if b != pair_bit]
 
-    class Weights:
-        def __init__(self, l, name):
-            self.l, self.name, self.step, self.done = l, name, 0, None
+    def later(owner, field, value, bit):
+        def make(total):
+            setattr(owner, field, send_img(value if total is None else hold(value, total), bit))
+
+        held.append(make)
+
+    class Meeting:
+        pass
+
+    class Conv:
+        def __init__(self, name):
+            self.name, self.l = name, int(name[-1])
 
         def take(self, x, place):
             self.x = Taps(x.home.reshape((-1,) + x.shape[-2:]), place, 1)
 
-        def split(self):
+    class Split:
+        def __init__(self, names):
+            self.names = names
+            for place, name in enumerate(names):
+                convs[name].split, convs[name].place_x = self, place
+
+        def go(self):
+            members = [convs[name] for name in self.names]
             out = run(
                 functools.partial(split_body, pair_bit),
-                (img, self.x),
-                [shape_of((2, sizes[self.l], 128), LOW)],
-                name=f"split{self.name}",
+                (img, *[c.x for c in members]),
+                [shape_of((len(members), 2, sizes[members[0].l], 128), LOW)],
+                name="split" + "".join(self.names),
             )[0]
-            self.later(out, pair_bit, "other_x")
-
-        def later(self, value, bit, name):
-            def make(total):
-                setattr(self, name, send_img(value if total is None else hold(value, total), bit))
-
-            held.append(make)
-
-        def meet(self, dys, place, other):
-            self.dy = Taps(dys.home.reshape((-1,) + dys.shape[-2:]), place, 1)
-            self.other_dy = other
+            later(self, "got", out, pair_bit)
+
+    class Weights:
+        def __init__(self, names):
+            self.members, self.name, self.step = [convs[n] for n in names], "".join(names), 0
+            self.parts, self.placed = [self], False
 
         def weigh(self):
-            n, half = sizes[self.l], images // 4
-            stay, leave = run(
-                functools.partial(pair_weight_body, widths[self.l], pair_bit, rest),
-                (img, self.x, self.other_x, self.dy, self.other_dy),
-                [shape_of((half, 9, share, 128), LOW)] * 2,
-                scratch=[pltpu.VMEM((n, 1152), LOW), pltpu.VMEM((256, 1152), F32)],
+            l = self.members[0].l
+            args, picks = [], []
+            for c in self.members:
+                args += [c.x, c.split.got, c.dy, c.meeting.got]
+                picks.append((c.place_x, c.place_dy))
+            shape = shape_of((images // 4, len(picks), 9, share, 128), LOW)
+            self.stay, leave = run(
+                functools.partial(pair_weight_body, widths[l], pair_bit, rest, picks),
+                (img, *args),
+                [shape] * 2,
+                scratch=[pltpu.VMEM((sizes[l], 1152), LOW), pltpu.VMEM((256, 1152), F32)],
                 name=f"weigh{self.name}",
                 away=(0,),
             )
-            self.stay, self.step = stay, 1
-            self.later(leave, rest[0], "got")
+            self.step = 1
+            later(self, "got", leave, rest[0])
 
         def halve(self):
-            half = self.stay.shape[0] // 2
-            stay, leave = run(
+            args = []
+            for part in self.parts:
+                args += [part.stay, part.got]
+            self.step = self.parts[0].step
+            self.parts = [self]
+            shape = (args[0].shape[0] // 2, len(self.members)) + args[0].shape[2:]
+            self.stay, leave = run(
                 halve_body,
-                (self.stay, self.got),
-                [shape_of((half, 9, share, 128)), shape_of((half, 9, share, 128), LOW)],
+                args,
+                [shape_of(shape), shape_of(shape, LOW)],
                 name=f"halve{self.name}_{self.step}",
                 away=(0,),
             )
-            self.stay = stay
-            self.later(leave, rest[self.step], "got")
+            later(self, "got", leave, rest[self.step])
             self.step += 1
 
-    class Shared(Weights):
-        def __init__(self, name):
-            self.name, self.step, self.got = name, 0, None
-
-        def add(self):
-            if self.step > 0:
-                self.value = run(
-                    add_body,
-                    (self.value, self.got),
-                    [shape_of(self.value.shape, LOW)],
-                    name=f"{self.name}_{self.step}",
-                    )[0]
-            else:
-                self.value = self.value.home
-            self.later(self.value, self.step, "got")
-            self.step += 1
-
-    jobs = {
-        name: Weights(int(name[-1]), name)
-        for name in ["t0_0", "t1_0", "t2_0", "t0_1", "t1_1", "t2_1", "a_0", "b_0", "a_1", "b_1"]
-    }
-    for name in ["up_0", "up_1", "down_0", "down_1"]:
-        jobs[name] = Shared(name)
-
-    def tasks_of(l):
-        return [jobs[f"t{t}_{l}"] for t in range(tasks)]
-
-    def meet(names, dys):
-        got = send_img(dys.home, pair_bit)
-        if len(names) == 1:
-            jobs[names[0]].meet(dys, 0, got)
+        def put(self):
+            self.placed = True
+            places = [PLACES[c.name] for c in self.members]
+            first = list(buffers)
+            count = len(places)
+
+            def body(*refs):
+                stay, got, _, turn, out, value, other, sems = refs[len(first) :]
+                load = pltpu.make_async_copy(stay.at[0], other, sems.at[count])
+                load.start()
+                turn[...] = jnp.zeros_like(turn)
+                load.wait()
+                copies = []
+                for n, place in enumerate(places):
+                    value[n] = other[n].astype(F32) + got[0, n].astype(F32)
+                    copies.append(pltpu.make_async_copy(value.at[n], out.at[place], sems.at[n]))
+                    copies[-1].start()
+                for copy in copies:
+                    copy.wait()
+
+            stay = self.stay.home
+            turn, *buffers[:] = pl.pallas_call(
+                body,
+                out_shape=[
+                    pltpu.VMEM((8, 128), F32),
+                    pltpu.HBM((2 * layers, 9, share, 128), F32),
+                ],
+                in_specs=[hbm] * len(first) + [hbm, vmem, vmem],
+                out_specs=[vmem, hbm],
+                input_output_aliases={i: i + 1 for i in range(len(first))},
+                scratch_shapes=[
+                    pltpu.VMEM((count, 9, share, 128), F32),
+                    pltpu.VMEM((count, 9, share, 128), stay.dtype),
+                    pltpu.SemaphoreType.DMA((count + 1,)),
+                ],
+                compiler_params=pltpu.CompilerParams(vmem_limit_bytes=VMEM_LIMIT),
+                cost_estimate=pl.CostEstimate(flops=0, bytes_accessed=1, transcendentals=0),
+                name=f"put{self.name}",
+            )(
+                *[pltpu.with_memory_space_constraint(v, pltpu.HBM) for v in first],
+                pltpu.with_memory_space_constraint(stay, pltpu.HBM),
+                self.got,
+                TURN.pop(),
+            )
+            TURN.append(turn)
+
+    hbm, vmem = pl.BlockSpec(memory_space=pltpu.HBM), pl.BlockSpec(memory_space=pltpu.VMEM)
+    buffers = []
+    PLACES = {"a_0": 0, "b_0": 1, "a_1": 2, "b_1": 3}
+    convs = {name: Conv(name) for name in PLACES}
+
+    jobs = {names: Weights(names.split()) for names in ["b_1", "a_1", "b_0", "a_0"]}
+    splits = {names: Split(names.split()) for names in ["b_0", "a_0", "b_1 a_1"]}
+
+    def task_weights(l):
+        k = kept[l]
+        out = run(
+            functools.partial(task_weights_body, widths[l]),
+            (k.k, k.dys),
+            [shape_of((tasks, 9, 512, 128), LOW)],
+            scratch=[pltpu.VMEM((sizes[l], 1152), LOW), pltpu.VMEM((512, 1152), F32)],
+            name=f"weight_{l}",
+            away=(0,),
+        )[0]
+
+        def make(total):
+            value = out.home if total is None else hold(out.home, total)
+            k.task_w = lax.psum_scatter(value, "img", scatter_dimension=2, tiled=True)
+
+        held.append(make)
+
+    def meet(names, dys, wait=False):
+        for t, name in enumerate(names):
+            c = convs[name]
+            c.dy = Taps(dys.home.reshape((-1,) + dys.shape[-2:]), t, 1)
+            c.meeting, c.place_dy = Meeting(), t if len(names) > 1 else None
+        meeting = convs[names[0]].meeting
+        for name in names:
+            convs[name].meeting = meeting
+        if wait:
+            later(meeting, "got", dys.home, pair_bit)
         else:
-            for t, name in enumerate(names):
-                jobs[name].meet(dys, t, got[t])
+            meeting.got = send_img(dys.home, pair_bit)
 
     blocks = near_and_far(feats.reshape(n0, 128))
-    add_last(blocks)
     down_w, up_w = Long(None, down_w), Long(None, up_w)
     wide, narrow, params = run(
         pack_body,
@@ -940,6 +1125,8 @@
     )
     gains = Rows(params, 0, 8)
     norms = (gains, Rows(params, 8, 16))
+    add_last(blocks, TURN[0])
+    blocks[0] = Long(None, blocks[0])
     bottles = (Long(None, bottle_gain), Long(None, bottle_shift))
     one.x, one.y1, stats = run(
         functools.partial(first_conv_body, widths[0], 0),
@@ -953,8 +1140,10 @@
     scales = jnp.stack([seg_mask, depth_mask, jnp.ones_like(seg_mask)]).astype(F32)
     dq = (task_cot.astype(F32) * scales[..., None]).reshape(tasks, n1 // 4, 128)
     dq, dx = Long(dq), Long(shared_cot.astype(F32).reshape(n1 // 4, 128))
-    jobs["a_0"].take(one.x, 0)
-    one.raw1 = total_of(stats, "total1_0", [jobs["a_0"].split], mid=(wides, narrows))
+    convs["a_0"].take(one.x, 0)
+    one.raw1 = total_of(
+        stats, "total1_0", [splits["a_0"].go], (wides, narrows), [params]
+    )
     one.row1 = 0
     low, one.g = run(
         functools.partial(first_act_body, counts[0]),
@@ -985,7 +1174,7 @@
         keep=(1, 2),
         away=(0,),
     )
-    one.raw2 = total_of(stats, "total2_0")
+    one.raw2 = total_of(stats, "total2_0", ahead=[params, up_all, *bottles])
 
     def hidden(l):
         k, n = kept[l], sizes[l]
@@ -996,7 +1185,7 @@
             def inner(y, p, raw, gain, shift, bgain, bshift, up, s, u, zstats, scratch):
                 body(y, p, raw, gain, shift, bgain, bshift, up, s, u, None, zstats, scratch)
 
-            outs += [shape_of((n + n // 4, 128), LOW), stats_of(6, 512)]
+            outs += [shape_of((n + n // 4, 128), LOW), shape_of((6, 512))]
         else:
             inner = body
             outs += [shape_of((n, 128), LOW), shape_of((n // 4, 128), LOW), stats_of(6, 512)]
@@ -1047,12 +1236,15 @@
             away=(0, 1),
         )
 
-    jobs["b_0"].take(one.x2, 0)
-    one.zraw = total_of(zstats, "totalz_0", [jobs["b_0"].split], [next_conv], mid=(u_blocks,))
-    one.k, one.yt, stats = task_convs(0, u_blocks, Taps(task_taps, 0, tasks), two.more)
-    for t, job in enumerate(tasks_of(0)):
-        job.take(one.k, t)
-    one.traw = total_of(stats, "totalt_0", *[[job.split] for job in tasks_of(0)[:2]])
+    convs["b_0"].take(one.x2, 0)
+    taps = Taps(task_taps, 0, tasks)
+    one.zraw = total_by_pairs(
+        zstats, "totalz_0", [], [next_conv], (u_blocks,), [up_all, gates, taps]
+    )
+    one.k, one.yt, stats = task_convs(0, u_blocks, taps, two.more)
+    one.traw = total_of(
+        stats, "totalt_0", [splits["b_0"].go], ahead=[params, down_w, two.y1]
+    )
     two.raw1, two.row1 = one.traw, 6
 
     low, two.g, part = run(
@@ -1083,15 +1275,14 @@
         keep=(1, 2),
         away=(0,),
     )
-    two.raw2 = total_of(stats, "total2_1")
-    jobs["a_1"].take(two.x, 0)
-    jobs["b_1"].take(two.x2, 0)
+    two.raw2 = total_of(stats, "total2_1", ahead=[params, up_all, *bottles])
+    convs["a_1"].take(two.x, 0)
+    convs["b_1"].take(two.x2, 0)
     two.s, u, shared_out, zstats = hidden(1)
     u_blocks = near_and_far(u)
-    two.zraw = total_of(zstats, "totalz_1", mid=(u_blocks,))
-    two.k, two.yt, stats = task_convs(1, u_blocks, Taps(task_taps, tasks, tasks))
-    for t, job in enumerate(tasks_of(1)):
-        job.take(two.k, t)
+    taps = Taps(task_taps, tasks, tasks)
+    two.zraw = total_of(zstats, "totalz_1", [splits["b_1 a_1"].go], (u_blocks,))
+    two.k, two.yt, stats = task_convs(1, u_blocks, taps)
     two.traw = total_of(stats, "totalt_1")
 
     task_out, d, stats = run(
@@ -1101,8 +1292,11 @@
         scratch=[pltpu.VMEM((n1, 128), F32)],
         name="tasklast_1",
     )
-    splits = [job.split for job in tasks_of(1)]
-    two.dtraw = total_of(stats, "dtotalt_1", splits[:2], splits[2:])
+    taps = Taps(task_taps, tasks, tasks)
+    two.dtraw = total_of(
+        stats,
+        "dtotalt_1",
+    )
     two.dtrow = 0
 
     def back_outs(n, lead=()):
@@ -1126,22 +1320,34 @@
         )
         return (part, lax.ppermute(near, "ch", CHIP))
 
-    def steps(weigh="", halve="", add="", split=""):
-        return (
-            [jobs[name].weigh for name in weigh.split()]
-            + [jobs[name].halve for name in halve.split()]
-            + [jobs[name].add for name in add.split()]
-            + [jobs[name].split for name in split.split()]
-        )
+    def steps(weigh="", halve="", split="", put=""):
+        kinds = ((jobs, weigh, "weigh"), (jobs, halve, "halve"))
+        kinds += ((splits, split, "go"), (jobs, put, "put"))
+        return [
+            getattr(table[name], kind)
+            for table, names, kind in kinds
+            for name in names.split(", ")
+            if name
+        ]
+
+    flat = []
+
+    def flatten():
+        rows = run(
+            flat_body,
+            [part for k in kept for part in k.both],
+            [shape_of((images, layers * 2 * tasks * 128 // images, 128), LOW)],
+            name="flat",
+        )[0]
+        flat.append(swap_img(rows))
 
     plan = {
-        "gate_1": (steps("t0_1", "", "", "t2_0"), steps("t1_1", "", "", "b_1")),
-        "bottle_1": (steps("t2_1", "", "", "a_1"), steps()),
-        "first_1": (steps("b_1", "t0_1"), steps("", "t1_1")),
-        "gate_0": (steps("t0_0"), steps("", "t2_1")),
-        "hidden_0": steps("a_1 t1_0", "b_1", "up_1 down_1"),
-        "bottle_0": (steps("t2_0"), steps("", "t0_0", "up_1 down_1")),
-        "first_0": (steps("b_0"), steps("", "t1_0 a_1", "up_0")),
+        "gate_1": [functools.partial(task_weights, 1)],
+        "bottle_1": (),
+        "first_1": steps("b_1"),
+        "gate_0": steps("", "b_1"),
+        "bottle_0": steps("a_1"),
+        "first_0": steps("b_0", "a_1") + [flatten],
     }
     unfinished = None
 
@@ -1149,27 +1355,53 @@
         k, n, w, count = kept[l], sizes[l], widths[l], counts[l]
         dys, send, keep, far = run(
             functools.partial(task_back_body, l, count, w, k.dtrow),
-            (own, d, k.yt, k.traw, k.dtraw, gains, Taps(task_taps, tasks * l, tasks)),
+            (own, d, k.yt, k.traw, k.dtraw, gains, taps),
             back_outs(n, (tasks,)),
             scratch=back_scratch(n),
             name=f"taskback_{l}",
             away=(0,),
         )
-        meet([f"t{t}_{l}" for t in range(tasks)], dys)
-        if unfinished is not None:
-            parts_before = unfinished()
-        parts = scatter_ch(send, keep, far, f"pairr_{l}")
-        gap(plan.get(f"task_{l}", ()))
-        if unfinished is not None:
-            dx = run(mixed_body, parts_before, [shape_of((sizes[l + 1], 128))], name=f"dx_{l + 1}")[0]
+        k.dys = dys
+        if unfinished is None:
+            parts = scatter_ch(send, keep, far, f"pairr_{l}")
+            rest_dx = dx
+        else:
+            send_x, keep_x, far_x = unfinished
+            near, part, rest_dx = run(
+                pair_tasks_body,
+                (
+                    keep,
+                    far,
+                    lax.ppermute(send, "ch", CORE),
+                    keep_x,
+                    far_x,
+                    lax.ppermute(send_x, "ch", CORE),
+                ),
+                [
+                    shape_of((tasks * n + sizes[l + 1], 128), LOW),
+                    shape_of((tasks, n, 128)),
+                    shape_of((sizes[l + 1], 128)),
+                ],
+                name=f"pairr_{l}",
+            )
+            parts = (part, lax.ppermute(near, "ch", CHIP))
+        if l == 0:
+            task_weights(0)
+
+        def gate_grad(ch, part, far, s, up, zraw, y, raw, gain, shift, dx, *rest, first=unfinished, l=l, w=w):
+            more = (dx,) if first is None else (dx, far)
+            gate_grad_body(l, counts[l], w, ch, part, far, s, up, zraw, y, raw, gain, shift, more, *rest)
+
         d, d2, stats = run(
-            functools.partial(gate_grad_body, l, count, w),
-            (own, *parts, k.s, up_w, k.zraw, k.y2, k.raw2, *norms, dx),
+            gate_grad,
+            (own, *parts, k.s, up_w, k.zraw, k.y2, k.raw2, *norms, rest_dx),
             [shape_of((tasks, n, 128)), shape_of((n, 128)), stats_of(8)],
             scratch=[pltpu.VMEM((n, 128), F32)],
             name=f"gategrad_{l}",
         )
-        k.draw2 = total_of(stats, f"dtotal2_{l}", *plan[f"gate_{l}"])
+        k.draw2 = total_of(
+            stats, f"dtotal2_{l}", plan[f"gate_{l}"], ahead=[k.s, up_w, k.zraw, params]
+        )
         d2 = Long(d2)
         ds, dup = run(
             functools.partial(hidden_grad_body, l, count),
@@ -1179,7 +1411,7 @@
             away=(1,),
             save=(d2,),
         )
-        jobs[f"up_{l}"].value = dup
+        k.dup = dup
         got = lax.ppermute(ds, "ch", CORE)
         near = run(pair_body, (ds, got), [shape_of(ds.shape, LOW)], name=f"pairs_{l}")[0]
         halves = near, lax.ppermute(near, "ch", CHIP)
@@ -1204,7 +1436,10 @@
             [shape_of((tasks, n, 128)), stats_of(6)],
             name=f"bottlegrad_{l}",
         )
-        k.draw3 = total_of(stats, f"dtotal3_{l}", *plan[f"bottle_{l}"])
+        wanted = [k.p, k.raw2, bottles[0], k.g, down_w, k.y1, k.raw1, params]
+        if l > 0:
+            wanted += [kept[l - 1].yt, kept[l - 1].traw]
+        k.draw3 = total_of(stats, f"dtotal3_{l}", plan[f"bottle_{l}"], ahead=wanted if l == 0 else ())
         args = (d, k.p, k.raw2, k.draw3, bottles[0], k.g, down_w, *parts, k.y1, k.raw1, *norms)
         outs = [shape_of((tasks, 128, 128), LOW), shape_of((n, 128))]
         if l > 0:
@@ -1226,8 +1461,13 @@
                 name=f"attendgrad_{l}",
                 away=(0,),
             )
-        jobs[f"down_{l}"].value = ddown
-        k.draw1 = total_of(stats, f"dtotal1_{l}", *plan[f"first_{l}"])
+        k.both = [ddown, k.dup]
+        last_taps = Taps(shared_taps, 2 * l, 1)
+        wanted = [k.y1, k.raw1, params, last_taps]
+        if l > 0:
+            taps = Taps(task_taps, tasks * (l - 1), tasks)
+            wanted.append(taps)
+        k.draw1 = total_of(stats, f"dtotal1_{l}", plan[f"first_{l}"], ahead=wanted if l == 0 else ())
         if l > 0:
             kept[l - 1].dtraw, kept[l - 1].dtrow = k.draw1, 2
             d1 = Long(d1)
@@ -1237,7 +1477,7 @@
 
         dys, send, keep, far = run(
             conv1_back,
-            (own, d1, k.y1, k.raw1, k.draw1, gains, Taps(shared_taps, 2 * l, 1)),
+            (own, d1, k.y1, k.raw1, k.draw1, gains, last_taps),
             back_outs(n),
             scratch=back_scratch(n),
             name=f"conv1back_{l}",
@@ -1245,14 +1485,31 @@
         )
         meet([f"a_{l}"], dys)
 
-        def unfinished(l=l, send=send, keep=keep, far=far):
-            return scatter_ch(send, keep, far, f"pairx_{l}")
-
-    parts = unfinished()
-    rows_of = [k.draw1, k.draw2, k.dtraw, k.draw3]
-    gap(steps("", "t2_0", "down_0 up_0"))
+        unfinished = (send, keep, far)
+
+    parts = scatter_ch(*unfinished, "pairx_0")
+    every = ["b_1", "a_1", "b_0", "a_0"]
+
+    def put_ready(names):
+        for name in names:
+            if jobs[name].step == len(rest) and not jobs[name].placed:
+                jobs[name].put()
+
+    put_ready(every[:2])
+    gap(steps("a_0"))
+    gap(steps("", "b_0"))
     dx = run(mixed_body, parts, [shape_of((n0, 128))], name="dx_0", away=(0,))[0].home
-    gap(steps("a_0", "b_0"))
+    gap(steps("", "a_0"))
+    flat = run(spread_sum_body, flat, [shape_of(flat[0].shape, LOW)], name="spread")[0]
+    flat = swap_img(flat)
+    tw = run(
+        widen_body,
+        [Long(None, k.task_w) for k in kept],
+        [shape_of((tasks * layers, 9, share, 128))],
+        name="tasksout",
+        away=(0,),
+    )[0].home
+
     order, places = [], []
     for k in kept:
         base = len(places)
@@ -1272,69 +1529,16 @@
         [shape_of((layers, 8, 128))] * 2 + [shape_of((layers, tasks, 128))] * 2,
         name="norms",
     )
-    gap(steps("", "", "down_0 up_0"))
-    gap(steps("", "a_0", "down_0"))
-    while any(job.step < (bits if isinstance(job, Shared) else len(rest)) for job in jobs.values()):
-        for job in jobs.values():
-            if job.step < (bits if isinstance(job, Shared) else len(rest)):
-                gap([job.add if isinstance(job, Shared) else job.halve])
-
-    names = ["b_0", "a_1", "b_1"]
-    names += [f"t{t}_{l}" for l in range(layers) for t in range(tasks)]
-    sums = ["up_0", "up_1", "down_0", "down_1"]
-    pieces = []
-    for name in names:
-        pieces += [jobs[name].stay, jobs[name].got]
-    for name in sums:
-        pieces += [jobs[name].value, jobs[name].got]
-
-    def finish(*refs):
-        sw, tw, down, up = refs[len(pieces) :]
-        for i in range(len(names)):
-            value = refs[2 * i][0].astype(F32) + refs[2 * i + 1][0].astype(F32)
-            if i < 3:
-                sw[i + 1] = value
-            else:
-                tw[i - 3] = value
-        flush(tw)
-        flush(sw)
-        for i in range(len(sums)):
-            first, second = refs[2 * (len(names) + i)], refs[2 * (len(names) + i) + 1]
-            value = first[...].astype(F32) + second[...].astype(F32)
-            (up if i < layers else down)[i % layers] = value
-
-    sw, tw, down, up = run(
-        finish,
-        pieces,
-        [
-            shape_of((2 * layers, 9, share, 128)),
-            shape_of((tasks * layers, 9, share, 128)),
-            shape_of((layers, tasks, 128, 128)),
-            shape_of((layers, tasks, 128, 128)),
-        ],
-        name="finish",
-        away=range(4),
-    )
-    tw, down, up = tw.home, down.home, up.home
-
-    def put_body(buffer, stay, got, turn, out, total, sem):
-        total[...] = stay[0].astype(F32) + got[0].astype(F32)
-        copy = pltpu.make_async_copy(total, out.at[0], sem)
-        copy.start()
-        copy.wait()
-
-    job = jobs["a_0"]
-    hbm, vmem = pl.BlockSpec(memory_space=pltpu.HBM), pl.BlockSpec(memory_space=pltpu.VMEM)
-    sw = pl.pallas_call(
-        put_body,
-        out_shape=pltpu.HBM(sw.shape, F32),
-        in_specs=[hbm, vmem, vmem, vmem],
-        out_specs=hbm,
-        input_output_aliases={0: 0},
-        scratch_shapes=[pltpu.VMEM((9, share, 128), F32), pltpu.SemaphoreType.DMA],
-        compiler_params=pltpu.CompilerParams(vmem_limit_bytes=VMEM_LIMIT),
-        name="put",
-    )(pltpu.with_memory_space_constraint(sw.home, pltpu.HBM), job.stay.home, job.got, TURN.pop())
+    while any(jobs[name].step < len(rest) for name in every):
+        for name in every:
+            if jobs[name].step < len(rest):
+                gap([jobs[name].halve])
+    put_ready(every[:3])
+    flat = hold(flat, TURN[0])
+    put_ready(every)
+    flat = flat.reshape(layers, 2, tasks, 128, 128).astype(F32)
+    down, up = flat[:, 0], flat[:, 1]
+    (sw,) = buffers
     return (
         shared_out.reshape(1, widths[1] // 2, widths[1] // 2, 128),
         task_out.reshape(tasks, 1, widths[1] // 2, widths[1] // 2, 128),

time: 433 us -> 382 us (0.88); the launches traced: 425 us -> 380 us
  starting transfers between devices: 154 us -> 95.7 us
  blocking collectives: 0 us -> 18.8 us
  waiting for transfers between devices: 128 us -> 113 us
  between operations: 2.29 us -> 15 us
  Pallas kernels: 135 us -> 127 us
  local copies, waits for them, and re-layouts: 5.88 us -> 10.3 us
    ppermute x56 -> x7, starting transfers between devices: 83.4 us -> 6.94 us  [the longest x4 4.86 us: total_by_pairs(): lax.ppermute(rows, 'img', [(i, i ^ s) for i in range(images)])]
    all_to_all x0 -> x13, starting transfers between devices: none -> 53.8 us  [swap_img(): return lax.all_to_all(copies, 'img', 0, 0)]
    all_to_all x0 -> x13, waiting for transfers between devices: none -> 41.1 us  [swap_img(): return lax.all_to_all(copies, 'img', 0, 0)]
    ppermute x56 -> x7, waiting for transfers between devices: 40.1 us -> 5.19 us  [the longest x1 2.85 us: on_device(): parts = (part, lax.ppermute(near, 'ch', CHIP))]
    ppermute x48 -> x15, starting transfers between devices: 49 us -> 15.3 us  [send_img(): got = lax.ppermute(value, 'img', [(i, i ^ 1 << bit) for i in range(images)])]
    pallas_call x106 -> x68, Pallas kernels: 134 us -> 108 us  [run(): pl.pallas_call(kernel, out_shape=out_shape, in_specs=specs + [vmem] * len...]
    ppermute x48 -> x15, waiting for transfers between devices: 51.4 us -> 25.8 us  [send_img(): got = lax.ppermute(value, 'img', [(i, i ^ 1 << bit) for i in range(images)])]
    all_to_all x0 -> x2, blocking collectives: none -> 18.8 us  [swap_img(): return lax.all_to_all(copies, 'img', 0, 0)]
  transfers between devices with their start and end apart: 143 -> 72, of which waited for: 61 -> 39; matrix products, arithmetic and copies ran while one was open for 1% -> 2% of each run, Pallas kernels for 24% -> 28%
where the time goes in v2:
time: 382 us; the launch traced here: 380 us
  Pallas kernels  127 us (33%)
  waiting for transfers between devices  113 us (30%)
  starting transfers between devices  95.7 us (25%)
  blocking collectives  18.8 us (5%)
  between operations  15 us (4%)
  local copies, waits for them, and re-layouts  10.3 us (3%)
    pallas_call x68, Pallas kernels, run(): pl.pallas_call(kernel, out_shape=out_shape, in_specs=specs + [vmem] * len...  108 us
    all_to_all x13, starting transfers between devices, swap_img(): return lax.all_to_all(copies, 'img', 0, 0)  53.8 us
    all_to_all x13, waiting for transfers between devices, swap_img(): return lax.all_to_all(copies, 'img', 0, 0)  41.1 us
    ppermute x15, waiting for transfers between devices, send_img(): got = lax.ppermute(value, 'img', [(i, i ^ 1 << bit) for i in range(images)])  25.8 us
    all_to_all x2, blocking collectives, swap_img(): return lax.all_to_all(copies, 'img', 0, 0)  18.8 us
    ppermute x15, starting transfers between devices, send_img(): got = lax.ppermute(value, 'img', [(i, i ^ 1 << bit) for i in range(images)])  15.3 us
    ppermute x7, waiting for transfers between devices, near_and_far(): far = lax.ppermute(value, 'ch', CHIP)  13.8 us
    pallas_call x9, Pallas kernels, bring(): pl.pallas_call(body, out_shape=[pltpu.VMEM(v.shape, v.dtype) for v in ite...  11.6 us
  transfers between devices with their start and end apart: 72, of which 39 were waited for; matrix products, arithmetic and copies ran while one was open for 2% of the time, Pallas kernels for 28%

profile of v2, /device:TPU:0, one launch (start us, length us, event | category | flops | bytes accessed | tf_op | source)
XLA Modules:
  0.0 379.9 jit_solution(12974679256606812587)
XLA Ops:
  20.6 5.8 %all-to-all-start = ((f32[8,2,128]{2,1,0:T(2,128)}), f32[8,2,128]{2,1,0:T(2,128)S(1)}, u32[]{:S(2)}, u32[]{:S(2)}) async-start(f32[8,2,128]{2,1,0:T(2,128)} %get-tuple-element.329), calls=%async_computation | async-start | bytes 16384 | tf_op jit(solution)/shard_map/all_to_all | solution.py:841
  40.3 4.0 %conv2_0.1 = (bf16[576,512]{1,0:T(8,128)(2,1)}, f32[576,128]{1,0:T(8,128)S(1)}, f32[3,576,128]{2,1,0:T(8,128)S(1)}, f32[8,8,128]{2,1,0:T(8,128)}, f32[8,128]{1,0...) custom-call(s32[1]{0:T(128)} %bitcast.refs_0_, bf16[576,128]{1,0:T(8,128)(2,1)S(1)} %get-tuple-element.338.refs_1_, ...), custom_call_target="tpu_custom_call" | custom-call | bytes 1 | tf_op jit(solution)/shard_map/conv2_0/pallas_call | solution.py:750
  44.3 4.5 %all-to-all-start.1 = ((f32[8,8,128]{2,1,0:T(8,128)}), f32[8,8,128]{2,1,0:T(8,128)S(1)}, u32[]{:S(2)}, u32[]{:S(2)}) async-start(f32[8,8,128]{2,1,0:T(8,128)} %get-tuple-element.353), calls=%async_computation.1 | async-start | bytes 65536 | tf_op jit(solution)/shard_map/all_to_all | solution.py:841
  51.2 4.3 %all-to-all-done.1.refs_0_ = f32[8,8,128]{2,1,0:T(8,128)S(1)} async-done(((f32[8,8,128]{2,1,0:T(8,128)}), f32[8,8,128]{2,1,0:T(8,128)S(1)}, u32[]{:S(2)}, u32[]{:S(2)}) %all-to-all-start.1) | async-done | bytes 32800 | tf_op jit(solution)/shard_map/all_to_all | solution.py:841
  69.2 5.2 %taskconv_0.1 = (bf16[3,576,512]{2,1,0:T(8,128)(2,1)}, f32[3,576,128]{2,1,0:T(8,128)S(1)}, f32[8,8,128]{2,1,0:T(8,128)}, f32[8,128]{1,0:T(8,128)S(1)}, bf16[3,576,128]{2,1,0:T(8,128)(2,1)}, /*index=5*/f32[6,512]{1,0:T(8,128)}) custom-call(s32[1]{0:T(128)} %bitcast.refs_0_, bf16[3,576,128]{2,1,0:T(8,128)(2,1)S(1)} %get-tuple-element.363.refs_1_, ...), custom_call_target="tpu_custom_call" | custom-call | bytes 1 | tf_op jit(solution)/shard_map/taskconv_0/pallas_call | solution.py:750
  80.0 4.5 %all-to-all-done.2.refs_0_ = f32[8,8,128]{2,1,0:T(8,128)S(1)} async-done(((f32[8,8,128]{2,1,0:T(8,128)}), f32[8,8,128]{2,1,0:T(8,128)S(1)}, u32[]{:S(2)}, u32[]{:S(2)}) %all-to-all-start.2) | async-done | bytes 32800 | tf_op jit(solution)/shard_map/all_to_all | solution.py:841
  101.4 5.4 %all-to-all-done.3.refs_0_ = f32[8,8,128]{2,1,0:T(8,128)S(1)} async-done(((f32[8,8,128]{2,1,0:T(8,128)}), f32[8,8,128]{2,1,0:T(8,128)S(1)}, u32[]{:S(2)}, u32[]{:S(2)}) %all-to-all-start.3) | async-done | bytes 32800 | tf_op jit(solution)/shard_map/all_to_all | solution.py:841
  112.9 6.1 %all-to-all-done.4.refs_0_ = f32[8,6,512]{2,1,0:T(8,128)S(1)} async-done(((f32[8,6,512]{2,1,0:T(8,128)}), f32[8,6,512]{2,1,0:T(8,128)S(1)}, u32[]{:S(2)}, u32[]{:S(2)}) %all-to-all-start.4) | async-done | bytes 98336 | tf_op jit(solution)/shard_map/all_to_all | solution.py:841
  128.0 9.7 %all_to_all.75.refs_0_ = f32[8,6,128]{2,1,0:T(8,128)S(1)} all-to-all(f32[8,6,128]{2,1,0:T(8,128)S(1)} %get-tuple-element.425), channel_id=1, replica_groups=mesh['img'=8,'ch'=4] {'img'}, dimensions={0} | all-to-all | bytes 49152 | tf_op jit(solution)/shard_map/all_to_all | solution.py:841
  138.8 9.1 %all_to_all.76.refs_0_ = f32[8,6,128]{2,1,0:T(8,128)S(1)} all-to-all(f32[8,6,128]{2,1,0:T(8,128)S(1)} %get-tuple-element.434), channel_id=1, replica_groups=mesh['img'=8,'ch'=4] {'img'}, dimensions={0} | all-to-all | bytes 49152 | tf_op jit(solution)/shard_map/all_to_all | solution.py:841
  147.9 4.0 %taskback_1.1 = (bf16[3,144,128]{2,1,0:T(8,128)(2,1)}, bf16[2,3,144,128]{3,2,1,0:T(8,128)(2,1)S(1)}, f32[3,144,128]{2,1,0:T(8,128)S(1)}, f32[3,144,128]{2,1,0:T(...) custom-call(s32[1]{0:T(128)} %bitcast.refs_0_, f32[3,144,128]{2,1,0:T(8,128)S(1)} %get-tuple-element.431.refs_1_, ...), custom_call_target="tpu_custom_call" | custom-call | bytes 1 | tf_op jit(solution)/shard_map/taskback_1/pallas_call | solution.py:750
  154.1 4.6 %collective-permute-done.31.refs_2_ = bf16[3,144,128]{2,1,0:T(8,128)(2,1)S(1)} collective-permute-done((bf16[3,144,128]{2,1,0:T(8,128)(2,1)S(1)}, bf16[3,144,128]{2,1,0:T(8,128)(2,1)S(1)}, u32[]{:S(2)}, u32[]{:S(2)}) %collective-permute-start.31) | collective-permute-done | bytes 110624 | tf_op jit(solution)/shard_map/ppermute | solution.py:1321
  164.2 4.6 %weight_1.1 = (bf16[3,9,512,128]{3,2,1,0:T(8,128)(2,1)}, f32[8,128]{1,0:T(8,128)S(1)}) custom-call(bf16[3,144,512]{2,1,0:T(8,128)(2,1)} %get-tuple-element.451.refs_0_, bf16[3,144,128]{2,1,0:T(8,128)(2,1)} %get-tuple-element.452.refs_1_, f32[8,128]{1,0:T(8,128)S(1)} %get-tuple-element.453.refs_2_), custom_call_target="tpu_custom_call" | custom-call | bytes 1 | tf_op jit(solution)/shard_map/weight_1/pallas_call | solution.py:750
  183.1 5.0 %all-to-all-start.8 = ((f32[8,6,128]{2,1,0:T(8,128)}), f32[8,6,128]{2,1,0:T(8,128)S(1)}, u32[]{:S(2)}, u32[]{:S(2)}) async-start(f32[8,6,128]{2,1,0:T(8,128)} %get-tuple-element.479), calls=%async_computation.8 | async-start | bytes 65536 | tf_op jit(solution)/shard_map/all_to_all | solution.py:841
  189.6 5.9 %all-to-all-done.8.refs_0_ = f32[8,6,128]{2,1,0:T(8,128)S(1)} async-done(((f32[8,6,128]{2,1,0:T(8,128)}), f32[8,6,128]{2,1,0:T(8,128)S(1)}, u32[]{:S(2)}, u32[]{:S(2)}) %all-to-all-start.8) | async-done | bytes 24608 | tf_op jit(solution)/shard_map/all_to_all | solution.py:841
  205.0 4.8 %all-to-all-done.9.refs_0_ = f32[8,8,128]{2,1,0:T(8,128)S(1)} async-done(((f32[8,8,128]{2,1,0:T(8,128)}), f32[8,8,128]{2,1,0:T(8,128)S(1)}, u32[]{:S(2)}, u32[]{:S(2)}) %all-to-all-start.9) | async-done | bytes 32800 | tf_op jit(solution)/shard_map/all_to_all | solution.py:841
  211.9 5.8 %taskback_0.1 = (bf16[3,576,128]{2,1,0:T(8,128)(2,1)}, bf16[2,3,576,128]{3,2,1,0:T(8,128)(2,1)S(1)}, f32[3,576,128]{2,1,0:T(8,128)S(1)}, f32[3,576,128]{2,1,0:T(8,128)S(1)}, f32[8,128]{1,0:T(8,128)S(1)}) custom-call(s32[1]{0:T(128)} %bitcast.refs_0_, f32[3,576,128]{2,1,0:T(8,128)S(1)} %get-tuple-element.488.refs_1_, ...), custom_call_target="tpu_custom_call" | custom-call | bytes 1 | tf_op jit(solution)/shard_map/taskback_0/pallas_call | solution.py:750
  223.3 7.4 %weight_0.1 = (bf16[3,9,512,128]{3,2,1,0:T(8,128)(2,1)}, f32[8,128]{1,0:T(8,128)S(1)}) custom-call(bf16[3,576,512]{2,1,0:T(8,128)(2,1)} %get-tuple-element.511.refs_0_, bf16[3,576,128]{2,1,0:T(8,128)(2,1)} %get-tuple-element.512.refs_1_, f32[8,128]{1,0:T(8,128)S(1)} %get-tuple-element.513.refs_2_), custom_call_target="tpu_custom_call" | custom-call | bytes 1 | tf_op jit(solution)/shard_map/weight_0/pallas_call | solution.py:750
  257.7 4.9 %collective-permute-done.43.refs_1_ = bf16[3,576,128]{2,1,0:T(8,128)(2,1)S(1)} collective-permute-done((bf16[3,576,128]{2,1,0:T(8,128)(2,1)S(1)}, bf16[3,576,128]{2,1,0:T(8,128)(2,1)S(1)}, u32[]{:S(2)}, u32[]{:S(2)}) %collective-permute-start.43) | collective-permute-done | bytes 442400 | tf_op jit(solution)/shard_map/ppermute | solution.py:1417
  288.8 4.8 %all-to-all-start.12 = ((f32[8,2,128]{2,1,0:T(2,128)}), f32[8,2,128]{2,1,0:T(2,128)S(1)}, u32[]{:S(2)}, u32[]{:S(2)}) async-start(f32[8,2,128]{2,1,0:T(2,128)} %get-tuple-element.583), calls=%async_computation.12 | async-start | bytes 16384 | tf_op jit(solution)/shard_map/all_to_all | solution.py:841
  301.6 6.0 %all-to-all-start.13 = ((bf16[8,192,128]{2,1,0:T(8,128)(2,1)}), bf16[8,192,128]{2,1,0:T(8,128)(2,1)S(1)}, u32[]{:S(2)}, u32[]{:S(2)}) async-start(bf16[8,192,128]{2,1,0:T(8,128)(2,1)} %get-tuple-element.621), calls=%async_computation.15 | async-start | bytes 786432 | tf_op jit(solution)/shard_map/all_to_all | solution.py:841
  318.1 4.7 %collective-permute-done.53.refs_2_ = bf16[1,1,9,64,128]{4,3,2,1,0:T(8,128)(2,1)S(1)} collective-permute-done((bf16[1,1,9,64,128]{4,3,2,1,0:T(8,128)(2,1)S(1)}, bf16[1,1,9,64,128]{4,3,2,1,0:T(8,128)(2,1)S(1)}, u32[]{:S(2)}, u32[]{:S(2)}) %collective-permute-start.53) | collective-permute-done | bytes 147488 | tf_op jit(solution)/shard_map/ppermute | solution.py:949
  339.5 4.0 %all-to-all-start.14 = ((bf16[8,192,128]{2,1,0:T(8,128)(2,1)}), bf16[8,192,128]{2,1,0:T(8,128)(2,1)S(1)}, u32[]{:S(2)}, u32[]{:S(2)}) async-start(bf16[8,192,128]{2,1,0:T(8,128)(2,1)} %get-tuple-element.635), calls=%async_computation.16 | async-start | bytes 786432 | tf_op jit(solution)/shard_map/all_to_all | solution.py:841
  350.9 14.7 %collective-permute-done.54.refs_2_ = bf16[1,1,9,64,128]{4,3,2,1,0:T(8,128)(2,1)S(1)} collective-permute-done((bf16[1,1,9,64,128]{4,3,2,1,0:T(8,128)(2,1)S(1)}, bf16[1,1,9,64,128]{4,3,2,1,0:T(8,128)(2,1)S(1)}, u32[]{:S(2)}, u32[]{:S(2)}) %collective-permute-start.54) | collective-permute-done | bytes 147488 | tf_op jit(solution)/shard_map/ppermute | solution.py:949
  (251 shorter events, 225.0 us)
Async XLA Ops:
  18.8 15.6 %collective-permute-start.7 = (bf16[2,2,3,128,128]{4,3,2,1,0:T(8,128)(2,1)S(1)}, bf16[2,2,3,128,128]{4,3,2,1,0:T(8,128)(2,1)S(1)}, u32[]{:S(2)}, u32[]{:S(2)}) collective-permute-start(bf16[2,2,3,128,128]{4,3,2,1,0:T(8,128)(2,1)S(1)} %get-tuple-element.340.refs_1_), channel_id=1, source_target_pairs={{0,2},{2,0},{1,3},{3,1},{4,6},{6,4},{5,7},{7,5},{8,10},{10,8},{9,1... | collective-permute-start | bytes 1179656 | tf_op jit(solution)/shard_map/ppermute | solution.py:821
  20.6 12.4 %all-to-all-start = ((f32[8,2,128]{2,1,0:T(2,128)}), f32[8,2,128]{2,1,0:T(2,128)S(1)}, u32[]{:S(2)}, u32[]{:S(2)}) async-start(f32[8,2,128]{2,1,0:T(2,128)} %get-tuple-element.329), calls=%async_computation | async-start | bytes 16384 | tf_op jit(solution)/shard_map/all_to_all | solution.py:841
  27.0 12.0 %collective-permute-start.6 = (bf16[2,2,3,128,128]{4,3,2,1,0:T(8,128)(2,1)S(1)}, bf16[2,2,3,128,128]{4,3,2,1,0:T(8,128)(2,1)S(1)}, u32[]{:S(2)}, u32[]{:S(2)}) collective-permute-start(bf16[2,2,3,128,128]{4,3,2,1,0:T(8,128)(2,1)S(1)} %get-tuple-element.340.refs_1_), channel_id=1, source_target_pairs={{0,1},{1,0},{2,3},{3,2},{4,5},{5,4},{6,7},{7,6},{8,9},{9,8},{10,11... | collective-permute-start | bytes 1179656 | tf_op jit(solution)/shard_map/ppermute | solution.py:822
  44.3 11.2 %all-to-all-start.1 = ((f32[8,8,128]{2,1,0:T(8,128)}), f32[8,8,128]{2,1,0:T(8,128)S(1)}, u32[]{:S(2)}, u32[]{:S(2)}) async-start(f32[8,8,128]{2,1,0:T(8,128)} %get-tuple-element.353), calls=%async_computation.1 | async-start | bytes 65536 | tf_op jit(solution)/shard_map/all_to_all | solution.py:841
  84.4 12.4 %collective-permute-start.25 = (bf16[1,2,576,128]{3,2,1,0:T(8,128)(2,1)S(1)}, bf16[1,2,576,128]{3,2,1,0:T(8,128)(2,1)S(1)}, u32[]{:S(2)}, u32[]{:S(2)}) collective-permute-start(bf16[1,2,576,128]{3,2,1,0:T(8,128)(2,1)S(1)} %get-tuple-element.400), channel_id=1, source_target_pairs={{0,8},{4,12},{8,0},{12,4},{16,24},{20,28},{24,16},{28,20},{1,9},{5... | collective-permute-start | bytes 884744 | tf_op jit(solution)/shard_map/ppermute | solution.py:949
  108.3 10.7 %all-to-all-start.4 = ((f32[8,6,512]{2,1,0:T(8,128)}), f32[8,6,512]{2,1,0:T(8,128)S(1)}, u32[]{:S(2)}, u32[]{:S(2)}) async-start(f32[8,6,512]{2,1,0:T(8,128)} %get-tuple-element.418), calls=%async_computation.4 | async-start | bytes 262144 | tf_op jit(solution)/shard_map/all_to_all | solution.py:841
  164.1 183.6 %reduce-scatter.5.cloned.1.call-start = ((), (), s32[]{:S(2)}) async-start(), calls=%async_computation.18 | async-start | bytes 3981312 | tf_op jit(solution)/shard_map/reduce_scatter | solution.py:1096
  183.1 12.4 %all-to-all-start.8 = ((f32[8,6,128]{2,1,0:T(8,128)}), f32[8,6,128]{2,1,0:T(8,128)S(1)}, u32[]{:S(2)}, u32[]{:S(2)}) async-start(f32[8,6,128]{2,1,0:T(8,128)} %get-tuple-element.479), calls=%async_computation.8 | async-start | bytes 65536 | tf_op jit(solution)/shard_map/all_to_all | solution.py:841
  220.5 13.1 %collective-permute-start.39 = (bf16[1872,128]{1,0:T(8,128)(2,1)S(1)}, bf16[1872,128]{1,0:T(8,128)(2,1)S(1)}, u32[]{:S(2)}, u32[]{:S(2)}) collective-permute-start(bf16[1872,128]{1,0:T(8,128)(2,1)S(1)} %get-tuple-element.505), channel_id=1, source_target_pairs={{0,2},{2,0},{1,3},{3,1},{4,6},{6,4},{5,7},{7,5},{8,10},{10,8},{9,1... | collective-permute-start | bytes 1437704 | tf_op jit(solution)/shard_map/ppermute | solution.py:1387
  222.0 14.4 %collective-permute-start.40 = (bf16[2,1,9,64,128]{4,3,2,1,0:T(8,128)(2,1)S(1)}, bf16[2,1,9,64,128]{4,3,2,1,0:T(8,128)(2,1)S(1)}, u32[]{:S(2)}, u32[]{:S(2)}) collective-permute-start(bf16[2,1,9,64,128]{4,3,2,1,0:T(8,128)(2,1)S(1)} %get-tuple-element.518), channel_id=1, source_target_pairs={{0,4},{4,0},{8,12},{12,8},{16,20},{20,16},{24,28},{28,24},{1,5},{5... | collective-permute-start | bytes 884744 | tf_op jit(solution)/shard_map/ppermute | solution.py:949
  222.7 13.7 %collective-permute-start.41 = (bf16[144,128]{1,0:T(8,128)(2,1)S(1)}, bf16[144,128]{1,0:T(8,128)(2,1)S(1)}, u32[]{:S(2)}, u32[]{:S(2)}) collective-permute-start(bf16[144,128]{1,0:T(8,128)(2,1)S(1)} %copy-done.8), channel_id=1, source_target_pairs={{0,8},{4,12},{8,0},{12,4},{16,24},{20,28},{24,16},{28,20},{1,9},{5... | collective-permute-start | bytes 110600 | tf_op jit(solution)/shard_map/ppermute | solution.py:949
  239.8 107.9 %reduce-scatter.3.cloned.1.call-start = ((), (), s32[]{:S(2)}) async-start(), calls=%async_computation.17 | async-start | bytes 3981312 | tf_op jit(solution)/shard_map/reduce_scatter | solution.py:1096
  250.3 12.3 %collective-permute-start.43 = (bf16[3,576,128]{2,1,0:T(8,128)(2,1)S(1)}, bf16[3,576,128]{2,1,0:T(8,128)(2,1)S(1)}, u32[]{:S(2)}, u32[]{:S(2)}) collective-permute-start(bf16[3,576,128]{2,1,0:T(8,128)(2,1)S(1)} %get-tuple-element.534.refs_0_), channel_id=1, source_target_pairs={{0,2},{2,0},{1,3},{3,1},{4,6},{6,4},{5,7},{7,5},{8,10},{10,8},{9,1... | collective-permute-start | bytes 1327112 | tf_op jit(solution)/shard_map/ppermute | solution.py:1417
  254.7 10.6 %collective-permute-start.45 = (bf16[1,1,9,64,128]{4,3,2,1,0:T(8,128)(2,1)S(1)}, bf16[1,1,9,64,128]{4,3,2,1,0:T(8,128)(2,1)S(1)}, u32[]{:S(2)}, u32[]{:S(2)}) collective-permute-start(bf16[1,1,9,64,128]{4,3,2,1,0:T(8,128)(2,1)S(1)} %get-tuple-element.554), channel_id=1, source_target_pairs={{0,16},{4,20},{8,24},{12,28},{16,0},{20,4},{24,8},{28,12},{1,17},{... | collective-permute-start | bytes 442376 | tf_op jit(solution)/shard_map/ppermute | solution.py:949
  255.2 10.8 %collective-permute-start.46 = (bf16[576,128]{1,0:T(8,128)(2,1)}, bf16[576,128]{1,0:T(8,128)(2,1)S(1)}, u32[]{:S(2)}, u32[]{:S(2)}) collective-permute-start(bf16[576,128]{1,0:T(8,128)(2,1)} %get-tuple-element.555), channel_id=1, source_target_pairs={{0,8},{4,12},{8,0},{12,4},{16,24},{20,28},{24,16},{28,20},{1,9},{5... | collective-permute-start | bytes 442376 | tf_op jit(solution)/shard_map/ppermute | solution.py:949
  277.2 11.6 %collective-permute-start.48 = (bf16[2,1,9,64,128]{4,3,2,1,0:T(8,128)(2,1)}, bf16[2,1,9,64,128]{4,3,2,1,0:T(8,128)(2,1)S(1)}, u32[]{:S(2)}, u32[]{:S(2)}) collective-permute-start(bf16[2,1,9,64,128]{4,3,2,1,0:T(8,128)(2,1)} %copy-done.6), channel_id=1, source_target_pairs={{0,4},{4,0},{8,12},{12,8},{16,20},{20,16},{24,28},{28,24},{1,5},{5... | collective-permute-start | bytes 884744 | tf_op jit(solution)/shard_map/ppermute | solution.py:949
  288.8 12.8 %all-to-all-start.12 = ((f32[8,2,128]{2,1,0:T(2,128)}), f32[8,2,128]{2,1,0:T(2,128)S(1)}, u32[]{:S(2)}, u32[]{:S(2)}) async-start(f32[8,2,128]{2,1,0:T(2,128)} %get-tuple-element.583), calls=%async_computation.12 | async-start | bytes 16384 | tf_op jit(solution)/shard_map/all_to_all | solution.py:841
  301.6 37.1 %all-to-all-start.13 = ((bf16[8,192,128]{2,1,0:T(8,128)(2,1)}), bf16[8,192,128]{2,1,0:T(8,128)(2,1)S(1)}, u32[]{:S(2)}, u32[]{:S(2)}) async-start(bf16[8,192,128]{2,1,0:T(8,128)(2,1)} %get-tuple-element.621), calls=%async_computation.15 | async-start | bytes 786432 | tf_op jit(solution)/shard_map/all_to_all | solution.py:841
  310.4 12.4 %collective-permute-start.53 = (bf16[1,1,9,64,128]{4,3,2,1,0:T(8,128)(2,1)S(1)}, bf16[1,1,9,64,128]{4,3,2,1,0:T(8,128)(2,1)S(1)}, u32[]{:S(2)}, u32[]{:S(2)}) collective-permute-start(bf16[1,1,9,64,128]{4,3,2,1,0:T(8,128)(2,1)S(1)} %get-tuple-element.604), channel_id=1, source_target_pairs={{0,16},{4,20},{8,24},{12,28},{16,0},{20,4},{24,8},{28,12},{1,17},{... | collective-permute-start | bytes 442376 | tf_op jit(solution)/shard_map/ppermute | solution.py:949
  313.4 11.2 %collective-permute-start.52 = (bf16[576,128]{1,0:T(8,128)(2,1)}, bf16[576,128]{1,0:T(8,128)(2,1)S(1)}, u32[]{:S(2)}, u32[]{:S(2)}) collective-permute-start(bf16[576,128]{1,0:T(8,128)(2,1)} %get-tuple-element.598), channel_id=1, source_target_pairs={{0,8},{4,12},{8,0},{12,4},{16,24},{20,28},{24,16},{28,20},{1,9},{5... | collective-permute-start | bytes 442376 | tf_op jit(solution)/shard_map/ppermute | solution.py:949
  314.9 16.1 %collective-permute-start.51 = (bf16[2,1,9,64,128]{4,3,2,1,0:T(8,128)(2,1)S(1)}, bf16[2,1,9,64,128]{4,3,2,1,0:T(8,128)(2,1)S(1)}, u32[]{:S(2)}, u32[]{:S(2)}) collective-permute-start(bf16[2,1,9,64,128]{4,3,2,1,0:T(8,128)(2,1)S(1)} %get-tuple-element.597), channel_id=1, source_target_pairs={{0,4},{4,0},{8,12},{12,8},{16,20},{20,16},{24,28},{28,24},{1,5},{5... | collective-permute-start | bytes 884744 | tf_op jit(solution)/shard_map/ppermute | solution.py:949
  339.5 27.9 %all-to-all-start.14 = ((bf16[8,192,128]{2,1,0:T(8,128)(2,1)}), bf16[8,192,128]{2,1,0:T(8,128)(2,1)S(1)}, u32[]{:S(2)}, u32[]{:S(2)}) async-start(bf16[8,192,128]{2,1,0:T(8,128)(2,1)} %get-tuple-element.635), calls=%async_computation.16 | async-start | bytes 786432 | tf_op jit(solution)/shard_map/all_to_all | solution.py:841
  343.5 22.2 %collective-permute-start.54 = (bf16[1,1,9,64,128]{4,3,2,1,0:T(8,128)(2,1)S(1)}, bf16[1,1,9,64,128]{4,3,2,1,0:T(8,128)(2,1)S(1)}, u32[]{:S(2)}, u32[]{:S(2)}) collective-permute-start(bf16[1,1,9,64,128]{4,3,2,1,0:T(8,128)(2,1)S(1)} %get-tuple-element.612), channel_id=1, source_target_pairs={{0,16},{4,20},{8,24},{12,28},{16,0},{20,4},{24,8},{28,12},{1,17},{... | collective-permute-start | bytes 442376 | tf_op jit(solution)/shard_map/ppermute | solution.py:949
  347.7 23.1 %collective-permute-start.56 = (bf16[1,1,9,64,128]{4,3,2,1,0:T(8,128)(2,1)S(1)}, bf16[1,1,9,64,128]{4,3,2,1,0:T(8,128)(2,1)S(1)}, u32[]{:S(2)}, u32[]{:S(2)}) collective-permute-start(bf16[1,1,9,64,128]{4,3,2,1,0:T(8,128)(2,1)S(1)} %get-tuple-element.631), channel_id=1, source_target_pairs={{0,16},{4,20},{8,24},{12,28},{16,0},{20,4},{24,8},{28,12},{1,17},{... | collective-permute-start | bytes 442376 | tf_op jit(solution)/shard_map/ppermute | solution.py:949
  (63 other events, 371.1 us)
Sparse Core Ops, SparseCore 0:
  170.9 83.9 reduce-scatter.4
  258.6 81.7 reduce-scatter.2

commit v3 on v2

--- a/solution.py
+++ b/solution.py
@@ -547,8 +547,8 @@
     spread_stats(stats, rows)
 
 
-def attend_grad_body(l, count, rawrow, d, p, raw, draw, bgain, g, down, part, far, y, raw1, gain, shift, more, ddown, d1, stats, more_out):
-    upstream = part[...] + far[...].astype(F32)
+def attend_grad_body(l, count, rawrow, d, p, raw, draw, bgain, g, down, dv, y, raw1, gain, shift, more, ddown, d1, stats, more_out):
+    upstream = dv[...]
     dtotal = draw[...]
     rows = []
     for t in range(3):
@@ -573,13 +573,13 @@
     spread_stats(stats, [sums(grad), sums(grad * normal)] + rows)
 
 
-def attend_grad_last_body(l, count, rawrow, d, p, raw, draw, bgain, g, down, part, far, y, raw1, gain, shift, ddown, d1, stats):
-    attend_grad_body(l, count, rawrow, d, p, raw, draw, bgain, g, down, part, far, y, raw1, gain, shift, None, ddown, d1, stats, None)
-
-
-def attend_grad_first_body(l, count, rawrow, tcount, twidth, d, p, raw, draw, bgain, g, down, part, far, y, raw1, gain, shift, yt, traw, ddown, d1, stats, dt, scratch):
+def attend_grad_last_body(l, count, rawrow, d, p, raw, draw, bgain, g, down, dv, y, raw1, gain, shift, ddown, d1, stats):
+    attend_grad_body(l, count, rawrow, d, p, raw, draw, bgain, g, down, dv, y, raw1, gain, shift, None, ddown, d1, stats, None)
+
+
+def attend_grad_first_body(l, count, rawrow, tcount, twidth, d, p, raw, draw, bgain, g, down, dv, y, raw1, gain, shift, yt, traw, ddown, d1, stats, dt, scratch):
     more = (yt, traw, tcount, twidth, scratch)
-    attend_grad_body(l, count, rawrow, d, p, raw, draw, bgain, g, down, part, far, y, raw1, gain, shift, more, ddown, d1, stats, dt)
+    attend_grad_body(l, count, rawrow, d, p, raw, draw, bgain, g, down, dv, y, raw1, gain, shift, more, ddown, d1, stats, dt)
 
 
 def finish_body(order, refs_in, gain, shift, bgain, bshift):
@@ -945,18 +945,19 @@
             make(None)
         held[:] = waiting
 
-    def send_img(value, bit):
+    def send_img(value, bit, tie=True):
         got = lax.ppermute(value, "img", [(i, i ^ (1 << bit)) for i in range(images)])
-        pending.append(got)
+        if tie:
+            pending.append(got)
         return got
 
     bits = images.bit_length() - 1
     pair_bit = 7 - (share.bit_length() - 1)
     rest = [b for b in range(bits) if b != pair_bit]
 
-    def later(owner, field, value, bit):
+    def later(owner, field, value, bit, tie=True):
         def make(total):
-            setattr(owner, field, send_img(value if total is None else hold(value, total), bit))
+            setattr(owner, field, send_img(value if total is None else hold(value, total), bit, tie))
 
         held.append(make)
 
@@ -1023,7 +1024,7 @@
                 name=f"halve{self.name}_{self.step}",
                 away=(0,),
             )
-            later(self, "got", leave, rest[self.step])
+            later(self, "got", leave, rest[self.step], self.step + 1 < len(rest))
             self.step += 1
 
         def put(self):
@@ -1095,7 +1096,7 @@
             value = out.home if total is None else hold(out.home, total)
             k.task_w = lax.psum_scatter(value, "img", scatter_dimension=2, tiled=True)
 
-        held.append(make)
+        return make
 
     def meet(names, dys, wait=False):
         for t, name in enumerate(names):
@@ -1281,7 +1282,7 @@
     two.s, u, shared_out, zstats = hidden(1)
     u_blocks = near_and_far(u)
     taps = Taps(task_taps, tasks, tasks)
-    two.zraw = total_of(zstats, "totalz_1", [splits["b_1 a_1"].go], (u_blocks,))
+    two.zraw = total_of(zstats, "totalz_1", mid=(u_blocks,))
     two.k, two.yt, stats = task_convs(1, u_blocks, taps)
     two.traw = total_of(stats, "totalt_1")
 
@@ -1296,6 +1297,7 @@
     two.dtraw = total_of(
         stats,
         "dtotalt_1",
+        [splits["b_1 a_1"].go],
     )
     two.dtrow = 0
 
@@ -1330,6 +1332,11 @@
             if name
         ]
 
+    def put_ready(names):
+        for name in names:
+            if jobs[name].step == len(rest) and not jobs[name].placed:
+                jobs[name].put()
+
     flat = []
 
     def flatten():
@@ -1342,12 +1349,12 @@
         flat.append(swap_img(rows))
 
     plan = {
-        "gate_1": [functools.partial(task_weights, 1)],
+        "gate_1": (),
         "bottle_1": (),
         "first_1": steps("b_1"),
-        "gate_0": steps("", "b_1"),
-        "bottle_0": steps("a_1"),
-        "first_0": steps("b_0", "a_1") + [flatten],
+        "gate_0": steps("a_1", "b_1"),
+        "bottle_0": steps("", "a_1"),
+        "first_0": steps("b_0") + [lambda: put_ready(["b_1"]), flatten],
     }
     unfinished = None
 
@@ -1385,8 +1392,7 @@
                 name=f"pairr_{l}",
             )
             parts = (part, lax.ppermute(near, "ch", CHIP))
-        if l == 0:
-            task_weights(0)
+        make_weights = task_weights(l)
 
         def gate_grad(ch, part, far, s, up, zraw, y, raw, gain, shift, dx, *rest, first=unfinished, l=l, w=w):
             more = (dx,) if first is None else (dx, far)
@@ -1399,6 +1405,10 @@
             scratch=[pltpu.VMEM((n, 128), F32)],
             name=f"gategrad_{l}",
         )
+        if l == 0:
+            held.append(make_weights)
+        else:
+            make_weights(stats)
         k.draw2 = total_of(
             stats, f"dtotal2_{l}", plan[f"gate_{l}"], ahead=[k.s, up_w, k.zraw, params]
         )
@@ -1429,6 +1439,10 @@
         )
         meet([f"b_{l}"], dys)
         parts = scatter_ch(send, keep, far, f"pairv_{l}", (1,))
+
+        def make_dv(k=k, parts=parts, n=n, l=l):
+            k.dv = run(mixed_body, parts, [shape_of((n, 128))], name=f"dv_{l}")[0]
+
         gap(plan.get(f"hidden_{l}", ()))
         d, stats = run(
             functools.partial(bottle_grad_body, l, count),
@@ -1439,8 +1453,8 @@
         wanted = [k.p, k.raw2, bottles[0], k.g, down_w, k.y1, k.raw1, params]
         if l > 0:
             wanted += [kept[l - 1].yt, kept[l - 1].traw]
-        k.draw3 = total_of(stats, f"dtotal3_{l}", plan[f"bottle_{l}"], ahead=wanted if l == 0 else ())
-        args = (d, k.p, k.raw2, k.draw3, bottles[0], k.g, down_w, *parts, k.y1, k.raw1, *norms)
+        k.draw3 = total_of(stats, f"dtotal3_{l}", [make_dv, *plan[f"bottle_{l}"]])
+        args = (d, k.p, k.raw2, k.draw3, bottles[0], k.g, down_w, k.dv, k.y1, k.raw1, *norms)
         outs = [shape_of((tasks, 128, 128), LOW), shape_of((n, 128))]
         if l > 0:
             ddown, d1, stats, d = run(
@@ -1490,18 +1504,13 @@
     parts = scatter_ch(*unfinished, "pairx_0")
     every = ["b_1", "a_1", "b_0", "a_0"]
 
-    def put_ready(names):
-        for name in names:
-            if jobs[name].step == len(rest) and not jobs[name].placed:
-                jobs[name].put()
-
     put_ready(every[:2])
     gap(steps("a_0"))
     gap(steps("", "b_0"))
+    flat = run(spread_sum_body, flat, [shape_of(flat[0].shape, LOW)], name="spread")[0]
+    flat = swap_img(flat)
     dx = run(mixed_body, parts, [shape_of((n0, 128))], name="dx_0", away=(0,))[0].home
     gap(steps("", "a_0"))
-    flat = run(spread_sum_body, flat, [shape_of(flat[0].shape, LOW)], name="spread")[0]
-    flat = swap_img(flat)
     tw = run(
         widen_body,
         [Long(None, k.task_w) for k in kept],
@@ -1533,7 +1542,6 @@
         for name in every:
             if jobs[name].step < len(rest):
                 gap([jobs[name].halve])
-    put_ready(every[:3])
     flat = hold(flat, TURN[0])
     put_ready(every)
     flat = flat.reshape(layers, 2, tasks, 128, 128).astype(F32)

time: 382 us -> 369 us (0.966)
  blocking collectives: 18.8 us -> 10.3 us
  waiting for transfers between devices: 113 us -> 107 us
  local copies, waits for them, and re-layouts: 10.3 us -> 5.83 us
  starting transfers between devices: 95.7 us -> 99.9 us
    all_to_all x2 -> x1, blocking collectives: 18.8 us -> 10.3 us  [swap_img(): return lax.all_to_all(copies, 'img', 0, 0)]
    ppermute x4, waiting for transfers between devices: 10.5 us -> 3.5 us  [scatter_ch(): return (part, lax.ppermute(near, 'ch', CHIP))]
    all_to_all x13 -> x14, waiting for transfers between devices: 41.1 us -> 46.4 us  [swap_img(): return lax.all_to_all(copies, 'img', 0, 0)]
    unnamed x36 -> x20, local copies, waits for them, and re-layouts: 8.04 us -> 3.57 us
    ppermute x15, starting transfers between devices: 15.3 us -> 19.5 us  [send_img(): got = lax.ppermute(value, 'img', [(i, i ^ 1 << bit) for i in range(images)])]
    pallas_call x68 -> x71, Pallas kernels: 108 us -> 112 us  [run(): pl.pallas_call(kernel, out_shape=out_shape, in_specs=specs + [vmem] * len...]
    pallas_call x9 -> x8, Pallas kernels: 11.6 us -> 10 us  [bring(): pl.pallas_call(body, out_shape=[pltpu.VMEM(v.shape, v.dtype) for v in ite...]
    all_to_all x13 -> x14, starting transfers between devices: 53.8 us -> 54.8 us  [swap_img(): return lax.all_to_all(copies, 'img', 0, 0)]
  transfers between devices with their start and end apart: 72 -> 73, of which waited for: 39 -> 39; matrix products, arithmetic and copies ran while one was open for 2% -> 2% of each run, Pallas kernels for 28% -> 28%
where the time goes in v3:
time: 369 us; the launch traced here: 367 us
  Pallas kernels  129 us (35%)
  waiting for transfers between devices  107 us (29%)
  starting transfers between devices  99.9 us (27%)
  between operations  15 us (4%)
  blocking collectives  10.3 us (3%)
  local copies, waits for them, and re-layouts  5.83 us (2%)
    pallas_call x71, Pallas kernels, run(): pl.pallas_call(kernel, out_shape=out_shape, in_specs=specs + [vmem] * len...  112 us
    all_to_all x14, starting transfers between devices, swap_img(): return lax.all_to_all(copies, 'img', 0, 0)  54.8 us
    all_to_all x14, waiting for transfers between devices, swap_img(): return lax.all_to_all(copies, 'img', 0, 0)  46.4 us
    ppermute x15, waiting for transfers between devices, send_img(): got = lax.ppermute(value, 'img', [(i, i ^ 1 << bit) for i in range(images)])  24.1 us
    ppermute x15, starting transfers between devices, send_img(): got = lax.ppermute(value, 'img', [(i, i ^ 1 << bit) for i in range(images)])  19.5 us
    ppermute x7, waiting for transfers between devices, near_and_far(): far = lax.ppermute(value, 'ch', CHIP)  13.2 us
    all_to_all x1, blocking collectives, swap_img(): return lax.all_to_all(copies, 'img', 0, 0)  10.3 us
    pallas_call x8, Pallas kernels, bring(): pl.pallas_call(body, out_shape=[pltpu.VMEM(v.shape, v.dtype) for v in ite...  10 us
  transfers between devices with their start and end apart: 73, of which 39 were waited for; matrix products, arithmetic and copies ran while one was open for 2% of the time, Pallas kernels for 28%

profile of v3, /device:TPU:0, one launch (start us, length us, event | category | flops | bytes accessed | tf_op | source)
XLA Modules:
  0.0 366.9 jit_solution(14146847557106811145)
XLA Ops:
  20.6 5.8 %all-to-all-start = ((f32[8,2,128]{2,1,0:T(2,128)}), f32[8,2,128]{2,1,0:T(2,128)S(1)}, u32[]{:S(2)}, u32[]{:S(2)}) async-start(f32[8,2,128]{2,1,0:T(2,128)} %get-tuple-element.324), calls=%async_computation | async-start | bytes 16384 | tf_op jit(solution)/shard_map/all_to_all | solution.py:841
  40.3 4.0 %conv2_0.1 = (bf16[576,512]{1,0:T(8,128)(2,1)}, f32[576,128]{1,0:T(8,128)S(1)}, f32[3,576,128]{2,1,0:T(8,128)S(1)}, f32[8,8,128]{2,1,0:T(8,128)}, f32[8,128]{1,0...) custom-call(s32[1]{0:T(128)} %bitcast.refs_0_, bf16[576,128]{1,0:T(8,128)(2,1)S(1)} %get-tuple-element.333.refs_1_, ...), custom_call_target="tpu_custom_call" | custom-call | bytes 1 | tf_op jit(solution)/shard_map/conv2_0/pallas_call | solution.py:750
  44.3 4.5 %all-to-all-start.1 = ((f32[8,8,128]{2,1,0:T(8,128)}), f32[8,8,128]{2,1,0:T(8,128)S(1)}, u32[]{:S(2)}, u32[]{:S(2)}) async-start(f32[8,8,128]{2,1,0:T(8,128)} %get-tuple-element.348), calls=%async_computation.1 | async-start | bytes 65536 | tf_op jit(solution)/shard_map/all_to_all | solution.py:841
  51.2 4.3 %all-to-all-done.1.refs_0_ = f32[8,8,128]{2,1,0:T(8,128)S(1)} async-done(((f32[8,8,128]{2,1,0:T(8,128)}), f32[8,8,128]{2,1,0:T(8,128)S(1)}, u32[]{:S(2)}, u32[]{:S(2)}) %all-to-all-start.1) | async-done | bytes 32800 | tf_op jit(solution)/shard_map/all_to_all | solution.py:841
  69.2 5.2 %taskconv_0.1 = (bf16[3,576,512]{2,1,0:T(8,128)(2,1)}, f32[3,576,128]{2,1,0:T(8,128)S(1)}, f32[8,8,128]{2,1,0:T(8,128)}, f32[8,128]{1,0:T(8,128)S(1)}, bf16[3,576,128]{2,1,0:T(8,128)(2,1)}, /*index=5*/f32[6,512]{1,0:T(8,128)}) custom-call(s32[1]{0:T(128)} %bitcast.refs_0_, bf16[3,576,128]{2,1,0:T(8,128)(2,1)S(1)} %get-tuple-element.358.refs_1_, ...), custom_call_target="tpu_custom_call" | custom-call | bytes 1 | tf_op jit(solution)/shard_map/taskconv_0/pallas_call | solution.py:750
  80.0 4.5 %all-to-all-done.2.refs_0_ = f32[8,8,128]{2,1,0:T(8,128)S(1)} async-done(((f32[8,8,128]{2,1,0:T(8,128)}), f32[8,8,128]{2,1,0:T(8,128)S(1)}, u32[]{:S(2)}, u32[]{:S(2)}) %all-to-all-start.2) | async-done | bytes 32800 | tf_op jit(solution)/shard_map/all_to_all | solution.py:841
  89.4 3.9 %collective-permute-done.21.refs_3_ = bf16[144,128]{1,0:T(8,128)(2,1)S(1)} collective-permute-done((bf16[144,128]{1,0:T(8,128)(2,1)S(1)}, bf16[144,128]{1,0:T(8,128)(2,1)S(1)}, u32[]{:S(2)}, u32[]{:S(2)}) %collective-permute-start.21) | collective-permute-done | bytes 36896 | tf_op jit(solution)/shard_map/ppermute | solution.py:821
  101.4 5.4 %all-to-all-done.3.refs_0_ = f32[8,8,128]{2,1,0:T(8,128)S(1)} async-done(((f32[8,8,128]{2,1,0:T(8,128)}), f32[8,8,128]{2,1,0:T(8,128)S(1)}, u32[]{:S(2)}, u32[]{:S(2)}) %all-to-all-start.3) | async-done | bytes 32800 | tf_op jit(solution)/shard_map/all_to_all | solution.py:841
  122.6 10.3 %all_to_all.75.refs_0_ = f32[8,6,128]{2,1,0:T(8,128)S(1)} all-to-all(f32[8,6,128]{2,1,0:T(8,128)S(1)} %get-tuple-element.415), channel_id=1, replica_groups=mesh['img'=8,'ch'=4] {'img'}, dimensions={0} | all-to-all | bytes 49152 | tf_op jit(solution)/shard_map/all_to_all | solution.py:841
  139.1 5.6 %all-to-all-done.6.refs_0_ = f32[8,6,128]{2,1,0:T(8,128)S(1)} async-done(((f32[8,6,128]{2,1,0:T(8,128)}), f32[8,6,128]{2,1,0:T(8,128)S(1)}, u32[]{:S(2)}, u32[]{:S(2)}) %all-to-all-start.6) | async-done | bytes 24608 | tf_op jit(solution)/shard_map/all_to_all | solution.py:841
  144.6 4.0 %taskback_1.1 = (bf16[3,144,128]{2,1,0:T(8,128)(2,1)}, bf16[2,3,144,128]{3,2,1,0:T(8,128)(2,1)S(1)}, f32[3,144,128]{2,1,0:T(8,128)S(1)}, f32[3,144,128]{2,1,0:T(...) custom-call(s32[1]{0:T(128)} %bitcast.refs_0_, f32[3,144,128]{2,1,0:T(8,128)S(1)} %get-tuple-element.421.refs_1_, ...), custom_call_target="tpu_custom_call" | custom-call | bytes 1 | tf_op jit(solution)/shard_map/taskback_1/pallas_call | solution.py:750
  150.9 4.6 %weight_1.1 = (bf16[3,9,512,128]{3,2,1,0:T(8,128)(2,1)}, f32[8,128]{1,0:T(8,128)S(1)}) custom-call(bf16[3,144,512]{2,1,0:T(8,128)(2,1)} %get-tuple-element.442.refs_0_, bf16[3,144,128]{2,1,0:T(8,128)(2,1)} %get-tuple-element.443.refs_1_, f32[8,128]{1,0:T(8,128)S(1)} %get-tuple-element.444.refs_2_), custom_call_target="tpu_custom_call" | custom-call | bytes 1 | tf_op jit(solution)/shard_map/weight_1/pallas_call | solution.py:750
  158.1 5.2 %collective-permute-done.31.refs_2_ = bf16[2,2,144,128]{3,2,1,0:T(8,128)(2,1)S(1)} collective-permute-done((bf16[2,2,144,128]{3,2,1,0:T(8,128)(2,1)S(1)}, bf16[2,2,144,128]{3,2,1,0:T(8,128)(2,1)S(1)}, u32[]{:S(2)}, u32[]{:S(2)}) %collective-permute-start.31) | collective-permute-done | bytes 147488 | tf_op jit(solution)/shard_map/ppermute | solution.py:949
  167.7 6.2 %all-to-all-done.7.refs_0_ = f32[8,8,128]{2,1,0:T(8,128)S(1)} async-done(((f32[8,8,128]{2,1,0:T(8,128)}), f32[8,8,128]{2,1,0:T(8,128)S(1)}, u32[]{:S(2)}, u32[]{:S(2)}) %all-to-all-start.7) | async-done | bytes 32800 | tf_op jit(solution)/shard_map/all_to_all | solution.py:841
  200.6 3.8 %all-to-all-start.9 = ((f32[8,8,128]{2,1,0:T(8,128)}), f32[8,8,128]{2,1,0:T(8,128)S(1)}, u32[]{:S(2)}, u32[]{:S(2)}) async-start(f32[8,8,128]{2,1,0:T(8,128)} %get-tuple-element.488), calls=%async_computation.9 | async-start | bytes 65536 | tf_op jit(solution)/shard_map/all_to_all | solution.py:841
  206.8 4.3 %all-to-all-done.9.refs_0_ = f32[8,8,128]{2,1,0:T(8,128)S(1)} async-done(((f32[8,8,128]{2,1,0:T(8,128)}), f32[8,8,128]{2,1,0:T(8,128)S(1)}, u32[]{:S(2)}, u32[]{:S(2)}) %all-to-all-start.9) | async-done | bytes 32800 | tf_op jit(solution)/shard_map/all_to_all | solution.py:841
  213.1 5.8 %taskback_0.1 = (bf16[3,576,128]{2,1,0:T(8,128)(2,1)}, bf16[2,3,576,128]{3,2,1,0:T(8,128)(2,1)S(1)}, f32[3,576,128]{2,1,0:T(8,128)S(1)}, f32[3,576,128]{2,1,0:T(8,128)S(1)}, f32[8,128]{1,0:T(8,128)S(1)}) custom-call(s32[1]{0:T(128)} %bitcast.refs_0_, f32[3,576,128]{2,1,0:T(8,128)S(1)} %get-tuple-element.486.refs_1_, ...), custom_call_target="tpu_custom_call" | custom-call | bytes 1 | tf_op jit(solution)/shard_map/taskback_0/pallas_call | solution.py:750
  223.6 7.4 %weight_0.1 = (bf16[3,9,512,128]{3,2,1,0:T(8,128)(2,1)}, f32[8,128]{1,0:T(8,128)S(1)}) custom-call(bf16[3,576,512]{2,1,0:T(8,128)(2,1)} %get-tuple-element.509.refs_0_, bf16[3,576,128]{2,1,0:T(8,128)(2,1)} %get-tuple-element.510.refs_1_, f32[8,128]{1,0:T(8,128)S(1)} %get-tuple-element.511.refs_2_), custom_call_target="tpu_custom_call" | custom-call | bytes 1 | tf_op jit(solution)/shard_map/weight_0/pallas_call | solution.py:750
  231.0 3.9 %collective-permute-done.39.refs_2_ = bf16[1872,128]{1,0:T(8,128)(2,1)S(1)} collective-permute-done((bf16[1872,128]{1,0:T(8,128)(2,1)S(1)}, bf16[1872,128]{1,0:T(8,128)(2,1)S(1)}, u32[]{:S(2)}, u32[]{:S(2)}) %collective-permute-start.39) | collective-permute-done | bytes 479264 | tf_op jit(solution)/shard_map/ppermute | solution.py:1394
  267.1 3.7 %collective-permute-done.46.refs_4_ = bf16[576,128]{1,0:T(8,128)(2,1)S(1)} collective-permute-done((bf16[576,128]{1,0:T(8,128)(2,1)}, bf16[576,128]{1,0:T(8,128)(2,1)S(1)}, u32[]{:S(2)}, u32[]{:S(2)}) %collective-permute-start.46) | collective-permute-done | bytes 147488 | tf_op jit(solution)/shard_map/ppermute | solution.py:949
  270.8 4.2 %all-to-all-start.11 = ((f32[8,6,128]{2,1,0:T(8,128)}), f32[8,6,128]{2,1,0:T(8,128)S(1)}, u32[]{:S(2)}, u32[]{:S(2)}) async-start(f32[8,6,128]{2,1,0:T(8,128)} %get-tuple-element.548), calls=%async_computation.11 | async-start | bytes 65536 | tf_op jit(solution)/shard_map/all_to_all | solution.py:841
  277.8 4.3 %all-to-all-done.11.refs_0_ = f32[8,6,128]{2,1,0:T(8,128)S(1)} async-done(((f32[8,6,128]{2,1,0:T(8,128)}), f32[8,6,128]{2,1,0:T(8,128)S(1)}, u32[]{:S(2)}, u32[]{:S(2)}) %all-to-all-start.11) | async-done | bytes 24608 | tf_op jit(solution)/shard_map/all_to_all | solution.py:841
  295.8 5.9 %all-to-all-start.13 = ((bf16[8,192,128]{2,1,0:T(8,128)(2,1)}), bf16[8,192,128]{2,1,0:T(8,128)(2,1)S(1)}, u32[]{:S(2)}, u32[]{:S(2)}) async-start(bf16[8,192,128]{2,1,0:T(8,128)(2,1)} %get-tuple-element.587), calls=%async_computation.13 | async-start | bytes 786432 | tf_op jit(solution)/shard_map/all_to_all | solution.py:841
  310.5 7.7 %collective-permute-done.53.refs_2_ = bf16[1,1,9,64,128]{4,3,2,1,0:T(8,128)(2,1)S(1)} collective-permute-done((bf16[1,1,9,64,128]{4,3,2,1,0:T(8,128)(2,1)S(1)}, bf16[1,1,9,64,128]{4,3,2,1,0:T(8,128)(2,1)S(1)}, u32[]{:S(2)}, u32[]{:S(2)}) %collective-permute-start.53) | collective-permute-done | bytes 147488 | tf_op jit(solution)/shard_map/ppermute | solution.py:949
  (238 shorter events, 227.5 us)
Async XLA Ops:
  18.8 15.6 %collective-permute-start.7 = (bf16[2,2,3,128,128]{4,3,2,1,0:T(8,128)(2,1)S(1)}, bf16[2,2,3,128,128]{4,3,2,1,0:T(8,128)(2,1)S(1)}, u32[]{:S(2)}, u32[]{:S(2)}) collective-permute-start(bf16[2,2,3,128,128]{4,3,2,1,0:T(8,128)(2,1)S(1)} %get-tuple-element.335.refs_1_), channel_id=1, source_target_pairs={{0,2},{2,0},{1,3},{3,1},{4,6},{6,4},{5,7},{7,5},{8,10},{10,8},{9,1... | collective-permute-start | bytes 1179656 | tf_op jit(solution)/shard_map/ppermute | solution.py:821
  20.6 12.4 %all-to-all-start = ((f32[8,2,128]{2,1,0:T(2,128)}), f32[8,2,128]{2,1,0:T(2,128)S(1)}, u32[]{:S(2)}, u32[]{:S(2)}) async-start(f32[8,2,128]{2,1,0:T(2,128)} %get-tuple-element.324), calls=%async_computation | async-start | bytes 16384 | tf_op jit(solution)/shard_map/all_to_all | solution.py:841
  27.0 12.0 %collective-permute-start.6 = (bf16[2,2,3,128,128]{4,3,2,1,0:T(8,128)(2,1)S(1)}, bf16[2,2,3,128,128]{4,3,2,1,0:T(8,128)(2,1)S(1)}, u32[]{:S(2)}, u32[]{:S(2)}) collective-permute-start(bf16[2,2,3,128,128]{4,3,2,1,0:T(8,128)(2,1)S(1)} %get-tuple-element.335.refs_1_), channel_id=1, source_target_pairs={{0,1},{1,0},{2,3},{3,2},{4,5},{5,4},{6,7},{7,6},{8,9},{9,8},{10,11... | collective-permute-start | bytes 1179656 | tf_op jit(solution)/shard_map/ppermute | solution.py:822
  44.3 11.2 %all-to-all-start.1 = ((f32[8,8,128]{2,1,0:T(8,128)}), f32[8,8,128]{2,1,0:T(8,128)S(1)}, u32[]{:S(2)}, u32[]{:S(2)}) async-start(f32[8,8,128]{2,1,0:T(8,128)} %get-tuple-element.348), calls=%async_computation.1 | async-start | bytes 65536 | tf_op jit(solution)/shard_map/all_to_all | solution.py:841
  84.4 12.4 %collective-permute-start.25 = (bf16[1,2,576,128]{3,2,1,0:T(8,128)(2,1)S(1)}, bf16[1,2,576,128]{3,2,1,0:T(8,128)(2,1)S(1)}, u32[]{:S(2)}, u32[]{:S(2)}) collective-permute-start(bf16[1,2,576,128]{3,2,1,0:T(8,128)(2,1)S(1)} %get-tuple-element.395), channel_id=1, source_target_pairs={{0,8},{4,12},{8,0},{12,4},{16,24},{20,28},{24,16},{28,20},{1,9},{5... | collective-permute-start | bytes 884744 | tf_op jit(solution)/shard_map/ppermute | solution.py:949
  138.0 206.9 %reduce-scatter.5.cloned.1.call-start = ((), (), s32[]{:S(2)}) async-start(), calls=%async_computation.18 | async-start | bytes 3981312 | tf_op jit(solution)/shard_map/reduce_scatter | solution.py:1097
  221.8 13.1 %collective-permute-start.39 = (bf16[1872,128]{1,0:T(8,128)(2,1)S(1)}, bf16[1872,128]{1,0:T(8,128)(2,1)S(1)}, u32[]{:S(2)}, u32[]{:S(2)}) collective-permute-start(bf16[1872,128]{1,0:T(8,128)(2,1)S(1)} %get-tuple-element.503), channel_id=1, source_target_pairs={{0,2},{2,0},{1,3},{3,1},{4,6},{6,4},{5,7},{7,5},{8,10},{10,8},{9,1... | collective-permute-start | bytes 1437704 | tf_op jit(solution)/shard_map/ppermute | solution.py:1394
  222.4 15.3 %collective-permute-start.40 = (bf16[2,1,9,64,128]{4,3,2,1,0:T(8,128)(2,1)S(1)}, bf16[2,1,9,64,128]{4,3,2,1,0:T(8,128)(2,1)S(1)}, u32[]{:S(2)}, u32[]{:S(2)}) collective-permute-start(bf16[2,1,9,64,128]{4,3,2,1,0:T(8,128)(2,1)S(1)} %get-tuple-element.516), channel_id=1, source_target_pairs={{0,4},{4,0},{8,12},{12,8},{16,20},{20,16},{24,28},{28,24},{1,5},{5... | collective-permute-start | bytes 884744 | tf_op jit(solution)/shard_map/ppermute | solution.py:949
  222.9 14.8 %collective-permute-start.41 = (bf16[144,128]{1,0:T(8,128)(2,1)S(1)}, bf16[144,128]{1,0:T(8,128)(2,1)S(1)}, u32[]{:S(2)}, u32[]{:S(2)}) collective-permute-start(bf16[144,128]{1,0:T(8,128)(2,1)S(1)} %copy-done), channel_id=1, source_target_pairs={{0,8},{4,12},{8,0},{12,4},{16,24},{20,28},{24,16},{28,20},{1,9},{5... | collective-permute-start | bytes 110600 | tf_op jit(solution)/shard_map/ppermute | solution.py:949
  241.0 103.9 %reduce-scatter.3.cloned.1.call-start = ((), (), s32[]{:S(2)}) async-start(), calls=%async_computation.17 | async-start | bytes 3981312 | tf_op jit(solution)/shard_map/reduce_scatter | solution.py:1097
  251.2 13.1 %collective-permute-start.43 = (bf16[3,576,128]{2,1,0:T(8,128)(2,1)S(1)}, bf16[3,576,128]{2,1,0:T(8,128)(2,1)S(1)}, u32[]{:S(2)}, u32[]{:S(2)}) collective-permute-start(bf16[3,576,128]{2,1,0:T(8,128)(2,1)S(1)} %get-tuple-element.533.refs_0_), channel_id=1, source_target_pairs={{0,2},{2,0},{1,3},{3,1},{4,6},{6,4},{5,7},{7,5},{8,10},{10,8},{9,1... | collective-permute-start | bytes 1327112 | tf_op jit(solution)/shard_map/ppermute | solution.py:1427
  254.6 12.5 %collective-permute-start.45 = (bf16[2,1,9,64,128]{4,3,2,1,0:T(8,128)(2,1)S(1)}, bf16[2,1,9,64,128]{4,3,2,1,0:T(8,128)(2,1)S(1)}, u32[]{:S(2)}, u32[]{:S(2)}) collective-permute-start(bf16[2,1,9,64,128]{4,3,2,1,0:T(8,128)(2,1)S(1)} %get-tuple-element.546), channel_id=1, source_target_pairs={{0,4},{4,0},{8,12},{12,8},{16,20},{20,16},{24,28},{28,24},{1,5},{5... | collective-permute-start | bytes 884744 | tf_op jit(solution)/shard_map/ppermute | solution.py:949
  255.3 15.5 %collective-permute-start.46 = (bf16[576,128]{1,0:T(8,128)(2,1)}, bf16[576,128]{1,0:T(8,128)(2,1)S(1)}, u32[]{:S(2)}, u32[]{:S(2)}) collective-permute-start(bf16[576,128]{1,0:T(8,128)(2,1)} %get-tuple-element.547), channel_id=1, source_target_pairs={{0,8},{4,12},{8,0},{12,4},{16,24},{20,28},{24,16},{28,20},{1,9},{5... | collective-permute-start | bytes 442376 | tf_op jit(solution)/shard_map/ppermute | solution.py:949
  257.5 17.5 %collective-permute-start.47 = (bf16[576,128]{1,0:T(8,128)(2,1)S(1)}, bf16[576,128]{1,0:T(8,128)(2,1)S(1)}, u32[]{:S(2)}, u32[]{:S(2)}) collective-permute-start(bf16[576,128]{1,0:T(8,128)(2,1)S(1)} %get-tuple-element.551), channel_id=1, source_target_pairs={{0,2},{2,0},{1,3},{3,1},{4,6},{6,4},{5,7},{7,5},{8,10},{10,8},{9,1... | collective-permute-start | bytes 442376 | tf_op jit(solution)/shard_map/ppermute | solution.py:1323
  259.1 33.1 %collective-permute-start.48 = (bf16[1,1,9,64,128]{4,3,2,1,0:T(8,128)(2,1)S(1)}, bf16[1,1,9,64,128]{4,3,2,1,0:T(8,128)(2,1)S(1)}, u32[]{:S(2)}, u32[]{:S(2)}) collective-permute-start(bf16[1,1,9,64,128]{4,3,2,1,0:T(8,128)(2,1)S(1)} %get-tuple-element.568), channel_id=1, source_target_pairs={{0,16},{4,20},{8,24},{12,28},{16,0},{20,4},{24,8},{28,12},{1,17},{... | collective-permute-start | bytes 442376 | tf_op jit(solution)/shard_map/ppermute | solution.py:949
  270.8 11.3 %all-to-all-start.11 = ((f32[8,6,128]{2,1,0:T(8,128)}), f32[8,6,128]{2,1,0:T(8,128)S(1)}, u32[]{:S(2)}, u32[]{:S(2)}) async-start(f32[8,6,128]{2,1,0:T(8,128)} %get-tuple-element.548), calls=%async_computation.11 | async-start | bytes 65536 | tf_op jit(solution)/shard_map/all_to_all | solution.py:841
  295.8 29.3 %all-to-all-start.13 = ((bf16[8,192,128]{2,1,0:T(8,128)(2,1)}), bf16[8,192,128]{2,1,0:T(8,128)(2,1)S(1)}, u32[]{:S(2)}, u32[]{:S(2)}) async-start(bf16[8,192,128]{2,1,0:T(8,128)(2,1)} %get-tuple-element.587), calls=%async_computation.13 | async-start | bytes 786432 | tf_op jit(solution)/shard_map/all_to_all | solution.py:841
  304.5 18.8 %collective-permute-start.51 = (bf16[2,1,9,64,128]{4,3,2,1,0:T(8,128)(2,1)S(1)}, bf16[2,1,9,64,128]{4,3,2,1,0:T(8,128)(2,1)S(1)}, u32[]{:S(2)}, u32[]{:S(2)}) collective-permute-start(bf16[2,1,9,64,128]{4,3,2,1,0:T(8,128)(2,1)S(1)} %get-tuple-element.590), channel_id=1, source_target_pairs={{0,4},{4,0},{8,12},{12,8},{16,20},{20,16},{24,28},{28,24},{1,5},{5... | collective-permute-start | bytes 884744 | tf_op jit(solution)/shard_map/ppermute | solution.py:949
  306.6 11.5 %collective-permute-start.53 = (bf16[1,1,9,64,128]{4,3,2,1,0:T(8,128)(2,1)S(1)}, bf16[1,1,9,64,128]{4,3,2,1,0:T(8,128)(2,1)S(1)}, u32[]{:S(2)}, u32[]{:S(2)}) collective-permute-start(bf16[1,1,9,64,128]{4,3,2,1,0:T(8,128)(2,1)S(1)} %get-tuple-element.595), channel_id=1, source_target_pairs={{0,16},{4,20},{8,24},{12,28},{16,0},{20,4},{24,8},{28,12},{1,17},{... | collective-permute-start | bytes 442376 | tf_op jit(solution)/shard_map/ppermute | solution.py:949
  309.0 10.9 %collective-permute-start.52 = (bf16[576,128]{1,0:T(8,128)(2,1)}, bf16[576,128]{1,0:T(8,128)(2,1)S(1)}, u32[]{:S(2)}, u32[]{:S(2)}) collective-permute-start(bf16[576,128]{1,0:T(8,128)(2,1)} %get-tuple-element.591), channel_id=1, source_target_pairs={{0,8},{4,12},{8,0},{12,4},{16,24},{20,28},{24,16},{28,20},{1,9},{5... | collective-permute-start | bytes 442376 | tf_op jit(solution)/shard_map/ppermute | solution.py:949
  325.9 25.7 %all-to-all-start.14 = ((bf16[8,192,128]{2,1,0:T(8,128)(2,1)}), bf16[8,192,128]{2,1,0:T(8,128)(2,1)S(1)}, u32[]{:S(2)}, u32[]{:S(2)}) async-start(bf16[8,192,128]{2,1,0:T(8,128)(2,1)} %get-tuple-element.625), calls=%async_computation.16 | async-start | bytes 786432 | tf_op jit(solution)/shard_map/all_to_all | solution.py:841
  329.5 11.6 %collective-permute-start.55 = (bf16[2,1,9,64,128]{4,3,2,1,0:T(8,128)(2,1)S(1)}, bf16[2,1,9,64,128]{4,3,2,1,0:T(8,128)(2,1)S(1)}, u32[]{:S(2)}, u32[]{:S(2)}) collective-permute-start(bf16[2,1,9,64,128]{4,3,2,1,0:T(8,128)(2,1)S(1)} %get-tuple-element.614), channel_id=1, source_target_pairs={{0,4},{4,0},{8,12},{12,8},{16,20},{20,16},{24,28},{28,24},{1,5},{5... | collective-permute-start | bytes 884744 | tf_op jit(solution)/shard_map/ppermute | solution.py:949
  333.5 21.3 %collective-permute-start.54 = (bf16[1,1,9,64,128]{4,3,2,1,0:T(8,128)(2,1)S(1)}, bf16[1,1,9,64,128]{4,3,2,1,0:T(8,128)(2,1)S(1)}, u32[]{:S(2)}, u32[]{:S(2)}) collective-permute-start(bf16[1,1,9,64,128]{4,3,2,1,0:T(8,128)(2,1)S(1)} %get-tuple-element.604), channel_id=1, source_target_pairs={{0,16},{4,20},{8,24},{12,28},{16,0},{20,4},{24,8},{28,12},{1,17},{... | collective-permute-start | bytes 442376 | tf_op jit(solution)/shard_map/ppermute | solution.py:949
  342.8 14.9 %collective-permute-start.56 = (bf16[1,1,9,64,128]{4,3,2,1,0:T(8,128)(2,1)S(1)}, bf16[1,1,9,64,128]{4,3,2,1,0:T(8,128)(2,1)S(1)}, u32[]{:S(2)}, u32[]{:S(2)}) collective-permute-start(bf16[1,1,9,64,128]{4,3,2,1,0:T(8,128)(2,1)S(1)} %get-tuple-element.621), channel_id=1, source_target_pairs={{0,16},{4,20},{8,24},{12,28},{16,0},{20,4},{24,8},{28,12},{1,17},{... | collective-permute-start | bytes 442376 | tf_op jit(solution)/shard_map/ppermute | solution.py:949
  (56 other events, 369.5 us)
Sparse Core Ops, SparseCore 0:
  157.7 81.3 reduce-scatter.4
  247.8 91.8 reduce-scatter.2

commit v4 on v3

--- a/solution.py
+++ b/solution.py
@@ -1346,7 +1346,7 @@
             [shape_of((images, layers * 2 * tasks * 128 // images, 128), LOW)],
             name="flat",
         )[0]
-        flat.append(swap_img(rows))
+        flat.append(rows)
 
     plan = {
         "gate_1": (),
@@ -1504,12 +1504,14 @@
     parts = scatter_ch(*unfinished, "pairx_0")
     every = ["b_1", "a_1", "b_0", "a_0"]
 
-    put_ready(every[:2])
+    flat[0] = swap_img(hold(flat[0], parts[0]))
+    put_ready(every[:1])
     gap(steps("a_0"))
     gap(steps("", "b_0"))
     flat = run(spread_sum_body, flat, [shape_of(flat[0].shape, LOW)], name="spread")[0]
     flat = swap_img(flat)
     dx = run(mixed_body, parts, [shape_of((n0, 128))], name="dx_0", away=(0,))[0].home
+    put_ready(every[1:2])
     gap(steps("", "a_0"))
     tw = run(
         widen_body,

time: 369 us -> 377 us (1.022)
  waiting for transfers between devices: 107 us -> 115 us
    ppermute x15, waiting for transfers between devices: 24.1 us -> 33.8 us  [send_img(): got = lax.ppermute(value, 'img', [(i, i ^ 1 << bit) for i in range(images)])]
    ppermute x15, starting transfers between devices: 19.5 us -> 15.7 us  [send_img(): got = lax.ppermute(value, 'img', [(i, i ^ 1 << bit) for i in range(images)])]
  transfers between devices with their start and end apart: 73 -> 73, of which waited for: 39 -> 37; matrix products, arithmetic and copies ran while one was open for 2% -> 2% of each run, Pallas kernels for 28% -> 28%
where the time goes in v4:
time: 377 us; the launch traced here: 375 us
  Pallas kernels  129 us (34%)
  waiting for transfers between devices  115 us (31%)
  starting transfers between devices  99.3 us (26%)
  between operations  15 us (4%)
  blocking collectives  10.3 us (3%)
  local copies, waits for them, and re-layouts  5.83 us (2%)
    pallas_call x71, Pallas kernels, run(): pl.pallas_call(kernel, out_shape=out_shape, in_specs=specs + [vmem] * len...  112 us
    all_to_all x14, starting transfers between devices, swap_img(): return lax.all_to_all(copies, 'img', 0, 0)  56.7 us
    all_to_all x14, waiting for transfers between devices, swap_img(): return lax.all_to_all(copies, 'img', 0, 0)  43.5 us
    ppermute x15, waiting for transfers between devices, send_img(): got = lax.ppermute(value, 'img', [(i, i ^ 1 << bit) for i in range(images)])  33.8 us
    ppermute x15, starting transfers between devices, send_img(): got = lax.ppermute(value, 'img', [(i, i ^ 1 << bit) for i in range(images)])  15.7 us
    ppermute x7, waiting for transfers between devices, near_and_far(): far = lax.ppermute(value, 'ch', CHIP)  13.2 us
    all_to_all x1, blocking collectives, swap_img(): return lax.all_to_all(copies, 'img', 0, 0)  10.3 us
    pallas_call x8, Pallas kernels, bring(): pl.pallas_call(body, out_shape=[pltpu.VMEM(v.shape, v.dtype) for v in ite...  9.99 us
  transfers between devices with their start and end apart: 73, of which 37 were waited for; matrix products, arithmetic and copies ran while one was open for 2% of the time, Pallas kernels for 28%

profile of v4, /device:TPU:0, one launch (start us, length us, event | category | flops | bytes accessed | tf_op | source)
XLA Modules:
  0.0 374.6 jit_solution(14884649874460765226)
XLA Ops:
  20.6 5.8 %all-to-all-start = ((f32[8,2,128]{2,1,0:T(2,128)}), f32[8,2,128]{2,1,0:T(2,128)S(1)}, u32[]{:S(2)}, u32[]{:S(2)}) async-start(f32[8,2,128]{2,1,0:T(2,128)} %get-tuple-element.325), calls=%async_computation | async-start | bytes 16384 | tf_op jit(solution)/shard_map/all_to_all | solution.py:841
  40.3 4.0 %conv2_0.1 = (bf16[576,512]{1,0:T(8,128)(2,1)}, f32[576,128]{1,0:T(8,128)S(1)}, f32[3,576,128]{2,1,0:T(8,128)S(1)}, f32[8,8,128]{2,1,0:T(8,128)}, f32[8,128]{1,0...) custom-call(s32[1]{0:T(128)} %bitcast.refs_0_, bf16[576,128]{1,0:T(8,128)(2,1)S(1)} %get-tuple-element.334.refs_1_, ...), custom_call_target="tpu_custom_call" | custom-call | bytes 1 | tf_op jit(solution)/shard_map/conv2_0/pallas_call | solution.py:750
  44.3 4.5 %all-to-all-start.1 = ((f32[8,8,128]{2,1,0:T(8,128)}), f32[8,8,128]{2,1,0:T(8,128)S(1)}, u32[]{:S(2)}, u32[]{:S(2)}) async-start(f32[8,8,128]{2,1,0:T(8,128)} %get-tuple-element.349), calls=%async_computation.1 | async-start | bytes 65536 | tf_op jit(solution)/shard_map/all_to_all | solution.py:841
  51.2 4.3 %all-to-all-done.1.refs_0_ = f32[8,8,128]{2,1,0:T(8,128)S(1)} async-done(((f32[8,8,128]{2,1,0:T(8,128)}), f32[8,8,128]{2,1,0:T(8,128)S(1)}, u32[]{:S(2)}, u32[]{:S(2)}) %all-to-all-start.1) | async-done | bytes 32800 | tf_op jit(solution)/shard_map/all_to_all | solution.py:841
  69.2 5.2 %taskconv_0.1 = (bf16[3,576,512]{2,1,0:T(8,128)(2,1)}, f32[3,576,128]{2,1,0:T(8,128)S(1)}, f32[8,8,128]{2,1,0:T(8,128)}, f32[8,128]{1,0:T(8,128)S(1)}, bf16[3,576,128]{2,1,0:T(8,128)(2,1)}, /*index=5*/f32[6,512]{1,0:T(8,128)}) custom-call(s32[1]{0:T(128)} %bitcast.refs_0_, bf16[3,576,128]{2,1,0:T(8,128)(2,1)S(1)} %get-tuple-element.359.refs_1_, ...), custom_call_target="tpu_custom_call" | custom-call | bytes 1 | tf_op jit(solution)/shard_map/taskconv_0/pallas_call | solution.py:750
  80.0 4.5 %all-to-all-done.2.refs_0_ = f32[8,8,128]{2,1,0:T(8,128)S(1)} async-done(((f32[8,8,128]{2,1,0:T(8,128)}), f32[8,8,128]{2,1,0:T(8,128)S(1)}, u32[]{:S(2)}, u32[]{:S(2)}) %all-to-all-start.2) | async-done | bytes 32800 | tf_op jit(solution)/shard_map/all_to_all | solution.py:841
  89.4 3.9 %collective-permute-done.21.refs_3_ = bf16[144,128]{1,0:T(8,128)(2,1)S(1)} collective-permute-done((bf16[144,128]{1,0:T(8,128)(2,1)S(1)}, bf16[144,128]{1,0:T(8,128)(2,1)S(1)}, u32[]{:S(2)}, u32[]{:S(2)}) %collective-permute-start.21) | collective-permute-done | bytes 36896 | tf_op jit(solution)/shard_map/ppermute | solution.py:821
  101.4 5.4 %all-to-all-done.3.refs_0_ = f32[8,8,128]{2,1,0:T(8,128)S(1)} async-done(((f32[8,8,128]{2,1,0:T(8,128)}), f32[8,8,128]{2,1,0:T(8,128)S(1)}, u32[]{:S(2)}, u32[]{:S(2)}) %all-to-all-start.3) | async-done | bytes 32800 | tf_op jit(solution)/shard_map/all_to_all | solution.py:841
  122.6 10.3 %all_to_all.75.refs_0_ = f32[8,6,128]{2,1,0:T(8,128)S(1)} all-to-all(f32[8,6,128]{2,1,0:T(8,128)S(1)} %get-tuple-element.416), channel_id=1, replica_groups=mesh['img'=8,'ch'=4] {'img'}, dimensions={0} | all-to-all | bytes 49152 | tf_op jit(solution)/shard_map/all_to_all | solution.py:841
  139.1 5.6 %all-to-all-done.6.refs_0_ = f32[8,6,128]{2,1,0:T(8,128)S(1)} async-done(((f32[8,6,128]{2,1,0:T(8,128)}), f32[8,6,128]{2,1,0:T(8,128)S(1)}, u32[]{:S(2)}, u32[]{:S(2)}) %all-to-all-start.6) | async-done | bytes 24608 | tf_op jit(solution)/shard_map/all_to_all | solution.py:841
  144.6 4.0 %taskback_1.1 = (bf16[3,144,128]{2,1,0:T(8,128)(2,1)}, bf16[2,3,144,128]{3,2,1,0:T(8,128)(2,1)S(1)}, f32[3,144,128]{2,1,0:T(8,128)S(1)}, f32[3,144,128]{2,1,0:T(...) custom-call(s32[1]{0:T(128)} %bitcast.refs_0_, f32[3,144,128]{2,1,0:T(8,128)S(1)} %get-tuple-element.422.refs_1_, ...), custom_call_target="tpu_custom_call" | custom-call | bytes 1 | tf_op jit(solution)/shard_map/taskback_1/pallas_call | solution.py:750
  150.9 4.6 %weight_1.1 = (bf16[3,9,512,128]{3,2,1,0:T(8,128)(2,1)}, f32[8,128]{1,0:T(8,128)S(1)}) custom-call(bf16[3,144,512]{2,1,0:T(8,128)(2,1)} %get-tuple-element.443.refs_0_, bf16[3,144,128]{2,1,0:T(8,128)(2,1)} %get-tuple-element.444.refs_1_, f32[8,128]{1,0:T(8,128)S(1)} %get-tuple-element.445.refs_2_), custom_call_target="tpu_custom_call" | custom-call | bytes 1 | tf_op jit(solution)/shard_map/weight_1/pallas_call | solution.py:750
  158.1 5.2 %collective-permute-done.31.refs_2_ = bf16[2,2,144,128]{3,2,1,0:T(8,128)(2,1)S(1)} collective-permute-done((bf16[2,2,144,128]{3,2,1,0:T(8,128)(2,1)S(1)}, bf16[2,2,144,128]{3,2,1,0:T(8,128)(2,1)S(1)}, u32[]{:S(2)}, u32[]{:S(2)}) %collective-permute-start.31) | collective-permute-done | bytes 147488 | tf_op jit(solution)/shard_map/ppermute | solution.py:949
  167.7 6.2 %all-to-all-done.7.refs_0_ = f32[8,8,128]{2,1,0:T(8,128)S(1)} async-done(((f32[8,8,128]{2,1,0:T(8,128)}), f32[8,8,128]{2,1,0:T(8,128)S(1)}, u32[]{:S(2)}, u32[]{:S(2)}) %all-to-all-start.7) | async-done | bytes 32800 | tf_op jit(solution)/shard_map/all_to_all | solution.py:841
  206.8 4.3 %all-to-all-done.9.refs_0_ = f32[8,8,128]{2,1,0:T(8,128)S(1)} async-done(((f32[8,8,128]{2,1,0:T(8,128)}), f32[8,8,128]{2,1,0:T(8,128)S(1)}, u32[]{:S(2)}, u32[]{:S(2)}) %all-to-all-start.9) | async-done | bytes 32800 | tf_op jit(solution)/shard_map/all_to_all | solution.py:841
  213.1 5.8 %taskback_0.1 = (bf16[3,576,128]{2,1,0:T(8,128)(2,1)}, bf16[2,3,576,128]{3,2,1,0:T(8,128)(2,1)S(1)}, f32[3,576,128]{2,1,0:T(8,128)S(1)}, f32[3,576,128]{2,1,0:T(8,128)S(1)}, f32[8,128]{1,0:T(8,128)S(1)}) custom-call(s32[1]{0:T(128)} %bitcast.refs_0_, f32[3,576,128]{2,1,0:T(8,128)S(1)} %get-tuple-element.487.refs_1_, ...), custom_call_target="tpu_custom_call" | custom-call | bytes 1 | tf_op jit(solution)/shard_map/taskback_0/pallas_call | solution.py:750
  223.6 7.4 %weight_0.1 = (bf16[3,9,512,128]{3,2,1,0:T(8,128)(2,1)}, f32[8,128]{1,0:T(8,128)S(1)}) custom-call(bf16[3,576,512]{2,1,0:T(8,128)(2,1)} %get-tuple-element.510.refs_0_, bf16[3,576,128]{2,1,0:T(8,128)(2,1)} %get-tuple-element.511.refs_1_, f32[8,128]{1,0:T(8,128)S(1)} %get-tuple-element.512.refs_2_), custom_call_target="tpu_custom_call" | custom-call | bytes 1 | tf_op jit(solution)/shard_map/weight_0/pallas_call | solution.py:750
  231.0 3.9 %collective-permute-done.39.refs_2_ = bf16[1872,128]{1,0:T(8,128)(2,1)S(1)} collective-permute-done((bf16[1872,128]{1,0:T(8,128)(2,1)S(1)}, bf16[1872,128]{1,0:T(8,128)(2,1)S(1)}, u32[]{:S(2)}, u32[]{:S(2)}) %collective-permute-start.39) | collective-permute-done | bytes 479264 | tf_op jit(solution)/shard_map/ppermute | solution.py:1394
  270.8 4.2 %all-to-all-start.11 = ((f32[8,6,128]{2,1,0:T(8,128)}), f32[8,6,128]{2,1,0:T(8,128)S(1)}, u32[]{:S(2)}, u32[]{:S(2)}) async-start(f32[8,6,128]{2,1,0:T(8,128)} %get-tuple-element.549), calls=%async_computation.11 | async-start | bytes 65536 | tf_op jit(solution)/shard_map/all_to_all | solution.py:841
  277.8 4.3 %all-to-all-done.11.refs_0_ = f32[8,6,128]{2,1,0:T(8,128)S(1)} async-done(((f32[8,6,128]{2,1,0:T(8,128)}), f32[8,6,128]{2,1,0:T(8,128)S(1)}, u32[]{:S(2)}, u32[]{:S(2)}) %all-to-all-start.11) | async-done | bytes 24608 | tf_op jit(solution)/shard_map/all_to_all | solution.py:841
  300.2 6.0 %all-to-all-start.13 = ((bf16[8,192,128]{2,1,0:T(8,128)(2,1)}), bf16[8,192,128]{2,1,0:T(8,128)(2,1)S(1)}, u32[]{:S(2)}, u32[]{:S(2)}) async-start(bf16[8,192,128]{2,1,0:T(8,128)(2,1)} %get-tuple-element.589), calls=%async_computation.13 | async-start | bytes 786432 | tf_op jit(solution)/shard_map/all_to_all | solution.py:841
  309.6 10.5 %collective-permute-done.52.refs_4_ = bf16[576,128]{1,0:T(8,128)(2,1)S(1)} collective-permute-done((bf16[576,128]{1,0:T(8,128)(2,1)}, bf16[576,128]{1,0:T(8,128)(2,1)S(1)}, u32[]{:S(2)}, u32[]{:S(2)}) %collective-permute-start.52) | collective-permute-done | bytes 147488 | tf_op jit(solution)/shard_map/ppermute | solution.py:949
  326.2 5.5 %all-to-all-start.14 = ((bf16[8,192,128]{2,1,0:T(8,128)(2,1)}), bf16[8,192,128]{2,1,0:T(8,128)(2,1)S(1)}, u32[]{:S(2)}, u32[]{:S(2)}) async-start(bf16[8,192,128]{2,1,0:T(8,128)(2,1)} %get-tuple-element.627), calls=%async_computation.16 | async-start | bytes 786432 | tf_op jit(solution)/shard_map/all_to_all | solution.py:841
  341.9 11.6 %collective-permute-done.53.refs_2_ = bf16[1,1,9,64,128]{4,3,2,1,0:T(8,128)(2,1)S(1)} collective-permute-done((bf16[1,1,9,64,128]{4,3,2,1,0:T(8,128)(2,1)S(1)}, bf16[1,1,9,64,128]{4,3,2,1,0:T(8,128)(2,1)S(1)}, u32[]{:S(2)}, u32[]{:S(2)}) %collective-permute-start.53) | collective-permute-done | bytes 147488 | tf_op jit(solution)/shard_map/ppermute | solution.py:949
  (238 shorter events, 222.8 us)
Async XLA Ops:
  18.8 15.6 %collective-permute-start.7 = (bf16[2,2,3,128,128]{4,3,2,1,0:T(8,128)(2,1)S(1)}, bf16[2,2,3,128,128]{4,3,2,1,0:T(8,128)(2,1)S(1)}, u32[]{:S(2)}, u32[]{:S(2)}) collective-permute-start(bf16[2,2,3,128,128]{4,3,2,1,0:T(8,128)(2,1)S(1)} %get-tuple-element.336.refs_1_), channel_id=1, source_target_pairs={{0,2},{2,0},{1,3},{3,1},{4,6},{6,4},{5,7},{7,5},{8,10},{10,8},{9,1... | collective-permute-start | bytes 1179656 | tf_op jit(solution)/shard_map/ppermute | solution.py:821
  20.6 12.4 %all-to-all-start = ((f32[8,2,128]{2,1,0:T(2,128)}), f32[8,2,128]{2,1,0:T(2,128)S(1)}, u32[]{:S(2)}, u32[]{:S(2)}) async-start(f32[8,2,128]{2,1,0:T(2,128)} %get-tuple-element.325), calls=%async_computation | async-start | bytes 16384 | tf_op jit(solution)/shard_map/all_to_all | solution.py:841
  27.0 12.0 %collective-permute-start.6 = (bf16[2,2,3,128,128]{4,3,2,1,0:T(8,128)(2,1)S(1)}, bf16[2,2,3,128,128]{4,3,2,1,0:T(8,128)(2,1)S(1)}, u32[]{:S(2)}, u32[]{:S(2)}) collective-permute-start(bf16[2,2,3,128,128]{4,3,2,1,0:T(8,128)(2,1)S(1)} %get-tuple-element.336.refs_1_), channel_id=1, source_target_pairs={{0,1},{1,0},{2,3},{3,2},{4,5},{5,4},{6,7},{7,6},{8,9},{9,8},{10,11... | collective-permute-start | bytes 1179656 | tf_op jit(solution)/shard_map/ppermute | solution.py:822
  44.3 11.2 %all-to-all-start.1 = ((f32[8,8,128]{2,1,0:T(8,128)}), f32[8,8,128]{2,1,0:T(8,128)S(1)}, u32[]{:S(2)}, u32[]{:S(2)}) async-start(f32[8,8,128]{2,1,0:T(8,128)} %get-tuple-element.349), calls=%async_computation.1 | async-start | bytes 65536 | tf_op jit(solution)/shard_map/all_to_all | solution.py:841
  84.4 12.4 %collective-permute-start.25 = (bf16[1,2,576,128]{3,2,1,0:T(8,128)(2,1)S(1)}, bf16[1,2,576,128]{3,2,1,0:T(8,128)(2,1)S(1)}, u32[]{:S(2)}, u32[]{:S(2)}) collective-permute-start(bf16[1,2,576,128]{3,2,1,0:T(8,128)(2,1)S(1)} %get-tuple-element.396), channel_id=1, source_target_pairs={{0,8},{4,12},{8,0},{12,4},{16,24},{20,28},{24,16},{28,20},{1,9},{5... | collective-permute-start | bytes 884744 | tf_op jit(solution)/shard_map/ppermute | solution.py:949
  138.0 219.1 %reduce-scatter.5.cloned.1.call-start = ((), (), s32[]{:S(2)}) async-start(), calls=%async_computation.18 | async-start | bytes 3981312 | tf_op jit(solution)/shard_map/reduce_scatter | solution.py:1097
  221.8 13.1 %collective-permute-start.39 = (bf16[1872,128]{1,0:T(8,128)(2,1)S(1)}, bf16[1872,128]{1,0:T(8,128)(2,1)S(1)}, u32[]{:S(2)}, u32[]{:S(2)}) collective-permute-start(bf16[1872,128]{1,0:T(8,128)(2,1)S(1)} %get-tuple-element.504), channel_id=1, source_target_pairs={{0,2},{2,0},{1,3},{3,1},{4,6},{6,4},{5,7},{7,5},{8,10},{10,8},{9,1... | collective-permute-start | bytes 1437704 | tf_op jit(solution)/shard_map/ppermute | solution.py:1394
  222.4 15.3 %collective-permute-start.40 = (bf16[2,1,9,64,128]{4,3,2,1,0:T(8,128)(2,1)S(1)}, bf16[2,1,9,64,128]{4,3,2,1,0:T(8,128)(2,1)S(1)}, u32[]{:S(2)}, u32[]{:S(2)}) collective-permute-start(bf16[2,1,9,64,128]{4,3,2,1,0:T(8,128)(2,1)S(1)} %get-tuple-element.517), channel_id=1, source_target_pairs={{0,4},{4,0},{8,12},{12,8},{16,20},{20,16},{24,28},{28,24},{1,5},{5... | collective-permute-start | bytes 884744 | tf_op jit(solution)/shard_map/ppermute | solution.py:949
  222.9 14.8 %collective-permute-start.41 = (bf16[144,128]{1,0:T(8,128)(2,1)S(1)}, bf16[144,128]{1,0:T(8,128)(2,1)S(1)}, u32[]{:S(2)}, u32[]{:S(2)}) collective-permute-start(bf16[144,128]{1,0:T(8,128)(2,1)S(1)} %copy-done), channel_id=1, source_target_pairs={{0,8},{4,12},{8,0},{12,4},{16,24},{20,28},{24,16},{28,20},{1,9},{5... | collective-permute-start | bytes 110600 | tf_op jit(solution)/shard_map/ppermute | solution.py:949
  241.0 116.1 %reduce-scatter.3.cloned.1.call-start = ((), (), s32[]{:S(2)}) async-start(), calls=%async_computation.17 | async-start | bytes 3981312 | tf_op jit(solution)/shard_map/reduce_scatter | solution.py:1097
  251.2 13.1 %collective-permute-start.43 = (bf16[3,576,128]{2,1,0:T(8,128)(2,1)S(1)}, bf16[3,576,128]{2,1,0:T(8,128)(2,1)S(1)}, u32[]{:S(2)}, u32[]{:S(2)}) collective-permute-start(bf16[3,576,128]{2,1,0:T(8,128)(2,1)S(1)} %get-tuple-element.534.refs_0_), channel_id=1, source_target_pairs={{0,2},{2,0},{1,3},{3,1},{4,6},{6,4},{5,7},{7,5},{8,10},{10,8},{9,1... | collective-permute-start | bytes 1327112 | tf_op jit(solution)/shard_map/ppermute | solution.py:1427
  254.6 12.5 %collective-permute-start.45 = (bf16[2,1,9,64,128]{4,3,2,1,0:T(8,128)(2,1)S(1)}, bf16[2,1,9,64,128]{4,3,2,1,0:T(8,128)(2,1)S(1)}, u32[]{:S(2)}, u32[]{:S(2)}) collective-permute-start(bf16[2,1,9,64,128]{4,3,2,1,0:T(8,128)(2,1)S(1)} %get-tuple-element.547), channel_id=1, source_target_pairs={{0,4},{4,0},{8,12},{12,8},{16,20},{20,16},{24,28},{28,24},{1,5},{5... | collective-permute-start | bytes 884744 | tf_op jit(solution)/shard_map/ppermute | solution.py:949
  255.3 15.5 %collective-permute-start.46 = (bf16[576,128]{1,0:T(8,128)(2,1)}, bf16[576,128]{1,0:T(8,128)(2,1)S(1)}, u32[]{:S(2)}, u32[]{:S(2)}) collective-permute-start(bf16[576,128]{1,0:T(8,128)(2,1)} %get-tuple-element.548), channel_id=1, source_target_pairs={{0,8},{4,12},{8,0},{12,4},{16,24},{20,28},{24,16},{28,20},{1,9},{5... | collective-permute-start | bytes 442376 | tf_op jit(solution)/shard_map/ppermute | solution.py:949
  257.5 17.5 %collective-permute-start.47 = (bf16[576,128]{1,0:T(8,128)(2,1)S(1)}, bf16[576,128]{1,0:T(8,128)(2,1)S(1)}, u32[]{:S(2)}, u32[]{:S(2)}) collective-permute-start(bf16[576,128]{1,0:T(8,128)(2,1)S(1)} %get-tuple-element.552), channel_id=1, source_target_pairs={{0,2},{2,0},{1,3},{3,1},{4,6},{6,4},{5,7},{7,5},{8,10},{10,8},{9,1... | collective-permute-start | bytes 442376 | tf_op jit(solution)/shard_map/ppermute | solution.py:1323
  259.1 33.1 %collective-permute-start.48 = (bf16[1,1,9,64,128]{4,3,2,1,0:T(8,128)(2,1)S(1)}, bf16[1,1,9,64,128]{4,3,2,1,0:T(8,128)(2,1)S(1)}, u32[]{:S(2)}, u32[]{:S(2)}) collective-permute-start(bf16[1,1,9,64,128]{4,3,2,1,0:T(8,128)(2,1)S(1)} %get-tuple-element.569), channel_id=1, source_target_pairs={{0,16},{4,20},{8,24},{12,28},{16,0},{20,4},{24,8},{28,12},{1,17},{... | collective-permute-start | bytes 442376 | tf_op jit(solution)/shard_map/ppermute | solution.py:949
  270.8 11.2 %all-to-all-start.11 = ((f32[8,6,128]{2,1,0:T(8,128)}), f32[8,6,128]{2,1,0:T(8,128)S(1)}, u32[]{:S(2)}, u32[]{:S(2)}) async-start(f32[8,6,128]{2,1,0:T(8,128)} %get-tuple-element.549), calls=%async_computation.11 | async-start | bytes 65536 | tf_op jit(solution)/shard_map/all_to_all | solution.py:841
  285.3 11.9 %all-to-all-start.12 = ((f32[8,2,128]{2,1,0:T(2,128)}), f32[8,2,128]{2,1,0:T(2,128)S(1)}, u32[]{:S(2)}, u32[]{:S(2)}) async-start(f32[8,2,128]{2,1,0:T(2,128)} %get-tuple-element.576), calls=%async_computation.12 | async-start | bytes 16384 | tf_op jit(solution)/shard_map/all_to_all | solution.py:841
  300.2 25.2 %all-to-all-start.13 = ((bf16[8,192,128]{2,1,0:T(8,128)(2,1)}), bf16[8,192,128]{2,1,0:T(8,128)(2,1)S(1)}, u32[]{:S(2)}, u32[]{:S(2)}) async-start(bf16[8,192,128]{2,1,0:T(8,128)(2,1)} %get-tuple-element.589), calls=%async_computation.13 | async-start | bytes 786432 | tf_op jit(solution)/shard_map/all_to_all | solution.py:841
  306.1 17.5 %collective-permute-start.51 = (bf16[2,1,9,64,128]{4,3,2,1,0:T(8,128)(2,1)S(1)}, bf16[2,1,9,64,128]{4,3,2,1,0:T(8,128)(2,1)S(1)}, u32[]{:S(2)}, u32[]{:S(2)}) collective-permute-start(bf16[2,1,9,64,128]{4,3,2,1,0:T(8,128)(2,1)S(1)} %get-tuple-element.592), channel_id=1, source_target_pairs={{0,4},{4,0},{8,12},{12,8},{16,20},{20,16},{24,28},{28,24},{1,5},{5... | collective-permute-start | bytes 884744 | tf_op jit(solution)/shard_map/ppermute | solution.py:949
  308.2 12.0 %collective-permute-start.52 = (bf16[576,128]{1,0:T(8,128)(2,1)}, bf16[576,128]{1,0:T(8,128)(2,1)S(1)}, u32[]{:S(2)}, u32[]{:S(2)}) collective-permute-start(bf16[576,128]{1,0:T(8,128)(2,1)} %get-tuple-element.593), channel_id=1, source_target_pairs={{0,8},{4,12},{8,0},{12,4},{16,24},{20,28},{24,16},{28,20},{1,9},{5... | collective-permute-start | bytes 442376 | tf_op jit(solution)/shard_map/ppermute | solution.py:949
  326.2 34.8 %all-to-all-start.14 = ((bf16[8,192,128]{2,1,0:T(8,128)(2,1)}), bf16[8,192,128]{2,1,0:T(8,128)(2,1)S(1)}, u32[]{:S(2)}, u32[]{:S(2)}) async-start(bf16[8,192,128]{2,1,0:T(8,128)(2,1)} %get-tuple-element.627), calls=%async_computation.16 | async-start | bytes 786432 | tf_op jit(solution)/shard_map/all_to_all | solution.py:841
  331.7 23.6 %collective-permute-start.55 = (bf16[2,1,9,64,128]{4,3,2,1,0:T(8,128)(2,1)S(1)}, bf16[2,1,9,64,128]{4,3,2,1,0:T(8,128)(2,1)S(1)}, u32[]{:S(2)}, u32[]{:S(2)}) collective-permute-start(bf16[2,1,9,64,128]{4,3,2,1,0:T(8,128)(2,1)S(1)} %get-tuple-element.616), channel_id=1, source_target_pairs={{0,4},{4,0},{8,12},{12,8},{16,20},{20,16},{24,28},{28,24},{1,5},{5... | collective-permute-start | bytes 884744 | tf_op jit(solution)/shard_map/ppermute | solution.py:949
  337.0 16.5 %collective-permute-start.53 = (bf16[1,1,9,64,128]{4,3,2,1,0:T(8,128)(2,1)S(1)}, bf16[1,1,9,64,128]{4,3,2,1,0:T(8,128)(2,1)S(1)}, u32[]{:S(2)}, u32[]{:S(2)}) collective-permute-start(bf16[1,1,9,64,128]{4,3,2,1,0:T(8,128)(2,1)S(1)} %get-tuple-element.602), channel_id=1, source_target_pairs={{0,16},{4,20},{8,24},{12,28},{16,0},{20,4},{24,8},{28,12},{1,17},{... | collective-permute-start | bytes 442376 | tf_op jit(solution)/shard_map/ppermute | solution.py:949
  339.4 23.4 %collective-permute-start.54 = (bf16[1,1,9,64,128]{4,3,2,1,0:T(8,128)(2,1)S(1)}, bf16[1,1,9,64,128]{4,3,2,1,0:T(8,128)(2,1)S(1)}, u32[]{:S(2)}, u32[]{:S(2)}) collective-permute-start(bf16[1,1,9,64,128]{4,3,2,1,0:T(8,128)(2,1)S(1)} %get-tuple-element.606), channel_id=1, source_target_pairs={{0,16},{4,20},{8,24},{12,28},{16,0},{20,4},{24,8},{28,12},{1,17},{... | collective-permute-start | bytes 442376 | tf_op jit(solution)/shard_map/ppermute | solution.py:949
  (56 other events, 365.1 us)
Sparse Core Ops, SparseCore 0:
  157.7 81.3 reduce-scatter.4
  247.8 87.4 reduce-scatter.2
